TPU v7x, 32 devices: a whole 2x2x4 slice. The times are simulated.
32 devices in a mesh: parts: 2 (over x), row: 8 (over z, y), col: 2 (over core).
Axes of the slice: x: 2, y: 2, z: 4, core: 2. Of those that a mesh axis runs over, the one named last changes fastest.
Arguments:
- density_real: float32 [32, 3, 128, 128], P(('row', 'col')), may hold values from -4 to 4, as said below
- density_imag: float32 [32, 3, 128, 128], P(('row', 'col')), may hold values from -4 to 4, as said below
- hamiltonian: float32 [32, 3, 128, 128], P(('row', 'col')), may hold values from -0.30618622 to 0.30618622, as said below
- dipole: float32 [64, 3, 128, 128], P(('parts', 'row', 'col')), parts along dimension 0, may hold values from -0.15309311 to 0.15309311, as said below
- field: float32 [2], P('parts'), parts along dimension 0, may hold values from 0.5 to 1.5
- pattern: int32 [6, 32, 3], P(None, ('row', 'col')), may hold values from 0 to 1, as said below
Outputs:
- final_real: float32 [64, 3, 128, 128], P(('parts', 'row', 'col')), parts along dimension 0
- final_imag: float32 [64, 3, 128, 128], P(('parts', 'row', 'col')), parts along dimension 0
There are 2 independent parts, one for each index of `parts`. A program takes and returns all parts, laid end to end along the dimension named above; an argument that names none is the same for every part. Nothing has to cross between parts.
Inputs may be any that keep to these rules, and one draw needn't show every extreme that they name: Blocks of the density's real part form a symmetric matrix: density_real[i, 1 + d] is the transpose of density_real[i + d mod 32, 1 - d] for d = 1 .. 1, and each density_real[i, 1] is symmetric. Blocks of the imaginary part form an antisymmetric matrix: density_imag[i, 1 + d] is minus the transpose of density_imag[i + d mod 32, 1 - d] for d = 1 .. 1, and each density_imag[i, 1] is antisymmetric. `hamiltonian`: symmetric in the same sense as density_real. `dipole`: symmetric in the same sense as density_real. pattern[t, i, 1] = 1 and pattern[t, i, 1 + d] = pattern[t, i + d mod 32, 1 - d] for d = 1 .. 1.
All inputs are finite; a program needn't handle non-finite values.
Results may differ from a plain program's by a relative error of at most 0.00022.
Values sent between devices are 32-bit elements; how exact they have to be, the bound alone decides.
No kernel may reach another device: no remote copies, remote signals or barrier semaphores. Data moves between devices by JAX's collectives and lax.ppermute only.
A program may use at most 64 MiB of HBM per device.

v0:
```python
import jax
import jax.numpy as jnp
from jax import lax
from jax.sharding import PartitionSpec as P

TERMS = 6


time_step = 0.5


def padded(cells, sides, width):
    for axis, dim in sides:
        count = lax.axis_size(axis)
        head = lax.slice_in_dim(cells, 0, width, axis=dim)
        tail = lax.slice_in_dim(cells, cells.shape[dim] - width, cells.shape[dim], axis=dim)
        cells = jnp.concatenate(
            [
                lax.ppermute(tail, axis, [(i, (i + 1) % count) for i in range(count)]),
                cells,
                lax.ppermute(head, axis, [((i + 1) % count, i) for i in range(count)]),
            ],
            axis=dim,
        )
    return cells


def apply_left(operator_rows, padded_terms, half_band):
    rows_here = operator_rows.shape[0]
    outputs = []
    for offset_out in range(-half_band, half_band + 1):
        accumulated = None
        for offset_mid in range(-half_band, half_band + 1):
            if abs(offset_out - offset_mid) <= half_band:
                start_row = half_band + offset_mid
                product_part = jnp.einsum(
                    "rab,mrbc->mrac",
                    operator_rows[:, offset_mid + half_band],
                    padded_terms[
                        :, start_row : start_row + rows_here, offset_out - offset_mid + half_band
                    ],
                    precision=lax.Precision.HIGHEST,
                )
                accumulated = product_part if accumulated is None else accumulated + product_part
        outputs.append(accumulated)
    return jnp.stack(outputs, axis=2)


def apply_right(terms_here, padded_operator, half_band):
    rows_here = terms_here.shape[1]
    outputs = []
    for offset_out in range(-half_band, half_band + 1):
        accumulated = None
        for offset_mid in range(-half_band, half_band + 1):
            if abs(offset_out - offset_mid) <= half_band:
                start_row = half_band + offset_mid
                product_part = jnp.einsum(
                    "mrab,rbc->mrac",
                    terms_here[:, :, offset_mid + half_band],
                    padded_operator[
                        start_row : start_row + rows_here, offset_out - offset_mid + half_band
                    ],
                    precision=lax.Precision.HIGHEST,
                )
                accumulated = product_part if accumulated is None else accumulated + product_part
        outputs.append(accumulated)
    return jnp.stack(outputs, axis=2)


def body(density_real, density_imag, hamiltonian, dipole, field, pattern):
    half_band = (hamiltonian.shape[1] - 1) // 2
    series = jnp.stack([density_real, density_imag])
    operators = padded(jnp.stack([hamiltonian, dipole]), ((("row", "col"), 1),), half_band)
    operator_now = hamiltonian + field[0] * dipole
    padded_operator = operators[0] + field[0] * operators[1]
    current = series
    for order_index in range(TERMS):
        coefficient = time_step / (order_index + 1)
        keep_mask = pattern[order_index].astype(jnp.float32)[None, :, :, None, None]
        padded_terms = padded(current, ((("row", "col"), 1),), half_band)
        left_product = apply_left(operator_now, padded_terms, half_band)
        right_product = apply_right(current, padded_operator, half_band)
        commutator = left_product - right_product
        weighted = coefficient * keep_mask * commutator
        current = jnp.stack([weighted[1], -weighted[0]])
        series = series + current
    return (series[0], series[1])


def solution(mesh):
    in_specs = (
        P(("row", "col"), None, None, None),
        P(("row", "col"), None, None, None),
        P(("row", "col"), None, None, None),
        P(("parts", "row", "col"), None, None, None),
        P("parts"),
        P(None, ("row", "col"), None),
    )
    out_specs = (
        P(("parts", "row", "col"), None, None, None),
        P(("parts", "row", "col"), None, None, None),
    )
    return jax.shard_map(body, mesh=mesh, in_specs=in_specs, out_specs=out_specs, check_vma=False)
```

profile of v0, /device:TPU:1, one launch (start us, length us, event | category | flops | bytes accessed | tf_op | source)
XLA Modules:
  0.0 108.7 jit_solution(65197398033374258)
XLA Ops:
  0.6 1.2 %copy.76 = f32[2,3,128,128]{2,3,0,1:T(8,128)S(1)} copy(f32[2,3,128,128]{3,2,1,0:T(8,128)} %param.8) | data formatting | bytes 786432 | tf_op args[2]
  1.9 1.2 %copy.77 = f32[2,3,128,128]{2,3,0,1:T(8,128)S(1)} copy(f32[2,3,128,128]{3,2,1,0:T(8,128)} %param.9) | data formatting | bytes 786432 | tf_op args[3]
  3.1 1.0 fusion.56
  4.0 2.6 %collective-permute-start.2 = (f32[2,1,3,128,128]{3,4,1,2,0:T(8,128)}, f32[2,1,3,128,128]{3,4,1,2,0:T(8,128)}, u32[]{:S(2)}, u32[]{:S(2)}) collective-permute-start(f32[2,1,3,128,128]{3,4,1,2,0:T(8,128)} %get-tuple-element.30), channel_id=1, source_target_pairs={{0,1},{1,2},{2,3},{3,4},{4,5},{5,6},{6,7},{7,8},{8,9},{9,10},{10,1... | collective-permute-start | bytes 1179656 | tf_op jit(solution)/shard_map/ppermute | solution.py:19
  7.0 0.9 fusion.67
  8.0 2.9 %collective-permute-start.1 = (f32[2,1,3,128,128]{3,4,0,1,2:T(8,128)}, f32[2,1,3,128,128]{3,4,0,1,2:T(8,128)S(1)}, u32[]{:S(2)}, u32[]{:S(2)}) collective-permute-start(f32[2,1,3,128,128]{3,4,0,1,2:T(8,128)} %get-tuple-element.33), channel_id=1, source_target_pairs={{1,0},{2,1},{3,2},{4,3},{5,4},{6,5},{7,6},{8,7},{9,8},{10,9},{11,1... | collective-permute-start | bytes 1179656 | tf_op jit(solution)/shard_map/ppermute | solution.py:21
  14.1 6.0 %collective-permute-done.2 = f32[2,1,3,128,128]{3,4,1,2,0:T(8,128)} collective-permute-done((f32[2,1,3,128,128]{3,4,1,2,0:T(8,128)}, f32[2,1,3,128,128]{3,4,1,2,0:T(8,128)}, u32[]{:S(2)}, u32[]{:S(2)}) %collective-permute-start.2) | collective-permute-done | bytes 393248 | tf_op jit(solution)/shard_map/ppermute | solution.py:19
  20.1 2.5 %collective-permute-done.3 = f32[2,1,3,128,128]{3,4,1,2,0:T(8,128)} collective-permute-done((f32[2,1,3,128,128]{3,4,1,2,0:T(8,128)}, f32[2,1,3,128,128]{3,4,1,2,0:T(8,128)}, u32[]{:S(2)}, u32[]{:S(2)}) %collective-permute-start.3) | collective-permute-done | bytes 393248 | tf_op jit(solution)/shard_map/ppermute | solution.py:21
  22.6 1.2 %pad_maximum_fusion = f32[2,4,3,128,128]{3,4,1,2,0:T(8,128)S(1)} fusion(f32[2,1,3,128,128]{3,4,1,2,0:T(8,128)} %collective-permute-done.3, f32[1,2,3,128,128]{3,4,1,2,0:T(8,128)S(1)} %bitcast.500, f32[1,2,3,128,128]{3,4,1,2,0:T(8,128)S(1)} %bitcast.498, f32[2,1,3,128,128]{3,4,1,2,0:T(8,128)} %collective-permute-done.2), kind=kLoop, calls=%fused_computation | loop fusion | flops 1179648 | bytes 3145728 | tf_op jit(solution)/shard_map/concatenate | solution.py:17
  25.8 0.9 collective-permute-done.1
  32.5 2.0 %collective-permute-start.4 = (f32[2,1,3,128,128]{3,4,0,1,2:T(8,128)S(1)}, f32[2,1,3,128,128]{3,4,0,1,2:T(8,128)S(1)}, u32[]{:S(2)}, u32[]{:S(2)}) collective-permute-start(f32[2,1,3,128,128]{3,4,0,1,2:T(8,128)S(1)} %get-tuple-element.26), channel_id=1, source_target_pairs={{0,1},{1,2},{2,3},{3,4},{4,5},{5,6},{6,7},{7,8},{8,9},{9,10},{10,1... | collective-permute-start | bytes 1179656 | tf_op jit(solution)/shard_map/ppermute | solution.py:19
  35.3 8.3 %collective-permute-done.5 = f32[2,1,3,128,128]{3,4,0,1,2:T(8,128)S(1)} collective-permute-done((f32[2,1,3,128,128]{3,4,0,1,2:T(8,128)S(1)}, f32[2,1,3,128,128]{3,4,0,1,2:T(8,128)S(1)}, u32[]{:S(2)}, u32[]{:S(2)}) %collective-permute-start.5) | collective-permute-done | bytes 393248 | tf_op jit(solution)/shard_map/ppermute | solution.py:21
  44.8 0.4 fusion.33
  48.6 1.8 %collective-permute-start.6 = (f32[2,1,3,128,128]{3,4,0,1,2:T(8,128)S(1)}, f32[2,1,3,128,128]{3,4,0,1,2:T(8,128)S(1)}, u32[]{:S(2)}, u32[]{:S(2)}) collective-permute-start(f32[2,1,3,128,128]{3,4,0,1,2:T(8,128)S(1)} %get-tuple-element.22), channel_id=1, source_target_pairs={{0,1},{1,2},{2,3},{3,4},{4,5},{5,6},{6,7},{7,8},{8,9},{9,10},{10,1... | collective-permute-start | bytes 1179656 | tf_op jit(solution)/shard_map/ppermute | solution.py:19
  51.2 7.5 %collective-permute-done.7 = f32[2,1,3,128,128]{3,4,0,1,2:T(8,128)S(1)} collective-permute-done((f32[2,1,3,128,128]{3,4,0,1,2:T(8,128)S(1)}, f32[2,1,3,128,128]{3,4,0,1,2:T(8,128)S(1)}, u32[]{:S(2)}, u32[]{:S(2)}) %collective-permute-start.7) | collective-permute-done | bytes 393248 | tf_op jit(solution)/shard_map/ppermute | solution.py:21
  63.8 2.0 %collective-permute-start.8 = (f32[2,1,3,128,128]{3,4,0,1,2:T(8,128)S(1)}, f32[2,1,3,128,128]{3,4,0,1,2:T(8,128)S(1)}, u32[]{:S(2)}, u32[]{:S(2)}) collective-permute-start(f32[2,1,3,128,128]{3,4,0,1,2:T(8,128)S(1)} %get-tuple-element.18), channel_id=1, source_target_pairs={{0,1},{1,2},{2,3},{3,4},{4,5},{5,6},{6,7},{7,8},{8,9},{9,10},{10,1... | collective-permute-start | bytes 1179656 | tf_op jit(solution)/shard_map/ppermute | solution.py:19
  66.6 7.0 %collective-permute-done.9 = f32[2,1,3,128,128]{3,4,0,1,2:T(8,128)S(1)} collective-permute-done((f32[2,1,3,128,128]{3,4,0,1,2:T(8,128)S(1)}, f32[2,1,3,128,128]{3,4,0,1,2:T(8,128)S(1)}, u32[]{:S(2)}, u32[]{:S(2)}) %collective-permute-start.9) | collective-permute-done | bytes 393248 | tf_op jit(solution)/shard_map/ppermute | solution.py:21
  78.6 1.8 %collective-permute-start.10 = (f32[2,1,3,128,128]{3,4,0,1,2:T(8,128)S(1)}, f32[2,1,3,128,128]{3,4,0,1,2:T(8,128)S(1)}, u32[]{:S(2)}, u32[]{:S(2)}) collective-permute-start(f32[2,1,3,128,128]{3,4,0,1,2:T(8,128)S(1)} %get-tuple-element.14), channel_id=1, source_target_pairs={{0,1},{1,2},{2,3},{3,4},{4,5},{5,6},{6,7},{7,8},{8,9},{9,10},{10,1... | collective-permute-start | bytes 1179656 | tf_op jit(solution)/shard_map/ppermute | solution.py:19
  81.2 7.2 %collective-permute-done.11 = f32[2,1,3,128,128]{3,4,0,1,2:T(8,128)S(1)} collective-permute-done((f32[2,1,3,128,128]{3,4,0,1,2:T(8,128)S(1)}, f32[2,1,3,128,128]{3,4,0,1,2:T(8,128)S(1)}, u32[]{:S(2)}, u32[]{:S(2)}) %collective-permute-start.11) | collective-permute-done | bytes 393248 | tf_op jit(solution)/shard_map/ppermute | solution.py:21
  93.4 2.0 %collective-permute-start.12 = (f32[2,1,3,128,128]{3,4,0,1,2:T(8,128)S(1)}, f32[2,1,3,128,128]{3,4,0,1,2:T(8,128)S(1)}, u32[]{:S(2)}, u32[]{:S(2)}) collective-permute-start(f32[2,1,3,128,128]{3,4,0,1,2:T(8,128)S(1)} %get-tuple-element.10), channel_id=1, source_target_pairs={{0,1},{1,2},{2,3},{3,4},{4,5},{5,6},{6,7},{7,8},{8,9},{9,10},{10,1... | collective-permute-start | bytes 1179656 | tf_op jit(solution)/shard_map/ppermute | solution.py:19
  96.3 8.2 %collective-permute-done.13 = f32[2,1,3,128,128]{3,4,0,1,2:T(8,128)S(1)} collective-permute-done((f32[2,1,3,128,128]{3,4,0,1,2:T(8,128)S(1)}, f32[2,1,3,128,128]{3,4,0,1,2:T(8,128)S(1)}, u32[]{:S(2)}, u32[]{:S(2)}) %collective-permute-start.13) | collective-permute-done | bytes 393248 | tf_op jit(solution)/shard_map/ppermute | solution.py:21
  106.4 0.4 fusion.43
  106.8 0.9 copy.130
  107.8 0.9 copy.131
  (153 shorter events, 35.3 us)
Async XLA Ops:
  0.6 6.1 %copy-start.2 = (f32[2,3,128,128]{3,2,1,0:T(8,128)S(1)}, f32[2,3,128,128]{3,2,1,0:T(8,128)}, u32[]{:S(2)}) copy-start(f32[2,3,128,128]{3,2,1,0:T(8,128)} %param.6) | copy-start | bytes 1179652
  1.9 5.0 %copy-start.3 = (f32[2,3,128,128]{3,2,1,0:T(8,128)S(1)}, f32[2,3,128,128]{3,2,1,0:T(8,128)}, u32[]{:S(2)}) copy-start(f32[2,3,128,128]{3,2,1,0:T(8,128)} %param.7) | copy-start | bytes 1179652
  4.0 16.1 %collective-permute-start.2 = (f32[2,1,3,128,128]{3,4,1,2,0:T(8,128)}, f32[2,1,3,128,128]{3,4,1,2,0:T(8,128)}, u32[]{:S(2)}, u32[]{:S(2)}) collective-permute-start(f32[2,1,3,128,128]{3,4,1,2,0:T(8,128)} %get-tuple-element.30), channel_id=1, source_target_pairs={{0,1},{1,2},{2,3},{3,4},{4,5},{5,6},{6,7},{7,8},{8,9},{9,10},{10,1... | collective-permute-start | bytes 1179656 | tf_op jit(solution)/shard_map/ppermute | solution.py:19
  6.7 4.9 %copy-start = (f32[2,3,128,128]{3,2,1,0:T(8,128)S(1)}, f32[2,3,128,128]{3,2,1,0:T(8,128)}, u32[]{:S(2)}) copy-start(f32[2,3,128,128]{3,2,1,0:T(8,128)} %param.8) | copy-start | bytes 1179652
  6.7 4.9 %copy-start.1 = (f32[2,3,128,128]{3,2,1,0:T(8,128)S(1)}, f32[2,3,128,128]{3,2,1,0:T(8,128)}, u32[]{:S(2)}) copy-start(f32[2,3,128,128]{3,2,1,0:T(8,128)} %param.9) | copy-start | bytes 1179652
  6.7 15.9 %collective-permute-start.3 = (f32[2,1,3,128,128]{3,4,1,2,0:T(8,128)}, f32[2,1,3,128,128]{3,4,1,2,0:T(8,128)}, u32[]{:S(2)}, u32[]{:S(2)}) collective-permute-start(f32[2,1,3,128,128]{3,4,1,2,0:T(8,128)} %get-tuple-element.31), channel_id=1, source_target_pairs={{1,0},{2,1},{3,2},{4,3},{5,4},{6,5},{7,6},{8,7},{9,8},{10,9},{11,1... | collective-permute-start | bytes 1179656 | tf_op jit(solution)/shard_map/ppermute | solution.py:21
  8.0 18.8 %collective-permute-start.1 = (f32[2,1,3,128,128]{3,4,0,1,2:T(8,128)}, f32[2,1,3,128,128]{3,4,0,1,2:T(8,128)S(1)}, u32[]{:S(2)}, u32[]{:S(2)}) collective-permute-start(f32[2,1,3,128,128]{3,4,0,1,2:T(8,128)} %get-tuple-element.33), channel_id=1, source_target_pairs={{1,0},{2,1},{3,2},{4,3},{5,4},{6,5},{7,6},{8,7},{9,8},{10,9},{11,1... | collective-permute-start | bytes 1179656 | tf_op jit(solution)/shard_map/ppermute | solution.py:21
  10.9 17.4 %collective-permute-start = (f32[2,1,3,128,128]{3,4,0,1,2:T(8,128)}, f32[2,1,3,128,128]{3,4,0,1,2:T(8,128)S(1)}, u32[]{:S(2)}, u32[]{:S(2)}) collective-permute-start(f32[2,1,3,128,128]{3,4,0,1,2:T(8,128)} %get-tuple-element.32), channel_id=1, source_target_pairs={{0,1},{1,2},{2,3},{3,4},{4,5},{5,6},{6,7},{7,8},{8,9},{9,10},{10,1... | collective-permute-start | bytes 1179656 | tf_op jit(solution)/shard_map/ppermute | solution.py:19
  11.6 0.9 copy-start.4
  32.1 11.5 %collective-permute-start.5 = (f32[2,1,3,128,128]{3,4,0,1,2:T(8,128)S(1)}, f32[2,1,3,128,128]{3,4,0,1,2:T(8,128)S(1)}, u32[]{:S(2)}, u32[]{:S(2)}) collective-permute-start(f32[2,1,3,128,128]{3,4,0,1,2:T(8,128)S(1)} %get-tuple-element.27), channel_id=1, source_target_pairs={{1,0},{2,1},{3,2},{4,3},{5,4},{6,5},{7,6},{8,7},{9,8},{10,9},{11,1... | collective-permute-start | bytes 1179656 | tf_op jit(solution)/shard_map/ppermute | solution.py:21
  32.5 11.8 %collective-permute-start.4 = (f32[2,1,3,128,128]{3,4,0,1,2:T(8,128)S(1)}, f32[2,1,3,128,128]{3,4,0,1,2:T(8,128)S(1)}, u32[]{:S(2)}, u32[]{:S(2)}) collective-permute-start(f32[2,1,3,128,128]{3,4,0,1,2:T(8,128)S(1)} %get-tuple-element.26), channel_id=1, source_target_pairs={{0,1},{1,2},{2,3},{3,4},{4,5},{5,6},{6,7},{7,8},{8,9},{9,10},{10,1... | collective-permute-start | bytes 1179656 | tf_op jit(solution)/shard_map/ppermute | solution.py:19
  48.2 10.5 %collective-permute-start.7 = (f32[2,1,3,128,128]{3,4,0,1,2:T(8,128)S(1)}, f32[2,1,3,128,128]{3,4,0,1,2:T(8,128)S(1)}, u32[]{:S(2)}, u32[]{:S(2)}) collective-permute-start(f32[2,1,3,128,128]{3,4,0,1,2:T(8,128)S(1)} %get-tuple-element.23), channel_id=1, source_target_pairs={{1,0},{2,1},{3,2},{4,3},{5,4},{6,5},{7,6},{8,7},{9,8},{10,9},{11,1... | collective-permute-start | bytes 1179656 | tf_op jit(solution)/shard_map/ppermute | solution.py:21
  48.6 10.9 %collective-permute-start.6 = (f32[2,1,3,128,128]{3,4,0,1,2:T(8,128)S(1)}, f32[2,1,3,128,128]{3,4,0,1,2:T(8,128)S(1)}, u32[]{:S(2)}, u32[]{:S(2)}) collective-permute-start(f32[2,1,3,128,128]{3,4,0,1,2:T(8,128)S(1)} %get-tuple-element.22), channel_id=1, source_target_pairs={{0,1},{1,2},{2,3},{3,4},{4,5},{5,6},{6,7},{7,8},{8,9},{9,10},{10,1... | collective-permute-start | bytes 1179656 | tf_op jit(solution)/shard_map/ppermute | solution.py:19
  63.3 10.2 %collective-permute-start.9 = (f32[2,1,3,128,128]{3,4,0,1,2:T(8,128)S(1)}, f32[2,1,3,128,128]{3,4,0,1,2:T(8,128)S(1)}, u32[]{:S(2)}, u32[]{:S(2)}) collective-permute-start(f32[2,1,3,128,128]{3,4,0,1,2:T(8,128)S(1)} %get-tuple-element.19), channel_id=1, source_target_pairs={{1,0},{2,1},{3,2},{4,3},{5,4},{6,5},{7,6},{8,7},{9,8},{10,9},{11,1... | collective-permute-start | bytes 1179656 | tf_op jit(solution)/shard_map/ppermute | solution.py:21
  63.8 10.6 %collective-permute-start.8 = (f32[2,1,3,128,128]{3,4,0,1,2:T(8,128)S(1)}, f32[2,1,3,128,128]{3,4,0,1,2:T(8,128)S(1)}, u32[]{:S(2)}, u32[]{:S(2)}) collective-permute-start(f32[2,1,3,128,128]{3,4,0,1,2:T(8,128)S(1)} %get-tuple-element.18), channel_id=1, source_target_pairs={{0,1},{1,2},{2,3},{3,4},{4,5},{5,6},{6,7},{7,8},{8,9},{9,10},{10,1... | collective-permute-start | bytes 1179656 | tf_op jit(solution)/shard_map/ppermute | solution.py:19
  78.2 10.2 %collective-permute-start.11 = (f32[2,1,3,128,128]{3,4,0,1,2:T(8,128)S(1)}, f32[2,1,3,128,128]{3,4,0,1,2:T(8,128)S(1)}, u32[]{:S(2)}, u32[]{:S(2)}) collective-permute-start(f32[2,1,3,128,128]{3,4,0,1,2:T(8,128)S(1)} %get-tuple-element.15), channel_id=1, source_target_pairs={{1,0},{2,1},{3,2},{4,3},{5,4},{6,5},{7,6},{8,7},{9,8},{10,9},{11,1... | collective-permute-start | bytes 1179656 | tf_op jit(solution)/shard_map/ppermute | solution.py:21
  78.6 10.5 %collective-permute-start.10 = (f32[2,1,3,128,128]{3,4,0,1,2:T(8,128)S(1)}, f32[2,1,3,128,128]{3,4,0,1,2:T(8,128)S(1)}, u32[]{:S(2)}, u32[]{:S(2)}) collective-permute-start(f32[2,1,3,128,128]{3,4,0,1,2:T(8,128)S(1)} %get-tuple-element.14), channel_id=1, source_target_pairs={{0,1},{1,2},{2,3},{3,4},{4,5},{5,6},{6,7},{7,8},{8,9},{9,10},{10,1... | collective-permute-start | bytes 1179656 | tf_op jit(solution)/shard_map/ppermute | solution.py:19
  93.0 11.5 %collective-permute-start.13 = (f32[2,1,3,128,128]{3,4,0,1,2:T(8,128)S(1)}, f32[2,1,3,128,128]{3,4,0,1,2:T(8,128)S(1)}, u32[]{:S(2)}, u32[]{:S(2)}) collective-permute-start(f32[2,1,3,128,128]{3,4,0,1,2:T(8,128)S(1)} %get-tuple-element.11), channel_id=1, source_target_pairs={{1,0},{2,1},{3,2},{4,3},{5,4},{6,5},{7,6},{8,7},{9,8},{10,9},{11,1... | collective-permute-start | bytes 1179656 | tf_op jit(solution)/shard_map/ppermute | solution.py:21
  93.4 11.8 %collective-permute-start.12 = (f32[2,1,3,128,128]{3,4,0,1,2:T(8,128)S(1)}, f32[2,1,3,128,128]{3,4,0,1,2:T(8,128)S(1)}, u32[]{:S(2)}, u32[]{:S(2)}) collective-permute-start(f32[2,1,3,128,128]{3,4,0,1,2:T(8,128)S(1)} %get-tuple-element.10), channel_id=1, source_target_pairs={{0,1},{1,2},{2,3},{3,4},{4,5},{5,6},{6,7},{7,8},{8,9},{9,10},{10,1... | collective-permute-start | bytes 1179656 | tf_op jit(solution)/shard_map/ppermute | solution.py:19
where the time goes:
time: 109 us
  waiting for transfers between devices  47.8 us (44%)
  matrix products  31.4 us (29%)
  starting transfers between devices  15.4 us (14%)
  local copies, waits for them, and re-layouts  5.87 us (5%)
  other arithmetic  5.84 us (5%)
  between operations  2.35 us (2%)
    ppermute x7, waiting for transfers between devices, padded(): lax.ppermute(head, axis, [((i + 1) % count, i) for i in range(count)])  41.7 us
    dot_general x42, matrix products, apply_left(): jnp.einsum('rab,mrbc->mrac', operator_rows[:, offset_mid + half_band], pa...  16.1 us
    dot_general x42, matrix products, apply_right(): jnp.einsum('mrab,rbc->mrac', terms_here[:, :, offset_mid + half_band], pa...  15.4 us
    ppermute x7, starting transfers between devices, padded(): lax.ppermute(tail, axis, [(i, (i + 1) % count) for i in range(count)])  12.2 us
    ppermute x7, waiting for transfers between devices, padded(): lax.ppermute(tail, axis, [(i, (i + 1) % count) for i in range(count)])  6.05 us
    unnamed x22, local copies, waits for them, and re-layouts  5.18 us
    ppermute x7, starting transfers between devices, padded(): lax.ppermute(head, axis, [((i + 1) % count, i) for i in range(count)])  3.21 us
  transfers between devices with their start and end apart: 14, of which 8 were waited for; matrix products, arithmetic and copies ran while one was open for 16% of the time, Pallas kernels for 0%

commit v1 on v0

v1 whole, which is shorter than its diff:
```python
import functools

import jax
import jax.numpy as jnp
from jax import lax
from jax.experimental import pallas as pl
from jax.experimental.pallas import tpu as pltpu
from jax.sharding import PartitionSpec as P

TERMS = 6
BS = 128
time_step = 0.5
RING = ("row", "col")
f32, bf16 = jnp.float32, jnp.bfloat16

ROWS = 6
SIGN_RE = (1.0, -1.0, -1.0, 1.0, 1.0, -1.0)
SIGN_IM = (-1.0, -1.0, 1.0, 1.0, -1.0, -1.0)
PAYLOAD_ROWS = 7 * BS + 8


def own_index(row, offset):
    core = lax.axis_index("col")
    return jnp.where(core == 0, row, 1 - row), jnp.where(core == 0, 1 + offset, 1 - offset)


def own(ref, row, offset):
    r, e = own_index(row, offset)
    return ref[r, e]


def slot(ref, index):
    return ref[index * BS : (index + 1) * BS, :]


class Band:
    def __init__(self, high, low):
        self.high, self.low = high, low

    def put(self, i, j, value):
        part = slice((j - i + 1) * BS, (j - i + 2) * BS)
        high = value.astype(bf16)
        self.high[i, :, part] = high
        self.low[i, :, part] = (value - high.astype(f32)).astype(bf16)

    def put_parts(self, i, j, high, low):
        part = slice((j - i + 1) * BS, (j - i + 2) * BS)
        self.high[i, :, part] = high
        self.low[i, :, part] = low

    def get_parts(self, i, j):
        part = slice((j - i + 1) * BS, (j - i + 2) * BS)
        return self.high[i, :, part], self.low[i, :, part]

    def left(self, i, first, last):
        part = slice((first - i + 1) * BS, (last - i + 2) * BS)
        high, low = self.high[i, :, part], self.low[i, :, part]
        return [high, high, low]

    def right(self, first, last, j):
        highs, lows = [], []
        for k in range(first, last + 1):
            part = slice((j - k + 1) * BS, (j - k + 2) * BS)
            highs.append(self.high[k, :, part])
            lows.append(self.low[k, :, part])
        return highs + lows + highs


def commute(h, hn, x, i, first, last, j):
    left = jnp.concatenate(h.left(i, first, last) + x.left(i, first, last), axis=1)
    right = jnp.concatenate(x.right(first, last, j) + hn.right(first, last, j), axis=0)
    return jnp.dot(left, right, preferred_element_type=f32)


def diagonal(h, hn, x, i, scale):
    return commute(h, hn, x, i, i - 1, i + 1, i) * scale


def edge(h, hn, x, i, scale):
    return (
        commute(h, hn, x, i, i, i + 1, i + 1) * scale,
        commute(h, hn, x, i + 1, i, i + 1, i) * scale,
    )


def put_h(h, hn, i, j, value):
    h.put(i, j, value)
    high, low = h.get_parts(i, j)
    hn.put_parts(i, j, -high, -low)


def coefficient(term):
    return time_step / (term + 1)


def own_scale(pattern, term, row, offset):
    r, e = own_index(row, offset)
    return pattern[term, r, e].astype(f32) * coefficient(term)


def pack_kernel(re, im, ham, dip, field, pattern, out):
    f = field[0]
    for index, (row, offset) in enumerate(((0, 0), (0, 1), (1, -1), (1, 0))):
        out[index * BS : (index + 1) * BS, :] = own(re, row, offset) + own(im, row, offset)
    for index, (row, offset) in enumerate(((0, 0), (0, 1), (1, 0))):
        out[(4 + index) * BS : (5 + index) * BS, :] = own(ham, row, offset) + f * own(dip, row, offset)
    for term in range(TERMS):
        out[7 * BS + term : 7 * BS + term + 1, :] = jnp.full((1, BS), own_scale(pattern, term, 0, 1), f32)


def place_h_inner(h, hn, ham, dip, f, near):
    def op(row, offset):
        return own(ham, row, offset) + f * own(dip, row, offset)

    put_h(h, hn, 2, 2, op(0, 0))
    put_h(h, hn, 3, 3, op(1, 0))
    put_h(h, hn, 2, 3, op(0, 1))
    put_h(h, hn, 3, 2, op(1, -1))
    below = op(0, -1)
    put_h(h, hn, 2, 1, below)
    put_h(h, hn, 1, 2, below.T)
    above = op(1, 1)
    put_h(h, hn, 3, 4, above)
    put_h(h, hn, 4, 3, above.T)
    put_h(h, hn, 4, 4, slot(near, 6))
    put_h(h, hn, 5, 5, slot(near, 4))
    put_h(h, hn, 5, 4, slot(near, 5))
    put_h(h, hn, 4, 5, slot(near, 5).T)


def inner_levels(h, hn, xs, base, near, pattern, record):
    def put(level, i, j, value):
        record(level, i, j, value)
        if level < 3:
            xs[level].put(i, j, value)

    def own_edge(level, i):
        term = base + level - 1
        up, down = edge(h, hn, xs[level - 1], i, own_scale(pattern, term, i - 2, 1))
        put(level, i, i + 1, up)
        put(level, i + 1, i, down)

    def own_diagonal(level, i):
        put(level, i, i, diagonal(h, hn, xs[level - 1], i, coefficient(base + level - 1)))

    own_edge(1, 2)
    own_diagonal(1, 3)
    own_edge(1, 3)
    own_diagonal(1, 4)
    row = 7 * BS + base
    up, down = edge(h, hn, xs[0], 4, near[row : row + 1, :])
    put(1, 4, 5, up)
    put(1, 5, 4, down)
    own_diagonal(1, 2)
    own_edge(2, 2)
    own_diagonal(2, 3)
    own_edge(2, 3)
    own_diagonal(2, 4)
    own_diagonal(3, 3)
    own_edge(3, 3)


KEPT_X = ((0, 2, 2), (0, 1, 2), (0, 2, 1), (1, 2, 2), (1, 2, 3), (1, 3, 2), (2, 2, 3), (2, 3, 2), (2, 3, 3))
KEPT_H = ((2, 2), (1, 2), (2, 1), (2, 3), (3, 2), (3, 3))
INNER_TERMS = (
    (1, 2, 2), (1, 3, 3), (1, 2, 3), (1, 3, 2), (1, 3, 4), (1, 4, 3),
    (2, 3, 3), (2, 2, 3), (2, 3, 2), (2, 3, 4), (2, 4, 3),
    (3, 3, 3), (3, 3, 4), (3, 4, 3),
)
OUTER_TERMS = (
    (1, 2, 1), (1, 1, 2), (2, 2, 1), (2, 1, 2), (2, 2, 2),
    (3, 2, 1), (3, 1, 2), (3, 2, 2), (3, 2, 3), (3, 3, 2),
)


def keep(kept, h, xs):
    for index, (level, i, j) in enumerate(KEPT_X):
        high, low = xs[level].get_parts(i, j)
        kept[index, 0], kept[index, 1] = high, low
    for index, (i, j) in enumerate(KEPT_H):
        high, low = h.get_parts(i, j)
        kept[len(KEPT_X) + index, 0], kept[len(KEPT_X) + index, 1] = high, low


def bands(scratch):
    h_high, h_low, hn_high, hn_low, x_high, x_low = scratch
    h, hn = Band(h_high, h_low), Band(hn_high, hn_low)
    xs = [Band(x_high.at[level], x_low.at[level]) for level in range(3)]
    return h, hn, xs


def band_scratch():
    one = pltpu.VMEM((ROWS, BS, 3 * BS), bf16)
    three = pltpu.VMEM((3, ROWS, BS, 3 * BS), bf16)
    return [one, one, one, one, three, three]


def inner_first(re, im, ham, dip, near, field, pattern, kept, terms, *scratch):
    h, hn, xs = bands(scratch)
    place_h_inner(h, hn, ham, dip, field[0], near)
    x0 = xs[0]
    for (i, j), (row, offset) in (((2, 2), (0, 0)), ((3, 3), (1, 0)), ((2, 3), (0, 1)), ((3, 2), (1, -1))):
        x0.put(i, j, own(re, row, offset) + own(im, row, offset))
    x0.put(2, 1, own(re, 0, -1) + own(im, 0, -1))
    x0.put(1, 2, (own(re, 0, -1) - own(im, 0, -1)).T)
    x0.put(3, 4, own(re, 1, 1) + own(im, 1, 1))
    x0.put(4, 3, (own(re, 1, 1) - own(im, 1, 1)).T)
    for (i, j), index in (((4, 4), 3), ((5, 5), 0), ((4, 5), 2), ((5, 4), 1)):
        x0.put(i, j, slot(near, index))

    def record(level, i, j, value):
        if (level, i, j) in INNER_TERMS:
            terms[INNER_TERMS.index((level, i, j))] = value

    inner_levels(h, hn, xs, 0, near, pattern, record)
    keep(kept, h, xs)


def outer_levels(h, hn, xs, base, far, far_scales, kept, pattern, record):
    for index, (level, i, j) in enumerate(KEPT_X):
        xs[level].put_parts(i, j, kept[index, 0], kept[index, 1])
    for index, (i, j) in enumerate(KEPT_H):
        high, low = kept[len(KEPT_X) + index, 0], kept[len(KEPT_X) + index, 1]
        h.put_parts(i, j, high, low)
        hn.put_parts(i, j, -high, -low)
    put_h(h, hn, 1, 1, slot(far_scales, 4))
    put_h(h, hn, 0, 0, slot(far_scales, 6))
    put_h(h, hn, 1, 0, slot(far_scales, 5))
    put_h(h, hn, 0, 1, slot(far_scales, 5).T)
    for (i, j), index in (((1, 1), 0), ((0, 0), 3), ((1, 0), 1), ((0, 1), 2)):
        xs[0].put(i, j, slot(far, index))

    def put(level, i, j, value):
        record(level, i, j, value)
        if level < 3:
            xs[level].put(i, j, value)

    def do_edge(level, i, scale):
        up, down = edge(h, hn, xs[level - 1], i, scale)
        put(level, i, i + 1, up)
        put(level, i + 1, i, down)

    def do_diagonal(level, i):
        put(level, i, i, diagonal(h, hn, xs[level - 1], i, coefficient(base + level - 1)))

    row = 7 * BS + base
    cross = [own_scale(pattern, base + n, 0, -1) for n in range(3)]
    do_edge(1, 0, far_scales[row : row + 1, :])
    do_diagonal(1, 1)
    do_edge(1, 1, cross[0])
    do_diagonal(2, 1)
    do_edge(2, 1, cross[1])
    do_diagonal(2, 2)
    do_edge(3, 1, cross[2])
    do_diagonal(3, 2)
    do_edge(3, 2, own_scale(pattern, base + 2, 0, 1))


def outer_first(far, kept, inner_terms, pattern, state, terms, *scratch):
    h, hn, xs = bands(scratch)

    def record(level, i, j, value):
        if (level, i, j) in OUTER_TERMS:
            terms[OUTER_TERMS.index((level, i, j))] = value
        if level == 3 and (i, j) in ((2, 2), (2, 3), (3, 2)):
            index = ((2, 2), (2, 3), (3, 2)).index((i, j))
            state[index * BS : (index + 1) * BS, :] = value

    outer_levels(h, hn, xs, 0, far, far, kept, pattern, record)
    state[3 * BS : 4 * BS, :] = inner_terms[INNER_TERMS.index((3, 3, 3))]


def weighted(terms_of, signs):
    total = None
    for sign, value in zip(signs, terms_of):
        total = (value if sign > 0 else -value) if total is None else (total + value if sign > 0 else total - value)
    return total


def parts_of(values, i, j, levels, base):
    re_signs = [SIGN_RE[base + level - 1] for level in levels]
    im_signs = [SIGN_IM[base + level - 1] for level in levels]
    here = [values[(level, i, j)] for level in levels]
    there = here if i == j else [values[(level, j, i)] for level in levels]
    real = 0.5 * (weighted(here, re_signs) + weighted(there, re_signs).T)
    imag = 0.5 * (weighted(here, im_signs) - weighted(there, im_signs).T)
    return real, imag


def inner_second(
    re, im, ham, dip, near, state, near_state, terms_a, terms_b, field, pattern, kept, out_re, out_im, *scratch
):
    h, hn, xs = bands(scratch)
    place_h_inner(h, hn, ham, dip, field[0], near)
    x0 = xs[0]
    for (i, j), index in (((2, 2), 0), ((2, 3), 1), ((3, 2), 2), ((3, 3), 3)):
        x0.put(i, j, slot(state, index))
    for (i, j), index in (((4, 4), 3), ((5, 5), 0), ((4, 5), 2), ((5, 4), 1)):
        x0.put(i, j, slot(near_state, index))
    for i, j in ((3, 4), (4, 3)):
        x0.put(i, j, terms_a[INNER_TERMS.index((3, i, j))])
    for i, j in ((2, 1), (1, 2)):
        x0.put(i, j, terms_b[OUTER_TERMS.index((3, i, j))])

    values = {}

    def record(level, i, j, value):
        values[(level, i, j)] = value

    inner_levels(h, hn, xs, 3, near, pattern, record)
    keep(kept, h, xs)

    first = {}
    for index, key in enumerate(INNER_TERMS):
        first[key] = terms_a[index]
    for index, key in enumerate(OUTER_TERMS):
        first[key] = terms_b[index]

    def finish(row, offset, i, j, levels):
        r, e = own_index(row, offset)
        real, imag = parts_of(first, i, j, (1, 2, 3), 0)
        real, imag = re[r, e] + real, im[r, e] + imag
        if levels:
            more_real, more_imag = parts_of(values, i, j, levels, 3)
            real, imag = real + more_real, imag + more_imag
        out_re[r, e], out_im[r, e] = real, imag

    finish(0, -1, 2, 1, ())
    finish(0, 0, 2, 2, (1,))
    finish(0, 1, 2, 3, (1, 2))
    finish(1, -1, 3, 2, (1, 2))
    finish(1, 0, 3, 3, (1, 2, 3))
    finish(1, 1, 3, 4, (1, 2, 3))


def outer_second(far, far_state, kept, base_re, base_im, pattern, out_re, out_im, *scratch):
    h, hn, xs = bands(scratch)
    values = {}

    def record(level, i, j, value):
        values[(level, i, j)] = value

    outer_levels(h, hn, xs, 3, far_state, far, kept, pattern, record)

    def finish(row, offset, i, j, levels):
        r, e = own_index(row, offset)
        if levels:
            real, imag = parts_of(values, i, j, levels, 3)
            out_re[r, e], out_im[r, e] = base_re[r, e] + real, base_im[r, e] + imag
        else:
            out_re[r, e], out_im[r, e] = base_re[r, e], base_im[r, e]

    finish(0, -1, 2, 1, (1, 2, 3))
    finish(0, 0, 2, 2, (2, 3))
    finish(0, 1, 2, 3, (3,))
    finish(1, -1, 3, 2, (3,))
    finish(1, 0, 3, 3, ())
    finish(1, 1, 3, 4, ())


VECTOR = pl.BlockSpec(memory_space=pltpu.VMEM)
SCALAR = pl.BlockSpec(memory_space=pltpu.SMEM)


def call(kernel, specs, outs, scratch, flops):
    many = isinstance(outs, tuple)
    return pl.pallas_call(
        kernel,
        out_shape=outs,
        in_specs=specs,
        out_specs=(VECTOR,) * len(outs) if many else VECTOR,
        scratch_shapes=scratch,
        compiler_params=pltpu.CompilerParams(vmem_limit_bytes=32 * 2**20),
        cost_estimate=pl.CostEstimate(flops=flops, bytes_accessed=4 * 2**20, transcendentals=0),
    )


def body(density_real, density_imag, hamiltonian, dipole, field, pattern):
    count = lax.axis_size(RING)
    pair = [(i, i ^ 1) for i in range(count)]
    cross = [(i, (i + 1) % count if i % 2 else (i - 1) % count) for i in range(count)]
    shape = jax.ShapeDtypeStruct
    kept_shape = shape((len(KEPT_X) + len(KEPT_H), 2, BS, BS), bf16)
    block_shape = shape(density_real.shape, f32)

    packed = call(pack_kernel, [VECTOR] * 4 + [SCALAR] * 2, shape((PAYLOAD_ROWS, BS), f32), [], 10**6)(
        density_real, density_imag, hamiltonian, dipole, field, pattern
    )
    far = lax.ppermute(packed, RING, cross)
    near = lax.ppermute(packed, RING, pair)
    kept, terms_a = call(
        inner_first,
        [VECTOR] * 5 + [SCALAR] * 2,
        (kept_shape, shape((len(INNER_TERMS), BS, BS), f32)),
        band_scratch(),
        2 * 10**9,
    )(density_real, density_imag, hamiltonian, dipole, near, field, pattern)
    state, terms_b = call(
        outer_first,
        [VECTOR] * 3 + [SCALAR],
        (shape((4 * BS, BS), f32), shape((len(OUTER_TERMS), BS, BS), f32)),
        band_scratch(),
        2 * 10**9,
    )(far, kept, terms_a, pattern)
    far_state = lax.ppermute(state, RING, cross)
    near_state = lax.ppermute(state, RING, pair)
    kept, base_re, base_im = call(
        inner_second,
        [VECTOR] * 9 + [SCALAR] * 2,
        (kept_shape, block_shape, block_shape),
        band_scratch(),
        2 * 10**9,
    )(
        density_real, density_imag, hamiltonian, dipole, near, state, near_state, terms_a, terms_b, field, pattern
    )
    return call(
        outer_second,
        [VECTOR] * 5 + [SCALAR],
        (block_shape, block_shape),
        band_scratch(),
        2 * 10**9,
    )(far, far_state, kept, base_re, base_im, pattern)


def solution(mesh):
    in_specs = (
        P(("row", "col"), None, None, None),
        P(("row", "col"), None, None, None),
        P(("row", "col"), None, None, None),
        P(("parts", "row", "col"), None, None, None),
        P("parts"),
        P(None, ("row", "col"), None),
    )
    out_specs = (
        P(("parts", "row", "col"), None, None, None),
        P(("parts", "row", "col"), None, None, None),
    )
    return jax.shard_map(body, mesh=mesh, in_specs=in_specs, out_specs=out_specs, check_vma=False)
```

time: 109 us -> 37.1 us (0.34)
  the two profiles are of different devices: /device:TPU:1 before, /device:TPU:0 now
where the time goes in v1:
time: 37.1 us; the launch traced here: 36.8 us
  Pallas kernels  14.3 us (39%)
  starting transfers between devices  12.9 us (35%)
  local copies, waits for them, and re-layouts  4.77 us (13%)
  waiting for transfers between devices  3.43 us (9%)
  between operations  1.33 us (4%)
    ppermute x1, starting transfers between devices, body(): far = lax.ppermute(packed, RING, cross)  5.67 us
    ppermute x1, starting transfers between devices, body(): far_state = lax.ppermute(state, RING, cross)  4.78 us
    unnamed x17, local copies, waits for them, and re-layouts  4.77 us
    pallas_call x1, Pallas kernels, body(): call(outer_second, [VECTOR] * 5 + [SCALAR], (block_shape, block_shape), b...  3.84 us
    pallas_call x1, Pallas kernels, body(): call(inner_second, [VECTOR] * 9 + [SCALAR] * 2, (kept_shape, block_shape,...  3.57 us
    pallas_call x1, Pallas kernels, body(): call(inner_first, [VECTOR] * 5 + [SCALAR] * 2, (kept_shape, shape((len(IN...  3.36 us
    ppermute x1, waiting for transfers between devices, body(): far = lax.ppermute(packed, RING, cross)  2.94 us
    pallas_call x1, Pallas kernels, body(): call(outer_first, [VECTOR] * 3 + [SCALAR], (shape((4 * BS, BS), f32), sha...  2.87 us
  transfers between devices with their start and end apart: 4, of which 2 were waited for; matrix products, arithmetic and copies ran while one was open for 0% of the time, Pallas kernels for 19%

profile of v1, /device:TPU:0, one launch (start us, length us, event | category | flops | bytes accessed | tf_op | source)
XLA Modules:
  0.0 36.8 jit_solution(15407804809301648964)
XLA Ops:
  1.3 0.8 %copy.8.pattern = s32[6,2,3]{2,1,0:T(2,128)S(1)} copy(s32[6,2,3]{0,1,2:T(2,128)} %param.11) | data formatting | bytes 288 | tf_op args[5]
  2.1 0.0 copy-start
  2.1 1.0 %copy-done = f32[2,3,128,128]{3,2,1,0:T(8,128)S(1)} copy-done((f32[2,3,128,128]{3,2,1,0:T(8,128)S(1)}, f32[2,3,128,128]{3,2,1,0:T(8,128)}, u32[]{:S(2)}) %copy-start) | copy-done | bytes 393240
  3.0 0.0 copy-start.2
  3.1 1.0 %copy-done.2 = f32[2,3,128,128]{3,2,1,0:T(8,128)S(1)} copy-done((f32[2,3,128,128]{3,2,1,0:T(8,128)S(1)}, f32[2,3,128,128]{3,2,1,0:T(8,128)}, u32[]{:S(2)}) %copy-start.2) | copy-done | bytes 393240
  4.0 1.0 %copy-done.4 = f32[2,3,128,128]{3,2,1,0:T(8,128)S(1)} copy-done((f32[2,3,128,128]{3,2,1,0:T(8,128)S(1)}, f32[2,3,128,128]{3,2,1,0:T(8,128)}, u32[]{:S(2)}) %copy-start.4) | copy-done | bytes 393240
  5.0 1.0 %copy-done.6 = f32[2,3,128,128]{3,2,1,0:T(8,128)S(1)} copy-done((f32[2,3,128,128]{3,2,1,0:T(8,128)S(1)}, f32[2,3,128,128]{3,2,1,0:T(8,128)}, u32[]{:S(2)}) %copy-start.6) | copy-done | bytes 393240
  6.0 0.7 %shard_map.77 = f32[904,128]{1,0:T(8,128)S(1)} custom-call(f32[2,3,128,128]{3,2,1,0:T(8,128)S(1)} %copy-done, f32[2,3,128,128]{3,2,1,0:T(8,128)S(1)} %copy-done.2, f32[2,3,128,128]{3,2,1,0:T(8,128)S(1)} %copy-done.4, f32[2,3,128,128]{3,2,1,0:T(8,128)S(1)} %copy-done.6, f32[1]{0:T(128)S(6)} %copy.13.field, s32[6,2,3]{2,1,0:T(2,128)S(1)} %copy.8.pattern), custom_call_target="tpu_custom_call" | custom-call | flops 1000000 | bytes 4194304 | tf_op jit(solution)/shard_map/pallas_call | solution.py:386
  6.7 0.5 %collective-permute-start.1 = (f32[904,128]{1,0:T(8,128)S(1)}, f32[904,128]{1,0:T(8,128)S(1)}, u32[]{:S(2)}, u32[]{:S(2)}) collective-permute-start(f32[904,128]{1,0:T(8,128)S(1)} %shard_map.77), channel_id=1, source_target_pairs={{0,1},{1,0},{2,3},{3,2},{4,5},{5,4},{6,7},{7,6},{8,9},{9,8},{10,11... | collective-permute-start | bytes 1388552 | tf_op jit(solution)/shard_map/ppermute | solution.py:390
  7.3 5.7 %collective-permute-start = (f32[904,128]{1,0:T(8,128)S(1)}, f32[904,128]{1,0:T(8,128)S(1)}, u32[]{:S(2)}, u32[]{:S(2)}) collective-permute-start(f32[904,128]{1,0:T(8,128)S(1)} %shard_map.77), channel_id=1, source_target_pairs={{0,15},{1,2},{2,1},{3,4},{4,3},{5,6},{6,5},{7,8},{8,7},{9,10},{10,... | collective-permute-start | bytes 1388552 | tf_op jit(solution)/shard_map/ppermute | solution.py:389
  12.9 0.0 collective-permute-done.1.near
  12.9 3.4 %shard_map.78 = (bf16[15,2,128,128]{3,2,1,0:T(8,128)(2,1)S(1)}, f32[14,128,128]{2,1,0:T(8,128)S(1)}) custom-call(f32[2,3,128,128]{3,2,1,0:T(8,128)S(1)} %copy-done, f32[2,3,128,128]{3,2,1,0:T(8,128)S(1)} %copy-done.2, f32[2,3,128,128]{3,2,1,0:T(8,128)S(1)} %copy-done.4, f32[2,3,128,128]{3,2,1,0:T(8,128)S(1)} %copy-done.6, ...), custom_call_target="tpu_custom_call" | custom-call | flops 2000000000 | bytes 4194304 | tf_op jit(solution)/shard_map/pallas_call | solution.py:391
  16.3 2.9 %collective-permute-done.far = f32[904,128]{1,0:T(8,128)S(1)} collective-permute-done((f32[904,128]{1,0:T(8,128)S(1)}, f32[904,128]{1,0:T(8,128)S(1)}, u32[]{:S(2)}, u32[]{:S(2)}) %collective-permute-start) | collective-permute-done | bytes 462880 | tf_op jit(solution)/shard_map/ppermute | solution.py:389
  19.2 2.9 %shard_map.79 = (f32[512,128]{1,0:T(8,128)S(1)}, f32[10,128,128]{2,1,0:T(8,128)S(1)}) custom-call(f32[904,128]{1,0:T(8,128)S(1)} %collective-permute-done.far, bf16[15,2,128,128]{3,2,1,0:T(8,128)(2,1)S(1)} %get-tuple-element.9.kept, f32[14,128,128]{2,1,0:T(8,128)S(1)} %get-tuple-element.10.inner_terms.terms_a, s32[6,2,3]{2,1,0:T(2,128)S(1)} %copy.8.pattern), custom_call_target="tpu_custom_call" | custom-call | flops 2000000000 | bytes 4194304 | tf_op jit(solution)/shard_map/pallas_call | solution.py:398
  22.1 2.0 %collective-permute-start.3 = (f32[512,128]{1,0:T(8,128)S(1)}, f32[512,128]{1,0:T(8,128)S(1)}, u32[]{:S(2)}, u32[]{:S(2)}) collective-permute-start(f32[512,128]{1,0:T(8,128)S(1)} %get-tuple-element.11.state), channel_id=1, source_target_pairs={{0,1},{1,0},{2,3},{3,2},{4,5},{5,4},{6,7},{7,6},{8,9},{9,8},{10,11... | collective-permute-start | bytes 786440 | tf_op jit(solution)/shard_map/ppermute | solution.py:406
  24.1 4.8 %collective-permute-start.2 = (f32[512,128]{1,0:T(8,128)S(1)}, f32[512,128]{1,0:T(8,128)S(1)}, u32[]{:S(2)}, u32[]{:S(2)}) collective-permute-start(f32[512,128]{1,0:T(8,128)S(1)} %get-tuple-element.11.state), channel_id=1, source_target_pairs={{0,15},{1,2},{2,1},{3,4},{4,3},{5,6},{6,5},{7,8},{8,7},{9,10},{10,... | collective-permute-start | bytes 786440 | tf_op jit(solution)/shard_map/ppermute | solution.py:405
  28.9 0.0 collective-permute-done.3.near_state
  28.9 0.0 copy-done.1
  28.9 0.0 copy-done.3
  28.9 0.0 copy-done.5
  28.9 0.0 copy-done.7
  28.9 3.6 %shard_map.80 = (bf16[15,2,128,128]{3,2,1,0:T(8,128)(2,1)S(1)}, f32[2,3,128,128]{3,2,1,0:T(8,128)S(1)}, f32[2,3,128,128]{3,2,1,0:T(8,128)S(1)}) custom-call(f32[2,3,128,128]{3,2,1,0:T(8,128)S(1)} %copy-done.1, f32[2,3,128,128]{3,2,1,0:T(8,128)S(1)} %copy-done.3, f32[2,3,128,128]{3,2,1,0:T(8,128)S(1)} %copy-done.5, f32[2,3,128,128]{3,2,1,0:T(8,128)S(1)} %copy-done.7, ...), custom_call_target="tpu_custom_call" | custom-call | flops 2000000000 | bytes 4194304 | tf_op jit(solution)/shard_map/pallas_call | solution.py:407
  32.5 0.5 %collective-permute-done.2.far_state = f32[512,128]{1,0:T(8,128)S(1)} collective-permute-done((f32[512,128]{1,0:T(8,128)S(1)}, f32[512,128]{1,0:T(8,128)S(1)}, u32[]{:S(2)}, u32[]{:S(2)}) %collective-permute-start.2) | collective-permute-done | bytes 262176 | tf_op jit(solution)/shard_map/ppermute | solution.py:405
  33.0 3.8 %shard_map.81 = (f32[2,3,128,128]{3,2,1,0:T(8,128)}, f32[2,3,128,128]{3,2,1,0:T(8,128)}) custom-call(f32[904,128]{1,0:T(8,128)S(1)} %collective-permute-done.far, f32[512,128]{1,0:T(8,128)S(1)} %collective-permute-done.2.far_state, bf16[15,2,128,128]{3,2,1,0:T(8,128)(2,1)S(1)} %get-tuple-element.13.kept, f32[2,3,128,128]{3,2,1,0:T(8,128)S(1)} %get-tuple-element.14.base_re, ...), custom_call_target="tpu_custom_call" | custom-call | flops 2000000000 | bytes 4194304 | tf_op jit(solution)/shard_map/pallas_call | solution.py:416
  (6 shorter events, 0.0 us)
Async XLA Ops:
  2.1 1.0 %copy-start = (f32[2,3,128,128]{3,2,1,0:T(8,128)S(1)}, f32[2,3,128,128]{3,2,1,0:T(8,128)}, u32[]{:S(2)}) copy-start(f32[2,3,128,128]{3,2,1,0:T(8,128)} %re.5) | copy-start | bytes 1179652
  3.0 1.0 %copy-start.2 = (f32[2,3,128,128]{3,2,1,0:T(8,128)S(1)}, f32[2,3,128,128]{3,2,1,0:T(8,128)}, u32[]{:S(2)}) copy-start(f32[2,3,128,128]{3,2,1,0:T(8,128)} %im.5) | copy-start | bytes 1179652
  4.0 1.0 %copy-start.4 = (f32[2,3,128,128]{3,2,1,0:T(8,128)S(1)}, f32[2,3,128,128]{3,2,1,0:T(8,128)}, u32[]{:S(2)}) copy-start(f32[2,3,128,128]{3,2,1,0:T(8,128)} %ham.5) | copy-start | bytes 1179652
  5.0 1.0 %copy-start.6 = (f32[2,3,128,128]{3,2,1,0:T(8,128)S(1)}, f32[2,3,128,128]{3,2,1,0:T(8,128)}, u32[]{:S(2)}) copy-start(f32[2,3,128,128]{3,2,1,0:T(8,128)} %dip.5) | copy-start | bytes 1179652
  6.7 6.2 %collective-permute-start.1 = (f32[904,128]{1,0:T(8,128)S(1)}, f32[904,128]{1,0:T(8,128)S(1)}, u32[]{:S(2)}, u32[]{:S(2)}) collective-permute-start(f32[904,128]{1,0:T(8,128)S(1)} %shard_map.77), channel_id=1, source_target_pairs={{0,1},{1,0},{2,3},{3,2},{4,5},{5,4},{6,7},{7,6},{8,9},{9,8},{10,11... | collective-permute-start | bytes 1388552 | tf_op jit(solution)/shard_map/ppermute | solution.py:390
  7.3 12.0 %collective-permute-start = (f32[904,128]{1,0:T(8,128)S(1)}, f32[904,128]{1,0:T(8,128)S(1)}, u32[]{:S(2)}, u32[]{:S(2)}) collective-permute-start(f32[904,128]{1,0:T(8,128)S(1)} %shard_map.77), channel_id=1, source_target_pairs={{0,15},{1,2},{2,1},{3,4},{4,3},{5,6},{6,5},{7,8},{8,7},{9,10},{10,... | collective-permute-start | bytes 1388552 | tf_op jit(solution)/shard_map/ppermute | solution.py:389
  19.2 9.6 %copy-start.1 = (f32[2,3,128,128]{3,2,1,0:T(8,128)S(1)}, f32[2,3,128,128]{3,2,1,0:T(8,128)}, u32[]{:S(2)}) copy-start(f32[2,3,128,128]{3,2,1,0:T(8,128)} %re.5) | copy-start | bytes 1179652
  19.2 9.6 %copy-start.3 = (f32[2,3,128,128]{3,2,1,0:T(8,128)S(1)}, f32[2,3,128,128]{3,2,1,0:T(8,128)}, u32[]{:S(2)}) copy-start(f32[2,3,128,128]{3,2,1,0:T(8,128)} %im.5) | copy-start | bytes 1179652
  19.2 9.6 %copy-start.5 = (f32[2,3,128,128]{3,2,1,0:T(8,128)S(1)}, f32[2,3,128,128]{3,2,1,0:T(8,128)}, u32[]{:S(2)}) copy-start(f32[2,3,128,128]{3,2,1,0:T(8,128)} %ham.5) | copy-start | bytes 1179652
  19.2 9.6 %copy-start.7 = (f32[2,3,128,128]{3,2,1,0:T(8,128)S(1)}, f32[2,3,128,128]{3,2,1,0:T(8,128)}, u32[]{:S(2)}) copy-start(f32[2,3,128,128]{3,2,1,0:T(8,128)} %dip.5) | copy-start | bytes 1179652
  22.1 6.7 %collective-permute-start.3 = (f32[512,128]{1,0:T(8,128)S(1)}, f32[512,128]{1,0:T(8,128)S(1)}, u32[]{:S(2)}, u32[]{:S(2)}) collective-permute-start(f32[512,128]{1,0:T(8,128)S(1)} %get-tuple-element.11.state), channel_id=1, source_target_pairs={{0,1},{1,0},{2,3},{3,2},{4,5},{5,4},{6,7},{7,6},{8,9},{9,8},{10,11... | collective-permute-start | bytes 786440 | tf_op jit(solution)/shard_map/ppermute | solution.py:406
  24.1 8.9 %collective-permute-start.2 = (f32[512,128]{1,0:T(8,128)S(1)}, f32[512,128]{1,0:T(8,128)S(1)}, u32[]{:S(2)}, u32[]{:S(2)}) collective-permute-start(f32[512,128]{1,0:T(8,128)S(1)} %get-tuple-element.11.state), channel_id=1, source_target_pairs={{0,15},{1,2},{2,1},{3,4},{4,3},{5,6},{6,5},{7,8},{8,7},{9,10},{10,... | collective-permute-start | bytes 786440 | tf_op jit(solution)/shard_map/ppermute | solution.py:405

commit v2 on v0

v2 whole, which is shorter than its diff:
```python
import functools

import jax
import jax.numpy as jnp
from jax import lax
from jax.experimental import pallas as pl
from jax.experimental.pallas import tpu as pltpu
from jax.sharding import PartitionSpec as P

TERMS = 6
BS = 128
time_step = 0.5
RING = ("row", "col")
f32, bf16 = jnp.float32, jnp.bfloat16

ROWS = 6
SIGN_RE = (1.0, -1.0, -1.0, 1.0, 1.0, -1.0)
SIGN_IM = (-1.0, -1.0, 1.0, 1.0, -1.0, -1.0)
PAYLOAD_ROWS = 7 * BS + 8


def own_index(row, offset):
    core = lax.axis_index("col")
    return jnp.where(core == 0, row, 1 - row), jnp.where(core == 0, 1 + offset, 1 - offset)


def own(ref, row, offset):
    r, e = own_index(row, offset)
    return ref[r, e]


def slot(ref, index):
    return ref[index * BS : (index + 1) * BS, :]


class Band:
    def __init__(self, high, low):
        self.high, self.low = high, low

    def put(self, i, j, value):
        part = slice((j - i + 1) * BS, (j - i + 2) * BS)
        high = value.astype(bf16)
        self.high[i, :, part] = high
        self.low[i, :, part] = (value - high.astype(f32)).astype(bf16)

    def put_parts(self, i, j, high, low):
        part = slice((j - i + 1) * BS, (j - i + 2) * BS)
        self.high[i, :, part] = high
        self.low[i, :, part] = low

    def get_parts(self, i, j):
        part = slice((j - i + 1) * BS, (j - i + 2) * BS)
        return self.high[i, :, part], self.low[i, :, part]

    def left(self, i, first, last):
        part = slice((first - i + 1) * BS, (last - i + 2) * BS)
        high, low = self.high[i, :, part], self.low[i, :, part]
        return [high, high, low]

    def right(self, first, last, j, j_last):
        highs, lows = [], []
        for k in range(first, last + 1):
            part = slice((j - k + 1) * BS, (j_last - k + 2) * BS)
            highs.append(self.high[k, :, part])
            lows.append(self.low[k, :, part])
        return highs + lows + highs


def piece(h, hn, x, rows, mids, cols):
    left = jnp.concatenate(
        [jnp.concatenate(h.left(i, *mids) + x.left(i, *mids), axis=1) for i in range(rows[0], rows[1] + 1)], axis=0
    )
    right = jnp.concatenate(x.right(*mids, *cols) + hn.right(*mids, *cols), axis=0)
    return jnp.dot(left, right, preferred_element_type=f32)


def one_side(a, b, row, mids, col):
    left = jnp.concatenate(a.left(row, *mids), axis=1)
    right = jnp.concatenate(b.right(*mids, col, col), axis=0)
    return jnp.dot(left, right, preferred_element_type=f32)


def corners(tile):
    return tile[:BS, :BS], tile[:BS, BS:], tile[BS:, :BS], tile[BS:, BS:]


def put_h(h, hn, i, j, value):
    h.put(i, j, value)
    high, low = h.get_parts(i, j)
    hn.put_parts(i, j, -high, -low)


def put_h_parts(h, hn, i, j, high, low):
    h.put_parts(i, j, high, low)
    hn.put_parts(i, j, -high, -low)


def coefficient(term):
    return time_step / (term + 1)


def own_scale(pattern, term, row, offset):
    r, e = own_index(row, offset)
    return pattern[e, r, term].astype(f32) * coefficient(term)


INNER_H = ((2, 2), (3, 3), (2, 3), (3, 2), (2, 1), (1, 2), (3, 4), (4, 3), (4, 4), (5, 5), (5, 4), (4, 5))
KEPT_X = ((0, 1, 2), (0, 2, 1), (1, 2, 2))
KEPT_H = ((1, 2), (2, 1), (2, 2), (2, 3), (3, 2))
SUMS = ((1, 1, 1), (1, 1, 2), (1, 2, 1), (2, 2, 2), (3, 2, 2), (3, 2, 3), (3, 3, 2))
OUTER_TERMS = ((1, 2, 1), (1, 1, 2), (2, 2, 1), (2, 1, 2), (3, 2, 1), (3, 1, 2), (2, 2, 2))
STATE = ((2, 2), (2, 3), (3, 2), (3, 3))


def pack_kernel(re, im, ham, dip, field, pattern, out, dens, oper, sems):
    copies = []
    for a, ref in enumerate((re, im)):
        for r in range(2):
            copies.append(pltpu.make_async_copy(ref.at[r, pl.ds(1 - r, 2)], dens.at[a, r], sems.at[len(copies)]))
    for a, ref in enumerate((ham, dip)):
        for n, (row, offset) in enumerate(((0, 0), (0, 1), (1, 0))):
            r, e = own_index(row, offset)
            copies.append(pltpu.make_async_copy(ref.at[r, e], oper.at[a, n], sems.at[len(copies)]))
    for copy in copies:
        copy.start()
    for term in range(TERMS):
        out[7 * BS + term : 7 * BS + term + 1, :] = jnp.full((1, BS), own_scale(pattern, term, 0, 1), f32)
    for copy in copies[:4]:
        copy.wait()
    for index, (row, offset) in enumerate(((0, 0), (0, 1), (1, -1), (1, 0))):
        r, e = own_index(row, offset)
        out[index * BS : (index + 1) * BS, :] = dens[0, r, e - 1 + r] + dens[1, r, e - 1 + r]
    for copy in copies[4:]:
        copy.wait()
    for n in range(3):
        out[(4 + n) * BS : (5 + n) * BS, :] = oper[0, n] + field[0] * oper[1, n]


def inner_levels(h, hn, xs, base, near, pattern, sums, record):
    def put(level, i, j, value):
        record(level, i, j, value)
        if level < 3:
            xs[level].put(i, j, value)

    def own_edge(level, i, up, down, scale=None):
        scale = own_scale(pattern, base + level - 1, i - 2, 1) if scale is None else scale
        put(level, i, i + 1, up * scale)
        put(level, i + 1, i, down * scale)

    def own_diagonal(level, i, total):
        put(level, i, i, total * coefficient(base + level - 1))

    def tile(level, i):
        return corners(piece(h, hn, xs[level - 1], (i, i + 1), (i, i + 1), (i, i + 1)))

    def part(level, i, k, j):
        return piece(h, hn, xs[level - 1], (i, i), (k, k), (j, j))

    def keep(level, i, j, value):
        sums[SUMS.index((level, i, j))] = value

    t2, t3, t4 = tile(1, 2), tile(1, 3), tile(1, 4)
    own_edge(1, 2, t2[1], t2[2])
    own_edge(1, 3, t3[1], t3[2])
    own_diagonal(1, 3, t2[3] + t3[0] - part(1, 3, 3, 3))
    own_diagonal(1, 4, t3[3] + t4[0] - part(1, 4, 4, 4))
    row = 7 * BS + base
    own_edge(1, 4, t4[1], t4[2], near[row : row + 1, :])
    own_diagonal(1, 2, part(1, 2, 1, 2) + t2[0])
    t2, t3 = tile(2, 2), tile(2, 3)
    own_edge(2, 2, t2[1], t2[2])
    own_diagonal(2, 3, t2[3] + t3[0] - part(2, 3, 3, 3))
    own_edge(2, 3, t3[1], t3[2])
    own_diagonal(2, 4, t3[3] + part(2, 4, 5, 4))
    t3 = tile(3, 3)
    own_edge(3, 3, t3[1], t3[2])
    own_diagonal(3, 3, t3[0] + part(3, 3, 2, 3))
    keep(1, 1, 1, part(1, 1, 2, 1))
    keep(1, 1, 2, part(1, 1, 2, 2))
    keep(1, 2, 1, part(1, 2, 2, 1))
    keep(2, 2, 2, part(2, 2, 3, 2))
    keep(3, 2, 2, part(3, 2, 3, 2))
    x2 = xs[2]
    keep(3, 2, 3, one_side(h, x2, 2, (2, 3), 3) + one_side(x2, hn, 2, (3, 3), 3))
    keep(3, 3, 2, one_side(h, x2, 3, (3, 3), 2) + one_side(x2, hn, 3, (2, 3), 2))


def keep_parts(kept, h, xs):
    for index, (level, i, j) in enumerate(KEPT_X):
        kept[index, 0], kept[index, 1] = xs[level].get_parts(i, j)
    for index, (i, j) in enumerate(KEPT_H):
        kept[len(KEPT_X) + index, 0], kept[len(KEPT_X) + index, 1] = h.get_parts(i, j)


def bands(scratch):
    h_high, h_low, hn_high, hn_low, x_high, x_low = scratch
    h, hn = Band(h_high, h_low), Band(hn_high, hn_low)
    xs = [Band(x_high.at[level], x_low.at[level]) for level in range(3)]
    return h, hn, xs


def band_scratch():
    one = pltpu.VMEM((ROWS, BS, 3 * BS), bf16)
    three = pltpu.VMEM((3, ROWS, BS, 3 * BS), bf16)
    return [one, one, one, one, three, three]


def weighted(terms_of, signs):
    total = None
    for sign, value in zip(signs, terms_of):
        total = (value if sign > 0 else -value) if total is None else (total + value if sign > 0 else total - value)
    return total


def parts_of(values, i, j, terms):
    re_signs, im_signs = [SIGN_RE[term] for term in terms], [SIGN_IM[term] for term in terms]
    here = [values[(term, i, j)] for term in terms]
    there = here if i == j else [values[(term, j, i)] for term in terms]
    real = 0.5 * (weighted(here, re_signs) + weighted(there, re_signs).T)
    imag = 0.5 * (weighted(here, im_signs) - weighted(there, im_signs).T)
    return real, imag


OWN = (((0, -1), (2, 1)), ((0, 0), (2, 2)), ((0, 1), (2, 3)), ((1, -1), (3, 2)), ((1, 0), (3, 3)), ((1, 1), (3, 4)))
INNER_DONE = {(2, 1): (), (2, 2): (1,), (2, 3): (1, 2), (3, 2): (1, 2), (3, 3): (1, 2, 3), (3, 4): (1, 2, 3)}
OUTER_DONE = {(2, 1): (1, 2, 3), (2, 2): (2, 3), (2, 3): (3,), (3, 2): (3,)}


def inner_first(
    re, im, ham, dip, near, field, pattern, kept, sums, h_kept, base, state, re_in, im_in, ham_in, dip_in, sems, *scratch
):
    copies = [
        pltpu.make_async_copy(source, target, sems.at[n])
        for n, (source, target) in enumerate(((ham, ham_in), (dip, dip_in), (re, re_in), (im, im_in)))
    ]
    for copy in copies:
        copy.start()
    h, hn, xs = bands(scratch)
    x0 = xs[0]
    put_h(h, hn, 4, 4, slot(near, 6))
    put_h(h, hn, 5, 5, slot(near, 4))
    put_h(h, hn, 5, 4, slot(near, 5))
    put_h(h, hn, 4, 5, slot(near, 5).T)
    for (i, j), index in (((4, 4), 3), ((5, 5), 0), ((4, 5), 2), ((5, 4), 1)):
        x0.put(i, j, slot(near, index))
    for copy in copies:
        copy.wait()
    for (row, offset), (i, j) in OWN:
        value = own(ham_in, row, offset) + field[0] * own(dip_in, row, offset)
        put_h(h, hn, i, j, value)
        if (j, i) in ((1, 2), (4, 3)):
            put_h(h, hn, j, i, value.T)
        real, imag = own(re_in, row, offset), own(im_in, row, offset)
        x0.put(i, j, real + imag)
        if (j, i) in ((1, 2), (4, 3)):
            x0.put(j, i, (real - imag).T)

    values = {}

    def record(level, i, j, value):
        values[(level - 1, i, j)] = value
        if level == 3:
            if (i, j) == (3, 3):
                state[0] = value
            if (i, j) == (3, 4):
                state[1] = value
            if (i, j) == (4, 3):
                state[2] = value

    inner_levels(h, hn, xs, 0, near, pattern, sums, record)
    keep_parts(kept, h, xs)
    for index, (i, j) in enumerate(INNER_H):
        h_kept[index, 0], h_kept[index, 1] = h.get_parts(i, j)
    for index, ((row, offset), (i, j)) in enumerate(OWN):
        real, imag = own(re_in, row, offset), own(im_in, row, offset)
        terms = [level - 1 for level in INNER_DONE[(i, j)]]
        if terms:
            more_real, more_imag = parts_of(values, i, j, terms)
            real, imag = real + more_real, imag + more_imag
        base[index, 0], base[index, 1] = real, imag


def outer_levels(h, hn, xs, base, far, far_payload, kept, sums, pattern, record):
    for index, (level, i, j) in enumerate(KEPT_X):
        xs[level].put_parts(i, j, kept[index, 0], kept[index, 1])
    for index, (i, j) in enumerate(KEPT_H):
        put_h_parts(h, hn, i, j, kept[len(KEPT_X) + index, 0], kept[len(KEPT_X) + index, 1])
    put_h(h, hn, 1, 1, slot(far_payload, 4))
    put_h(h, hn, 0, 0, slot(far_payload, 6))
    put_h(h, hn, 1, 0, slot(far_payload, 5))
    put_h(h, hn, 0, 1, slot(far_payload, 5).T)
    for (i, j), index in (((1, 1), 0), ((0, 0), 3), ((1, 0), 1), ((0, 1), 2)):
        xs[0].put(i, j, slot(far, index))

    def put(level, i, j, value):
        record(level, i, j, value)
        if level < 3:
            xs[level].put(i, j, value)

    def part(level, i, k, j):
        return piece(h, hn, xs[level - 1], (i, i), (k, k), (j, j))

    def tile(level, i):
        return corners(piece(h, hn, xs[level - 1], (i, i + 1), (i, i + 1), (i, i + 1)))

    def known(level, i, j):
        return sums[SUMS.index((level, i, j))]

    row = 7 * BS + base
    cross = [own_scale(pattern, base + n, 0, -1) for n in range(3)]
    c = [coefficient(base + n) for n in range(3)]
    t0 = tile(1, 0)
    scale = far_payload[row : row + 1, :]
    put(1, 0, 1, t0[1] * scale)
    put(1, 1, 0, t0[2] * scale)
    put(1, 1, 1, (t0[3] + known(1, 1, 1)) * c[0])
    put(1, 1, 2, (part(1, 1, 1, 2) + known(1, 1, 2)) * cross[0])
    put(1, 2, 1, (part(1, 2, 1, 1) + known(1, 2, 1)) * cross[0])
    t1 = tile(2, 1)
    put(2, 1, 1, (part(2, 1, 0, 1) + t1[0]) * c[1])
    put(2, 1, 2, t1[1] * cross[1])
    put(2, 2, 1, t1[2] * cross[1])
    put(2, 2, 2, (t1[3] + known(2, 2, 2)) * c[1])
    t1 = tile(3, 1)
    put(3, 1, 2, t1[1] * cross[2])
    put(3, 2, 1, t1[2] * cross[2])
    put(3, 2, 2, (t1[3] + known(3, 2, 2)) * c[2])
    scale = own_scale(pattern, base + 2, 0, 1)
    put(3, 2, 3, (one_side(xs[2], hn, 2, (2, 2), 3) + known(3, 2, 3)) * scale)
    put(3, 3, 2, (one_side(h, xs[2], 3, (2, 2), 2) + known(3, 3, 2)) * scale)


def outer_first(far, kept, sums, inner_state, pattern, state, terms, *scratch):
    h, hn, xs = bands(scratch)

    def record(level, i, j, value):
        if (level, i, j) in OUTER_TERMS:
            terms[OUTER_TERMS.index((level, i, j))] = value
        if level == 3 and (i, j) in STATE:
            index = STATE.index((i, j))
            state[index * BS : (index + 1) * BS, :] = value

    outer_levels(h, hn, xs, 0, far, far, kept, sums, pattern, record)
    state[3 * BS : 4 * BS, :] = inner_state[0]


def inner_second(
    near, state, near_state, inner_state, terms, h_kept, base, pattern,
    kept, sums, base_out, out_re, out_im, stage, sems, *scratch
):
    h, hn, xs = bands(scratch)
    x0 = xs[0]
    for index, (i, j) in enumerate(INNER_H):
        put_h_parts(h, hn, i, j, h_kept[index, 0], h_kept[index, 1])
    for index, (i, j) in enumerate(STATE):
        x0.put(i, j, slot(state, index))
    for (i, j), index in (((4, 4), 3), ((5, 5), 0), ((4, 5), 2), ((5, 4), 1)):
        x0.put(i, j, slot(near_state, index))
    x0.put(3, 4, inner_state[1])
    x0.put(4, 3, inner_state[2])
    for i, j in ((2, 1), (1, 2)):
        x0.put(i, j, terms[OUTER_TERMS.index((3, i, j))])

    values = {(level - 1, i, j): (terms, index) for index, (level, i, j) in enumerate(OUTER_TERMS)}
    values = {key: ref[index] for key, (ref, index) in values.items()}
    for index, (i, j) in enumerate(STATE):
        values[(2, i, j)] = slot(state, index)

    def record(level, i, j, value):
        values[(level + 2, i, j)] = value

    inner_levels(h, hn, xs, 3, near, pattern, sums, record)
    keep_parts(kept, h, xs)
    for index, ((row, offset), (i, j)) in enumerate(OWN):
        real, imag = base[index, 0], base[index, 1]
        terms_here = [level - 1 for level in OUTER_DONE.get((i, j), ())] + [level + 2 for level in INNER_DONE[(i, j)]]
        more_real, more_imag = parts_of(values, i, j, terms_here)
        real, imag = real + more_real, imag + more_imag
        if index < 4:
            base_out[index, 0], base_out[index, 1] = real, imag
        else:
            stage[index - 4, 0], stage[index - 4, 1] = real, imag
    copies = []
    for n, (row, offset) in enumerate(((1, 0), (1, 1))):
        r, e = own_index(row, offset)
        for a, out in enumerate((out_re, out_im)):
            copies.append(pltpu.make_async_copy(stage.at[n, a], out.at[r, e], sems.at[len(copies)]))
    for copy in copies:
        copy.start()
    for copy in copies:
        copy.wait()


def outer_second(
    far, far_state, kept, sums, base, in_re, in_im, pattern, out_re, out_im, stage, sems, *scratch
):
    h, hn, xs = bands(scratch)
    values = {}

    def record(level, i, j, value):
        values[(level + 2, i, j)] = value

    outer_levels(h, hn, xs, 3, far_state, far, kept, sums, pattern, record)
    copies = []
    for index, ((row, offset), (i, j)) in enumerate(OWN[:4]):
        real, imag = parts_of(values, i, j, [level + 2 for level in OUTER_DONE[(i, j)]])
        stage[index, 0], stage[index, 1] = base[index, 0] + real, base[index, 1] + imag
        r, e = own_index(row, offset)
        for a, out in enumerate((out_re, out_im)):
            copies.append(pltpu.make_async_copy(stage.at[index, a], out.at[r, e], sems.at[len(copies)]))
            copies[-1].start()
    for copy in copies:
        copy.wait()


VECTOR = pl.BlockSpec(memory_space=pltpu.VMEM)
SCALAR = pl.BlockSpec(memory_space=pltpu.SMEM)
BIG = pl.BlockSpec(memory_space=pltpu.HBM)


def call(kernel, ins, outs, scratch, flops, aliases=None):
    return pl.pallas_call(
        kernel,
        out_shape=[shape for shape, _ in outs],
        in_specs=ins,
        out_specs=[spec for _, spec in outs],
        scratch_shapes=scratch,
        input_output_aliases=aliases or {},
        compiler_params=pltpu.CompilerParams(vmem_limit_bytes=32 * 2**20),
        cost_estimate=pl.CostEstimate(flops=flops, bytes_accessed=4 * 2**20, transcendentals=0),
    )


def blocks(*lead, dtype=f32):
    return jax.ShapeDtypeStruct((*lead, BS, BS), dtype)


def body(density_real, density_imag, hamiltonian, dipole, field, pattern):
    count = lax.axis_size(RING)
    pair = [(i, i ^ 1) for i in range(count)]
    cross = [(i, (i + 1) % count if i % 2 else (i - 1) % count) for i in range(count)]
    pattern = jnp.transpose(pattern, (2, 1, 0))
    whole = density_real.shape
    arrays = [
        pltpu.with_memory_space_constraint(x, pltpu.HBM) for x in (density_real, density_imag, hamiltonian, dipole)
    ]
    dma = pltpu.SemaphoreType.DMA
    kept_out = (blocks(len(KEPT_X) + len(KEPT_H), 2, dtype=bf16), VECTOR)
    sums_out = (blocks(len(SUMS)), VECTOR)

    (packed,) = call(
        pack_kernel,
        [BIG] * 4 + [SCALAR] * 2,
        [(jax.ShapeDtypeStruct((PAYLOAD_ROWS, BS), f32), VECTOR)],
        [pltpu.VMEM((2, 2, 2, BS, BS), f32), pltpu.VMEM((2, 3, BS, BS), f32), dma((10,))],
        10**6,
    )(*arrays, field, pattern)
    far = lax.ppermute(packed, RING, cross)
    near = lax.ppermute(packed, RING, pair)
    kept, sums, h_kept, base, inner_state = call(
        inner_first,
        [BIG] * 4 + [VECTOR] + [SCALAR] * 2,
        [
            kept_out,
            sums_out,
            (blocks(len(INNER_H), 2, dtype=bf16), VECTOR),
            (blocks(len(OWN), 2), VECTOR),
            (blocks(3), VECTOR),
        ],
        [pltpu.VMEM(whole, f32)] * 4 + [dma((4,))] + band_scratch(),
        2 * 10**9,
    )(*arrays, near, field, pattern)
    state, terms = call(
        outer_first,
        [VECTOR] * 4 + [SCALAR],
        [(jax.ShapeDtypeStruct((4 * BS, BS), f32), VECTOR), (blocks(len(OUTER_TERMS)), VECTOR)],
        band_scratch(),
        2 * 10**9,
    )(far, kept, sums, inner_state, pattern)
    far_state = lax.ppermute(state, RING, cross)
    near_state = lax.ppermute(state, RING, pair)
    out = (jax.ShapeDtypeStruct(whole, f32), BIG)
    kept, sums, base, out_re, out_im = call(
        inner_second,
        [VECTOR] * 7 + [SCALAR],
        [kept_out, sums_out, (blocks(4, 2), VECTOR), out, out],
        [pltpu.VMEM((2, 2, BS, BS), f32), dma((4,))] + band_scratch(),
        2 * 10**9,
    )(near, state, near_state, inner_state, terms, h_kept, base, pattern)
    return tuple(
        call(
            outer_second,
            [VECTOR] * 5 + [BIG] * 2 + [SCALAR],
            [out, out],
            [pltpu.VMEM((4, 2, BS, BS), f32), dma((8,))] + band_scratch(),
            2 * 10**9,
            {5: 0, 6: 1},
        )(far, far_state, kept, sums, base, out_re, out_im, pattern)
    )


def solution(mesh):
    in_specs = (
        P(("row", "col"), None, None, None),
        P(("row", "col"), None, None, None),
        P(("row", "col"), None, None, None),
        P(("parts", "row", "col"), None, None, None),
        P("parts"),
        P(None, ("row", "col"), None),
    )
    out_specs = (
        P(("parts", "row", "col"), None, None, None),
        P(("parts", "row", "col"), None, None, None),
    )
    return jax.shard_map(body, mesh=mesh, in_specs=in_specs, out_specs=out_specs, check_vma=False)
```

time: 109 us -> 32.2 us (0.30)
  the two profiles are of different devices: /device:TPU:1 before, /device:TPU:0 now
where the time goes in v2:
time: 32.2 us; the launch traced here: 32 us
  Pallas kernels  16 us (50%)
  starting transfers between devices  12.9 us (40%)
  waiting for transfers between devices  1.77 us (5%)
  between operations  1.33 us (4%)
    ppermute x1, starting transfers between devices, body(): far = lax.ppermute(packed, RING, cross)  5.67 us
    pallas_call x1, Pallas kernels, body(): call(inner_first, [BIG] * 4 + [VECTOR] + [SCALAR] * 2, [kept_out, sums_ou...  4.79 us
    ppermute x1, starting transfers between devices, body(): far_state = lax.ppermute(state, RING, cross)  4.78 us
    pallas_call x1, Pallas kernels, body(): call(inner_second, [VECTOR] * 7 + [SCALAR], [kept_out, sums_out, (blocks(...  3.83 us
    pallas_call x1, Pallas kernels, body(): call(outer_second, [VECTOR] * 5 + [BIG] * 2 + [SCALAR], [out, out], [pltp...  3.19 us
    pallas_call x1, Pallas kernels, body(): call(outer_first, [VECTOR] * 4 + [SCALAR], [(jax.ShapeDtypeStruct((4 * BS...  2.29 us
    ppermute x1, starting transfers between devices, body(): near_state = lax.ppermute(state, RING, pair)  1.96 us
    pallas_call x1, Pallas kernels, body(): call(pack_kernel, [BIG] * 4 + [SCALAR] * 2, [(jax.ShapeDtypeStruct((PAYLO...  1.88 us
  transfers between devices with their start and end apart: 4, of which 2 were waited for; matrix products, arithmetic and copies ran while one was open for 0% of the time, Pallas kernels for 27%

profile of v2, /device:TPU:0, one launch (start us, length us, event | category | flops | bytes accessed | tf_op | source)
XLA Modules:
  0.0 32.0 jit_solution(12705330142710463726)
XLA Ops:
  0.6 0.0 copy-start
  1.3 0.0 copy-done
  1.3 1.9 %shard_map.77 = f32[904,128]{1,0:T(8,128)S(1)} custom-call(f32[2,3,128,128]{3,2,1,0:T(8,128)} %re.3, f32[2,3,128,128]{3,2,1,0:T(8,128)} %im.3, f32[2,3,128,128]{3,2,1,0:T(8,128)} %ham.3, f32[2,3,128,128]{3,2,1,0:T(8,128)} %dip.3, f32[1]{0:T(128)S(6)} %copy.12.field, s32[3,2,6]{2,1,0:T(2,128)S(1)} %bitcast.1), custom_call_target="tpu_custom_call" | custom-call | flops 1000000 | bytes 4194304 | tf_op jit(solution)/shard_map/pallas_call | solution.py:451
  3.2 0.5 %collective-permute-start.1 = (f32[904,128]{1,0:T(8,128)S(1)}, f32[904,128]{1,0:T(8,128)S(1)}, u32[]{:S(2)}, u32[]{:S(2)}) collective-permute-start(f32[904,128]{1,0:T(8,128)S(1)} %shard_map.77), channel_id=1, source_target_pairs={{0,1},{1,0},{2,3},{3,2},{4,5},{5,4},{6,7},{7,6},{8,9},{9,8},{10,11... | collective-permute-start | bytes 1388552 | tf_op jit(solution)/shard_map/ppermute | solution.py:459
  3.7 5.7 %collective-permute-start = (f32[904,128]{1,0:T(8,128)S(1)}, f32[904,128]{1,0:T(8,128)S(1)}, u32[]{:S(2)}, u32[]{:S(2)}) collective-permute-start(f32[904,128]{1,0:T(8,128)S(1)} %shard_map.77), channel_id=1, source_target_pairs={{0,15},{1,2},{2,1},{3,4},{4,3},{5,6},{6,5},{7,8},{8,7},{9,10},{10,... | collective-permute-start | bytes 1388552 | tf_op jit(solution)/shard_map/ppermute | solution.py:458
  9.4 0.0 collective-permute-done.1.near
  9.4 4.8 %shard_map.78 = (bf16[8,2,128,128]{3,2,1,0:T(8,128)(2,1)S(1)}, f32[7,128,128]{2,1,0:T(8,128)S(1)}, bf16[12,2,128,128]{3,2,1,0:T(8,128)(2,1)S(1)}, f32[6,2,128,128]{3,2,1,0:T(8,128)S(1)}, f32[3,128,128]{2,1,0:T(8,128)S(1)}) custom-call(f32[2,3,128,128]{3,2,1,0:T(8,128)} %re.3, f32[2,3,128,128]{3,2,1,0:T(8,128)} %im.3, f32[2,3,128,128]{3,2,1,0:T(8,128)} %ham.3, ...), custom_call_target="tpu_custom_call" | custom-call | flops 2000000000 | bytes 4194304 | tf_op jit(solution)/shard_map/pallas_call | solution.py:460
  14.2 1.5 %collective-permute-done.far = f32[904,128]{1,0:T(8,128)S(1)} collective-permute-done((f32[904,128]{1,0:T(8,128)S(1)}, f32[904,128]{1,0:T(8,128)S(1)}, u32[]{:S(2)}, u32[]{:S(2)}) %collective-permute-start) | collective-permute-done | bytes 462880 | tf_op jit(solution)/shard_map/ppermute | solution.py:458
  15.7 2.3 %shard_map.79 = (f32[512,128]{1,0:T(8,128)S(1)}, f32[7,128,128]{2,1,0:T(8,128)S(1)}) custom-call(f32[904,128]{1,0:T(8,128)S(1)} %collective-permute-done.far, bf16[8,2,128,128]{3,2,1,0:T(8,128)(2,1)S(1)} %get-tuple-element.14.kept, f32[7,128,128]{2,1,0:T(8,128)S(1)} %get-tuple-element.15.sums, f32[3,128,128]{2,1,0:T(8,128)S(1)} %get-tuple-element.16.inner_state, ...), custom_call_target="tpu_custom_call" | custom-call | flops 2000000000 | bytes 4194304 | tf_op jit(solution)/shard_map/pallas_call | solution.py:473
  18.0 2.0 %collective-permute-start.3 = (f32[512,128]{1,0:T(8,128)S(1)}, f32[512,128]{1,0:T(8,128)S(1)}, u32[]{:S(2)}, u32[]{:S(2)}) collective-permute-start(f32[512,128]{1,0:T(8,128)S(1)} %get-tuple-element.17.state), channel_id=1, source_target_pairs={{0,1},{1,0},{2,3},{3,2},{4,5},{5,4},{6,7},{7,6},{8,9},{9,8},{10,11... | collective-permute-start | bytes 786440 | tf_op jit(solution)/shard_map/ppermute | solution.py:481
  20.0 4.8 %collective-permute-start.2 = (f32[512,128]{1,0:T(8,128)S(1)}, f32[512,128]{1,0:T(8,128)S(1)}, u32[]{:S(2)}, u32[]{:S(2)}) collective-permute-start(f32[512,128]{1,0:T(8,128)S(1)} %get-tuple-element.17.state), channel_id=1, source_target_pairs={{0,15},{1,2},{2,1},{3,4},{4,3},{5,6},{6,5},{7,8},{8,7},{9,10},{10,... | collective-permute-start | bytes 786440 | tf_op jit(solution)/shard_map/ppermute | solution.py:480
  24.7 0.0 collective-permute-done.3.near_state
  24.7 3.8 %shard_map.80 = (bf16[8,2,128,128]{3,2,1,0:T(8,128)(2,1)S(1)}, f32[7,128,128]{2,1,0:T(8,128)S(1)}, f32[4,2,128,128]{3,2,1,0:T(8,128)S(1)}, f32[2,3,128,128]{3,2,1,0:T(8,128)}, f32[2,3,128,128]{3,2,1,0:T(8,128)}) custom-call(f32[904,128]{1,0:T(8,128)S(1)} %collective-permute-done.1.near, f32[512,128]{1,0:T(8,128)S(1)} %get-tuple-element.17.state, ...), custom_call_target="tpu_custom_call" | custom-call | flops 2000000000 | bytes 4194304 | tf_op jit(solution)/shard_map/pallas_call | solution.py:483
  28.6 0.2 collective-permute-done.2.far_state
  28.8 3.2 %shard_map.81 = (f32[2,3,128,128]{3,2,1,0:T(8,128)}, f32[2,3,128,128]{3,2,1,0:T(8,128)}) custom-call(f32[904,128]{1,0:T(8,128)S(1)} %collective-permute-done.far, f32[512,128]{1,0:T(8,128)S(1)} %collective-permute-done.2.far_state, bf16[8,2,128,128]{3,2,1,0:T(8,128)(2,1)S(1)} %get-tuple-element.21.kept, ...), custom_call_target="tpu_custom_call", output_to_operand_aliasing={{0}: (5, {}), {1}: (6, {})} | custom-call | flops 2000000000 | bytes 4194304 | tf_op jit(solution)/shard_map/pallas_call | solution.py:491
Async XLA Ops:
  0.6 0.7 %copy-start = (s32[6,2,3]{0,1,2:T(2,128)S(1)}, s32[6,2,3]{0,1,2:T(2,128)}, u32[]{:S(2)}) copy-start(s32[6,2,3]{0,1,2:T(2,128)} %param.11) | copy-start | bytes 436
  3.2 6.2 %collective-permute-start.1 = (f32[904,128]{1,0:T(8,128)S(1)}, f32[904,128]{1,0:T(8,128)S(1)}, u32[]{:S(2)}, u32[]{:S(2)}) collective-permute-start(f32[904,128]{1,0:T(8,128)S(1)} %shard_map.77), channel_id=1, source_target_pairs={{0,1},{1,0},{2,3},{3,2},{4,5},{5,4},{6,7},{7,6},{8,9},{9,8},{10,11... | collective-permute-start | bytes 1388552 | tf_op jit(solution)/shard_map/ppermute | solution.py:459
  3.7 12.0 %collective-permute-start = (f32[904,128]{1,0:T(8,128)S(1)}, f32[904,128]{1,0:T(8,128)S(1)}, u32[]{:S(2)}, u32[]{:S(2)}) collective-permute-start(f32[904,128]{1,0:T(8,128)S(1)} %shard_map.77), channel_id=1, source_target_pairs={{0,15},{1,2},{2,1},{3,4},{4,3},{5,6},{6,5},{7,8},{8,7},{9,10},{10,... | collective-permute-start | bytes 1388552 | tf_op jit(solution)/shard_map/ppermute | solution.py:458
  18.0 6.7 %collective-permute-start.3 = (f32[512,128]{1,0:T(8,128)S(1)}, f32[512,128]{1,0:T(8,128)S(1)}, u32[]{:S(2)}, u32[]{:S(2)}) collective-permute-start(f32[512,128]{1,0:T(8,128)S(1)} %get-tuple-element.17.state), channel_id=1, source_target_pairs={{0,1},{1,0},{2,3},{3,2},{4,5},{5,4},{6,7},{7,6},{8,9},{9,8},{10,11... | collective-permute-start | bytes 786440 | tf_op jit(solution)/shard_map/ppermute | solution.py:481
  20.0 8.9 %collective-permute-start.2 = (f32[512,128]{1,0:T(8,128)S(1)}, f32[512,128]{1,0:T(8,128)S(1)}, u32[]{:S(2)}, u32[]{:S(2)}) collective-permute-start(f32[512,128]{1,0:T(8,128)S(1)} %get-tuple-element.17.state), channel_id=1, source_target_pairs={{0,15},{1,2},{2,1},{3,4},{4,3},{5,6},{6,5},{7,8},{8,7},{9,10},{10,... | collective-permute-start | bytes 786440 | tf_op jit(solution)/shard_map/ppermute | solution.py:480

commit v3 on v0

v3 whole, which is shorter than its diff:
```python
import functools

import jax
import jax.numpy as jnp
from jax import lax
from jax.experimental import pallas as pl
from jax.experimental.pallas import tpu as pltpu
from jax.sharding import PartitionSpec as P

TERMS = 6
BS = 128
time_step = 0.5
RING = ("row", "col")
f32, bf16 = jnp.float32, jnp.bfloat16

ROWS = 6
SIGN_RE = (1.0, -1.0, -1.0, 1.0, 1.0, -1.0)
SIGN_IM = (-1.0, -1.0, 1.0, 1.0, -1.0, -1.0)
FIRST_ROWS = 6 * BS + 8
SECOND_ROWS = 4 * BS
MORE = 8
TABLE_ROWS = 32
TABLE_FIELD = 24


def own_index(row, offset):
    core = lax.axis_index("col")
    return jnp.where(core == 0, row, 1 - row), jnp.where(core == 0, 1 + offset, 1 - offset)


def own(ref, row, offset):
    r, e = own_index(row, offset)
    return ref[r, e]


def slot(ref, index):
    return ref[index * BS : (index + 1) * BS, :]


def line(ref, index):
    return ref[index : index + 1, :]


class Band:
    def __init__(self, ref, negated=False):
        self.high, self.low = ref.at[0], ref.at[1]
        self.minus = Band(ref.at[pl.ds(2, 2)]) if negated else None

    def put(self, i, j, value):
        part = slice((j - i + 1) * BS, (j - i + 2) * BS)
        high = value.astype(bf16)
        low = (value - high.astype(f32)).astype(bf16)
        self.high[i, :, part] = high
        self.low[i, :, part] = low
        if self.minus is not None:
            self.minus.high[i, :, part] = -high
            self.minus.low[i, :, part] = -low

    def left(self, i, first, last):
        part = slice((first - i + 1) * BS, (last - i + 2) * BS)
        high, low = self.high[i, :, part], self.low[i, :, part]
        return [high, high, low]

    def right(self, first, last, j, j_last):
        highs, lows = [], []
        for k in range(first, last + 1):
            part = slice((j - k + 1) * BS, (j_last - k + 2) * BS)
            highs.append(self.high[k, :, part])
            lows.append(self.low[k, :, part])
        return highs + lows + highs


def piece(h, x, rows, mids, cols):
    right = jnp.concatenate(x.right(*mids, *cols) + h.minus.right(*mids, *cols), axis=0)
    return [
        jnp.dot(
            jnp.concatenate(h.left(i, *mids) + x.left(i, *mids), axis=1), right, preferred_element_type=f32
        )
        for i in rows
    ]


def one_side(a, b, row, mids, col):
    left = jnp.concatenate(a.left(row, *mids), axis=1)
    right = jnp.concatenate(b.right(*mids, col, col), axis=0)
    return jnp.dot(left, right, preferred_element_type=f32)


def tile(h, x, i):
    upper, lower = piece(h, x, (i, i + 1), (i, i + 1), (i, i + 1))
    return upper[:, :BS], upper[:, BS:], lower[:, :BS], lower[:, BS:]


def part(h, x, i, k, j):
    return piece(h, x, (i,), (k, k), (j, j))[0]


def coefficient(term):
    return time_step / (term + 1)


SUMS = ((1, 1, 1), (1, 1, 2), (1, 2, 1), (2, 2, 2), (3, 2, 2), (3, 2, 3), (3, 3, 2))
OUTER_TERMS = ((1, 2, 1), (1, 1, 2), (2, 2, 1), (2, 1, 2), (3, 2, 1), (3, 1, 2), (2, 2, 2))
STATE = ((2, 2), (2, 3), (3, 2), (3, 3))
INNER_STATE = ((3, 3), (3, 4), (4, 3))
OWN = (((0, -1), (2, 1)), ((0, 0), (2, 2)), ((0, 1), (2, 3)), ((1, -1), (3, 2)), ((1, 0), (3, 3)), ((1, 1), (3, 4)))
DONE_A = {(2, 2): (1,), (2, 3): (1,), (3, 2): (1,)}
DONE_B = {(2, 3): (2,), (3, 2): (2,), (3, 3): (1, 2, 3), (3, 4): (1, 2, 3)}
DONE_OUTER = {(2, 1): (1, 2, 3), (2, 2): (2, 3), (2, 3): (3,), (3, 2): (3,)}
NEAR_X = (((4, 4), 3), ((5, 5), 0), ((4, 5), 2), ((5, 4), 1))
FAR_X = (((1, 1), 0), ((0, 0), 3), ((1, 0), 1), ((0, 1), 2))


def weighted(terms_of, signs):
    total = None
    for sign, value in zip(signs, terms_of):
        total = (value if sign > 0 else -value) if total is None else (total + value if sign > 0 else total - value)
    return total


def parts_of(values, i, j, terms):
    re_signs, im_signs = [SIGN_RE[term] for term in terms], [SIGN_IM[term] for term in terms]
    here = [values[(term, i, j)] for term in terms]
    there = here if i == j else [values[(term, j, i)] for term in terms]
    real = 0.5 * (weighted(here, re_signs) + weighted(there, re_signs).T)
    imag = 0.5 * (weighted(here, im_signs) - weighted(there, im_signs).T)
    return real, imag


def add_terms(base, values, done, phase):
    for index, (_, (i, j)) in enumerate(OWN):
        terms = [level - 1 + 3 * phase for level in done.get((i, j), ())]
        if terms:
            real, imag = parts_of(values, i, j, terms)
            base[index, 0] = base[index, 0] + real
            base[index, 1] = base[index, 1] + imag


def triangle(test):
    rows = lax.broadcasted_iota(jnp.int32, (BS, BS), 0)
    cols = lax.broadcasted_iota(jnp.int32, (BS, BS), 1)
    return test(rows, cols)


def unpack_h(payload):
    both = slot(payload, 4)
    turned = both.T
    first = jnp.where(triangle(lambda r, c: r <= c), both, turned)
    second = jnp.where(triangle(lambda r, c: r > c), both, turned)
    second = jnp.where(triangle(lambda r, c: r == c), line(payload, 6 * BS + 6), second)
    return first, second, slot(payload, 5)


def pack_kernel(re, im, ham, dip, pattern_in, field, far, near, table, dens, oper, pattern, sems):
    copies = [pltpu.make_async_copy(pattern_in, pattern, sems.at[0])]
    for a, ref in enumerate((re, im)):
        for r in range(2):
            copies.append(pltpu.make_async_copy(ref.at[r, pl.ds(1 - r, 2)], dens.at[a, r], sems.at[len(copies)]))
    for a, ref in enumerate((ham, dip)):
        for n, (row, offset) in enumerate(((0, 0), (0, 1), (1, 0))):
            r, e = own_index(row, offset)
            copies.append(pltpu.make_async_copy(ref.at[r, e], oper.at[a, n], sems.at[len(copies)]))
    for copy in copies:
        copy.start()
    for copy in copies[:5]:
        copy.wait()

    def put(first, value):
        far[first : first + value.shape[0], :] = value
        near[first : first + value.shape[0], :] = value

    for index, (row, offset) in enumerate(((0, 0), (0, 1), (1, -1), (1, 0))):
        r, e = own_index(row, offset)
        put(index * BS, dens[0, r, e - 1 + r] + dens[1, r, e - 1 + r])
    f = field[0]
    for n, (row, offset) in enumerate(((0, -1), (0, 1), (1, 1))):
        r, e = own_index(row, offset)
        for term in range(TERMS):
            value = jnp.full((1, BS), pattern[e, r, term].astype(f32) * coefficient(term), f32)
            table[8 * n + term : 8 * n + term + 1, :] = value
            if n == 1:
                put(6 * BS + term, value)
    table[TABLE_FIELD : TABLE_FIELD + 1, :] = jnp.full((1, BS), f, f32)
    for copy in copies[5:]:
        copy.wait()
    first, between, second = [oper[0, n] + f * oper[1, n] for n in range(3)]
    put(4 * BS, jnp.where(triangle(lambda r, c: r <= c), first, second))
    put(5 * BS, between)
    diagonal = jnp.where(triangle(lambda r, c: r == c), second, 0.0)
    put(6 * BS + 6, jnp.sum(diagonal, axis=0, keepdims=True))


def views(h_ref, x_ref):
    return Band(h_ref, True), [Band(x_ref.at[level]) for level in range(3)]


def inner_a(h, xs, phase, table, base, sums, carry, values):
    term = 3 * phase
    t2 = tile(h, xs[0], 2)
    scale = line(table, 8 + term)
    first = {
        (2, 3): t2[1] * scale,
        (3, 2): t2[2] * scale,
        (2, 2): (part(h, xs[0], 2, 1, 2) + t2[0]) * coefficient(term),
    }
    carry[...] = t2[3]
    for (i, j), value in first.items():
        xs[1].put(i, j, value)
        values[(term, i, j)] = value
    sums[0] = part(h, xs[0], 1, 2, 1)
    sums[1] = part(h, xs[0], 1, 2, 2)
    sums[2] = part(h, xs[0], 2, 2, 1)
    add_terms(base, values, DONE_A, phase)


def inner_a_first(re, im, ham, dip, table, h_ref, x_ref, base, sums, carry, re_in, im_in, ham_in, dip_in, sems):
    copies = [
        pltpu.make_async_copy(source, target, sems.at[n])
        for n, (source, target) in enumerate(((ham, ham_in), (dip, dip_in), (re, re_in), (im, im_in)))
    ]
    for copy in copies:
        copy.start()
    h, xs = views(h_ref, x_ref)
    for copy in copies:
        copy.wait()
    f = line(table, TABLE_FIELD)
    for index, ((row, offset), (i, j)) in enumerate(OWN):
        value = own(ham_in, row, offset) + f * own(dip_in, row, offset)
        h.put(i, j, value)
        real, imag = own(re_in, row, offset), own(im_in, row, offset)
        xs[0].put(i, j, real + imag)
        if j in (1, 4):
            h.put(j, i, value.T)
            xs[0].put(j, i, (real - imag).T)
        base[index, 0], base[index, 1] = real, imag
    inner_a(h, xs, 0, table, base, sums, carry, {})


def inner_b(h, xs, phase, near_scale, table, base, sums, carry, values):
    term = 3 * phase
    c = [coefficient(term + n) for n in range(3)]
    own_edge = [line(table, 8 + term + n) for n in range(3)]
    near_edge = [line(table, 16 + term + n) for n in range(3)]

    def put(level, i, j, value):
        values[(term + level - 1, i, j)] = value
        if level < 3:
            xs[level].put(i, j, value)

    x0, x1, x2 = xs
    t3, t4 = tile(h, x0, 3), tile(h, x0, 4)
    put(1, 3, 4, t3[1] * near_edge[0])
    put(1, 4, 3, t3[2] * near_edge[0])
    put(1, 3, 3, (carry[...] + t3[0] - part(h, x0, 3, 3, 3)) * c[0])
    put(1, 4, 4, (t3[3] + t4[0] - part(h, x0, 4, 4, 4)) * c[0])
    put(1, 4, 5, t4[1] * near_scale)
    put(1, 5, 4, t4[2] * near_scale)
    t2, t3 = tile(h, x1, 2), tile(h, x1, 3)
    put(2, 2, 3, t2[1] * own_edge[1])
    put(2, 3, 2, t2[2] * own_edge[1])
    put(2, 3, 3, (t2[3] + t3[0] - part(h, x1, 3, 3, 3)) * c[1])
    put(2, 3, 4, t3[1] * near_edge[1])
    put(2, 4, 3, t3[2] * near_edge[1])
    put(2, 4, 4, (t3[3] + part(h, x1, 4, 5, 4)) * c[1])
    sums[3] = part(h, x1, 2, 3, 2)
    t3 = tile(h, x2, 3)
    put(3, 3, 4, t3[1] * near_edge[2])
    put(3, 4, 3, t3[2] * near_edge[2])
    put(3, 3, 3, (t3[0] + part(h, x2, 3, 2, 3)) * c[2])
    sums[4] = part(h, x2, 2, 3, 2)
    sums[5] = one_side(h, x2, 2, (2, 3), 3) + one_side(x2, h.minus, 2, (3, 3), 3)
    sums[6] = one_side(h, x2, 3, (3, 3), 2) + one_side(x2, h.minus, 3, (2, 3), 2)
    add_terms(base, values, DONE_B, phase)


def inner_b_first(near, table, carry, h_in, x_in, base_in, sums_in, h_ref, x_ref, base, sums, state):
    h, xs = views(h_ref, x_ref)
    inside, outside, between = second_first(near)
    h.put(4, 4, inside)
    h.put(5, 5, outside)
    h.put(5, 4, between)
    h.put(4, 5, between.T)
    for (i, j), index in NEAR_X:
        xs[0].put(i, j, slot(near, index))
    values = {}
    inner_b(h, xs, 0, line(near, 6 * BS), table, base, sums, carry, values)
    for index, (i, j) in enumerate(INNER_STATE):
        state[index] = values[(2, i, j)]


def second_first(payload):
    first, second, between = unpack_h(payload)
    return second, first, between


def outer(h, xs, phase, far_scale, table, sums, record):
    term = 3 * phase
    c = [coefficient(term + n) for n in range(3)]
    cross = [line(table, term + n) for n in range(3)]

    def put(level, i, j, value):
        record(level, i, j, value)
        if level < 3:
            xs[level].put(i, j, value)

    def known(level, i, j):
        return sums[SUMS.index((level, i, j))]

    x0, x1, x2 = xs
    t0 = tile(h, x0, 0)
    put(1, 1, 1, (t0[3] + known(1, 1, 1)) * c[0])
    put(1, 1, 2, (part(h, x0, 1, 1, 2) + known(1, 1, 2)) * cross[0])
    put(1, 2, 1, (part(h, x0, 2, 1, 1) + known(1, 2, 1)) * cross[0])
    put(1, 0, 1, t0[1] * far_scale)
    put(1, 1, 0, t0[2] * far_scale)
    t1 = tile(h, x1, 1)
    put(2, 1, 1, (part(h, x1, 1, 0, 1) + t1[0]) * c[1])
    put(2, 1, 2, t1[1] * cross[1])
    put(2, 2, 1, t1[2] * cross[1])
    put(2, 2, 2, (t1[3] + known(2, 2, 2)) * c[1])
    t1 = tile(h, x2, 1)
    scale = line(table, 8 + term + 2)
    put(3, 2, 3, (one_side(x2, h.minus, 2, (2, 2), 3) + known(3, 2, 3)) * scale)
    put(3, 3, 2, (one_side(h, x2, 3, (2, 2), 2) + known(3, 3, 2)) * scale)
    put(3, 1, 2, t1[1] * cross[2])
    put(3, 2, 1, t1[2] * cross[2])
    put(3, 2, 2, (t1[3] + known(3, 2, 2)) * c[2])


def outer_first(far, table, sums, inner_state, h_in, x_in, h_ref, x_ref, state, state_near, terms):
    h, xs = views(h_ref, x_ref)
    inside, outside, between = unpack_h(far)
    h.put(1, 1, inside)
    h.put(0, 0, outside)
    h.put(1, 0, between)
    h.put(0, 1, between.T)
    for (i, j), index in FAR_X:
        xs[0].put(i, j, slot(far, index))

    def put(index, value):
        state[index * BS : (index + 1) * BS, :] = value
        state_near[index * BS : (index + 1) * BS, :] = value

    def record(level, i, j, value):
        if (level, i, j) in OUTER_TERMS:
            terms[OUTER_TERMS.index((level, i, j))] = value
        if level == 3 and (i, j) in STATE:
            put(STATE.index((i, j)), value)

    put(3, inner_state[0])
    outer(h, xs, 0, line(far, 6 * BS), table, sums, record)


def inner_a_second(state, inner_state, terms, table, h_ref, x_in, base_in, x_ref, base, sums, carry):
    h, xs = views(h_ref, x_ref)
    values = {(level - 1, i, j): terms[index] for index, (level, i, j) in enumerate(OUTER_TERMS)}
    for index, (i, j) in enumerate(STATE):
        values[(2, i, j)] = slot(state, index)
    for index, (i, j) in enumerate(INNER_STATE):
        values[(2, i, j)] = inner_state[index]
    for i, j in STATE + INNER_STATE[1:] + ((1, 2), (2, 1)):
        xs[0].put(i, j, values[(2, i, j)])
    add_terms(base, values, DONE_OUTER, 0)
    inner_a(h, xs, 1, table, base, sums, carry, {})


def inner_b_second(
    near_state, near, table, carry, h_ref, x_in, base_in, sums_in, x_ref, base, sums, out_re, out_im, sems
):
    h, xs = views(h_ref, x_ref)
    for (i, j), index in NEAR_X:
        xs[0].put(i, j, slot(near_state, index))
    inner_b(h, xs, 1, line(near, 6 * BS + 3), table, base, sums, carry, {})
    copies = []
    for index, ((row, offset), _) in tuple(enumerate(OWN))[4:]:
        r, e = own_index(row, offset)
        for a, out in enumerate((out_re, out_im)):
            copies.append(pltpu.make_async_copy(base.at[index, a], out.at[r, e], sems.at[len(copies)]))
    for copy in copies:
        copy.start()
    for copy in copies:
        copy.wait()


def outer_second(
    far_state, far, table, sums, base, h_ref, x_in, in_re, in_im, x_ref, out_re, out_im, stage, sems
):
    h, xs = views(h_ref, x_ref)
    for (i, j), index in FAR_X:
        xs[0].put(i, j, slot(far_state, index))
    values = {}

    def record(level, i, j, value):
        values[(level + 2, i, j)] = value

    outer(h, xs, 1, line(far, 6 * BS + 3), table, sums, record)
    copies = []
    for index in (2, 3, 0, 1):
        (row, offset), (i, j) = OWN[index]
        real, imag = parts_of(values, i, j, [level + 2 for level in DONE_OUTER[(i, j)]])
        stage[index, 0], stage[index, 1] = base[index, 0] + real, base[index, 1] + imag
        r, e = own_index(row, offset)
        for a, out in enumerate((out_re, out_im)):
            copies.append(pltpu.make_async_copy(stage.at[index, a], out.at[r, e], sems.at[len(copies)]))
            copies[-1].start()
    for copy in copies:
        copy.wait()


VECTOR = pl.BlockSpec(memory_space=pltpu.VMEM)
SCALAR = pl.BlockSpec(memory_space=pltpu.SMEM)
BIG = pl.BlockSpec(memory_space=pltpu.HBM)


def call(kernel, ins, outs, scratch=(), aliases=None):
    return pl.pallas_call(
        kernel,
        out_shape=[shape for shape, _ in outs],
        in_specs=ins,
        out_specs=[spec for _, spec in outs],
        scratch_shapes=list(scratch),
        input_output_aliases=aliases or {},
        compiler_params=pltpu.CompilerParams(vmem_limit_bytes=24 * 2**20),
        cost_estimate=pl.CostEstimate(flops=0, bytes_accessed=0, transcendentals=0),
    )


def vector(*shape, dtype=f32):
    return jax.ShapeDtypeStruct(shape, dtype), VECTOR


def body(density_real, density_imag, hamiltonian, dipole, field, pattern):
    count = lax.axis_size(RING)
    pair = [(i, i ^ 1) for i in range(count)]
    cross = [(i, (i + 1) % count if i % 2 else (i - 1) % count) for i in range(count)]
    pattern = jnp.transpose(pattern, (2, 1, 0))
    whole = density_real.shape
    inputs = [
        pltpu.with_memory_space_constraint(x, pltpu.HBM)
        for x in (density_real, density_imag, hamiltonian, dipole, pattern)
    ]
    dma = pltpu.SemaphoreType.DMA
    h_out, x_out = vector(4, ROWS, BS, 3 * BS, dtype=bf16), vector(3, 2, ROWS, BS, 3 * BS, dtype=bf16)
    base_out, sums_out, carry_out = vector(len(OWN), 2, BS, BS), vector(len(SUMS), BS, BS), vector(BS, BS)
    table_out = vector(TABLE_ROWS, BS)
    out = (jax.ShapeDtypeStruct(whole, f32), BIG)

    far_pack, near_pack, table = call(
        pack_kernel,
        [BIG] * 5 + [SCALAR],
        [vector(FIRST_ROWS + MORE, BS), vector(FIRST_ROWS, BS), table_out],
        [
            pltpu.VMEM((2, 2, 2, BS, BS), f32),
            pltpu.VMEM((2, 3, BS, BS), f32),
            pltpu.SMEM(pattern.shape, jnp.int32),
            dma((11,)),
        ],
    )(*inputs, field)
    far = lax.ppermute(far_pack, RING, cross)
    near = lax.ppermute(near_pack, RING, pair)
    h, x, base, sums, carry = call(
        inner_a_first,
        [BIG] * 4 + [VECTOR],
        [h_out, x_out, base_out, sums_out, carry_out],
        [pltpu.VMEM(whole, f32)] * 4 + [dma((4,))],
    )(*inputs[:4], table)
    h, x, base, sums, inner_state = call(
        inner_b_first,
        [VECTOR] * 7,
        [h_out, x_out, base_out, sums_out, vector(len(INNER_STATE), BS, BS)],
        aliases={3: 0, 4: 1, 5: 2, 6: 3},
    )(near, table, carry, h, x, base, sums)
    h, x, state, state_near, terms = call(
        outer_first,
        [VECTOR] * 6,
        [
            h_out,
            x_out,
            vector(SECOND_ROWS + MORE, BS),
            vector(SECOND_ROWS, BS),
            vector(len(OUTER_TERMS), BS, BS),
        ],
        aliases={4: 0, 5: 1},
    )(far, table, sums, inner_state, h, x)
    far_state = lax.ppermute(state, RING, cross)
    near_state = lax.ppermute(state_near, RING, pair)
    x, base, sums, carry = call(
        inner_a_second,
        [VECTOR] * 7,
        [x_out, base_out, sums_out, carry_out],
        aliases={5: 0, 6: 1},
    )(state, inner_state, terms, table, h, x, base)
    x, base, sums, out_re, out_im = call(
        inner_b_second,
        [VECTOR] * 8,
        [x_out, base_out, sums_out, out, out],
        [dma((4,))],
        aliases={5: 0, 6: 1, 7: 2},
    )(near_state, near, table, carry, h, x, base, sums)
    _, out_re, out_im = call(
        outer_second,
        [VECTOR] * 7 + [BIG] * 2,
        [x_out, out, out],
        [pltpu.VMEM((4, 2, BS, BS), f32), dma((8,))],
        aliases={6: 0, 7: 1, 8: 2},
    )(far_state, far, table, sums, base, h, x, out_re, out_im)
    return out_re, out_im


def solution(mesh):
    in_specs = (
        P(("row", "col"), None, None, None),
        P(("row", "col"), None, None, None),
        P(("row", "col"), None, None, None),
        P(("parts", "row", "col"), None, None, None),
        P("parts"),
        P(None, ("row", "col"), None),
    )
    out_specs = (
        P(("parts", "row", "col"), None, None, None),
        P(("parts", "row", "col"), None, None, None),
    )
    return jax.shard_map(body, mesh=mesh, in_specs=in_specs, out_specs=out_specs, check_vma=False)
```

time: 109 us -> 27.9 us (0.26)
  waiting for transfers between devices: 47.8 us -> 4.97 us
  matrix products: 31.4 us -> 0 us
  Pallas kernels: 0 us -> 12.7 us
  starting transfers between devices: 15.4 us -> 8.75 us
  local copies, waits for them, and re-layouts: 5.87 us -> 0 us
  other arithmetic: 5.84 us -> 0 us
    ppermute x14 -> x4, waiting for transfers between devices: 47.8 us -> 4.97 us  [the longest x1 2.76 us: body(): far = lax.ppermute(far_pack, RING, cross)]
    dot_general x84 -> x0, matrix products: 31.4 us -> none  [the longest x42 16.1 us: apply_left(): jnp.einsum('rab,mrbc->mrac', operator_rows[:, offset_mid + half_band], pa...]
    pallas_call x0 -> x7, Pallas kernels: none -> 12.7 us  [the longest x1 2.68 us: body(): call(inner_b_second, [VECTOR] * 8, [x_out, base_out, sums_out, out, out],...]
    ppermute x14 -> x4, starting transfers between devices: 15.4 us -> 8.75 us  [the longest x1 2.87 us: body(): near = lax.ppermute(near_pack, RING, pair)]
    unnamed x22 -> x0, local copies, waits for them, and re-layouts: 5.18 us -> none
    another operation x7 -> x0, other arithmetic: 2.15 us -> none  [the longest x1 0.96 us: body(): jnp.stack([hamiltonian, dipole])]
    mul x12 -> x0, other arithmetic: 1.39 us -> none  [body(): weighted = coefficient * keep_mask * commutator]
    concatenate x1 -> x0, other arithmetic: 1.22 us -> none  [padded(): jnp.concatenate([lax.ppermute(tail, axis, [(i, (i + 1) % count) for i in...]
  transfers between devices with their start and end apart: 14 -> 4, of which waited for: 8 -> 3; matrix products, arithmetic and copies ran while one was open for 16% -> 0% of each run, Pallas kernels for 0% -> 27%
where the time goes in v3:
time: 27.9 us; the launch traced here: 27.7 us
  Pallas kernels  12.7 us (46%)
  starting transfers between devices  8.75 us (31%)
  waiting for transfers between devices  4.97 us (18%)
  between operations  1.32 us (5%)
    ppermute x1, starting transfers between devices, body(): near = lax.ppermute(near_pack, RING, pair)  2.87 us
    ppermute x1, waiting for transfers between devices, body(): far = lax.ppermute(far_pack, RING, cross)  2.76 us
    ppermute x1, starting transfers between devices, body(): far = lax.ppermute(far_pack, RING, cross)  2.69 us
    pallas_call x1, Pallas kernels, body(): call(inner_b_second, [VECTOR] * 8, [x_out, base_out, sums_out, out, out],...  2.68 us
    pallas_call x1, Pallas kernels, body(): call(outer_second, [VECTOR] * 7 + [BIG] * 2, [x_out, out, out], [pltpu.VM...  2.32 us
    pallas_call x1, Pallas kernels, body(): call(inner_a_first, [BIG] * 4 + [VECTOR], [h_out, x_out, base_out, sums_o...  2.11 us
    pallas_call x1, Pallas kernels, body(): call(inner_b_first, [VECTOR] * 7, [h_out, x_out, base_out, sums_out, vect...  2.08 us
    ppermute x1, starting transfers between devices, body(): far_state = lax.ppermute(state, RING, cross)  1.81 us
  transfers between devices with their start and end apart: 4, of which 3 were waited for; matrix products, arithmetic and copies ran while one was open for 0% of the time, Pallas kernels for 27%

profile of v3, /device:TPU:1, one launch (start us, length us, event | category | flops | bytes accessed | tf_op | source)
XLA Modules:
  0.0 27.7 jit_solution(1814168579527360954)
XLA Ops:
  1.3 1.3 %shard_map.77 = (f32[784,128]{1,0:T(8,128)S(1)}, f32[776,128]{1,0:T(8,128)S(1)}, f32[32,128]{1,0:T(8,128)S(1)}) custom-call(f32[2,3,128,128]{3,2,1,0:T(8,128)} %re.3, f32[2,3,128,128]{3,2,1,0:T(8,128)} %im.3, f32[2,3,128,128]{3,2,1,0:T(8,128)} %ham.3, f32[2,3,128,128]{3,2,1,0:T(8,128)} %dip.3, s32[3,2,6]{2,1,0:T(2,128)} %bitcast.1, f32[1]{0:T(128)S(6)} %copy.36.field), custom_call_target="tpu_custom_call" | custom-call | tf_op jit(solution)/shard_map/pallas_call | solution.py:448
  2.6 2.7 %collective-permute-start = (f32[784,128]{1,0:T(8,128)S(1)}, f32[784,128]{1,0:T(8,128)S(1)}, u32[]{:S(2)}, u32[]{:S(2)}) collective-permute-start(f32[784,128]{1,0:T(8,128)S(1)} %get-tuple-element.31), channel_id=1, source_target_pairs={{0,15},{1,2},{2,1},{3,4},{4,3},{5,6},{6,5},{7,8},{8,7},{9,10},{10,... | collective-permute-start | bytes 1204232 | tf_op jit(solution)/shard_map/ppermute | solution.py:459
  5.3 2.9 %collective-permute-start.1 = (f32[776,128]{1,0:T(8,128)S(1)}, f32[776,128]{1,0:T(8,128)S(1)}, u32[]{:S(2)}, u32[]{:S(2)}) collective-permute-start(f32[776,128]{1,0:T(8,128)S(1)} %get-tuple-element.33), channel_id=1, source_target_pairs={{0,1},{1,0},{2,3},{3,2},{4,5},{5,4},{6,7},{7,6},{8,9},{9,8},{10,11... | collective-permute-start | bytes 1191944 | tf_op jit(solution)/shard_map/ppermute | solution.py:460
  8.2 2.1 %shard_map.78 = (bf16[4,6,128,384]{3,2,1,0:T(8,128)(2,1)S(1)}, bf16[3,2,6,128,384]{4,3,2,1,0:T(8,128)(2,1)S(1)}, f32[6,2,128,128]{3,2,1,0:T(8,128)S(1)}, f32[7,128,128]{2,1,0:T(8,128)S(1)}, f32[128,128]{1,0:T(8,128)S(1)}) custom-call(f32[2,3,128,128]{3,2,1,0:T(8,128)} %re.3, f32[2,3,128,128]{3,2,1,0:T(8,128)} %im.3, f32[2,3,128,128]{3,2,1,0:T(8,128)} %ham.3, ...), custom_call_target="tpu_custom_call" | custom-call | tf_op jit(solution)/shard_map/pallas_call | solution.py:461
  10.3 0.0 collective-permute-done.1.near
  10.3 2.1 %shard_map.79 = (bf16[4,6,128,384]{3,2,1,0:T(8,128)(2,1)S(1)}, bf16[3,2,6,128,384]{4,3,2,1,0:T(8,128)(2,1)S(1)}, f32[6,2,128,128]{3,2,1,0:T(8,128)S(1)}, f32[7,128,128]{2,1,0:T(8,128)S(1)}, f32[3,128,128]{2,1,0:T(8,128)S(1)}) custom-call(f32[776,128]{1,0:T(8,128)S(1)} %collective-permute-done., ...), custom_call_target="tpu_custom_call", output_to_operand_aliasing={{0}: (3, {}), {1}: (4, {}), {2}: (5, {}), {3}: (6, {})} | custom-call | tf_op jit(solution)/shard_map/pallas_call | solution.py:467
  12.4 2.8 %collective-permute-done.far = f32[784,128]{1,0:T(8,128)S(1)} collective-permute-done((f32[784,128]{1,0:T(8,128)S(1)}, f32[784,128]{1,0:T(8,128)S(1)}, u32[]{:S(2)}, u32[]{:S(2)}) %collective-permute-start) | collective-permute-done | bytes 401440 | tf_op jit(solution)/shard_map/ppermute | solution.py:459
  15.2 1.5 %shard_map.80 = (bf16[4,6,128,384]{3,2,1,0:T(8,128)(2,1)S(1)}, bf16[3,2,6,128,384]{4,3,2,1,0:T(8,128)(2,1)S(1)}, f32[520,128]{1,0:T(8,128)S(1)}, f32[512,128]{1,0:T(8,128)S(1)}, f32[7,128,128]{2,1,0:T(8,128)S(1)}) custom-call(f32[784,128]{1,0:T(8,128)S(1)} %collective-permute-done.far, ...), custom_call_target="tpu_custom_call", output_to_operand_aliasing={{0}: (4, {}), {1}: (5, {})} | custom-call | tf_op jit(solution)/shard_map/pallas_call | solution.py:473
  16.6 1.8 %collective-permute-start.2 = (f32[520,128]{1,0:T(8,128)S(1)}, f32[520,128]{1,0:T(8,128)S(1)}, u32[]{:S(2)}, u32[]{:S(2)}) collective-permute-start(f32[520,128]{1,0:T(8,128)S(1)} %get-tuple-element.43.state), channel_id=1, source_target_pairs={{0,15},{1,2},{2,1},{3,4},{4,3},{5,6},{6,5},{7,8},{8,7},{9,10},{10,... | collective-permute-start | bytes 798728 | tf_op jit(solution)/shard_map/ppermute | solution.py:485
  18.4 1.4 %collective-permute-start.3 = (f32[512,128]{1,0:T(8,128)S(1)}, f32[512,128]{1,0:T(8,128)S(1)}, u32[]{:S(2)}, u32[]{:S(2)}) collective-permute-start(f32[512,128]{1,0:T(8,128)S(1)} %get-tuple-element.44), channel_id=1, source_target_pairs={{0,1},{1,0},{2,3},{3,2},{4,5},{5,4},{6,7},{7,6},{8,9},{9,8},{10,11... | collective-permute-start | bytes 786440 | tf_op jit(solution)/shard_map/ppermute | solution.py:486
  19.8 0.7 %shard_map.81 = (bf16[3,2,6,128,384]{4,3,2,1,0:T(8,128)(2,1)S(1)}, f32[6,2,128,128]{3,2,1,0:T(8,128)S(1)}, f32[7,128,128]{2,1,0:T(8,128)S(1)}, f32[128,128]{1,0:T(8,128)S(1)}) custom-call(f32[520,128]{1,0:T(8,128)S(1)} %get-tuple-element.43.state, f32[3,128,128]{2,1,0:T(8,128)S(1)} %get-tuple-element.40.inner_state, ...), custom_call_target="tpu_custom_call", output_to_operand_aliasing={{0}: (5, {}), {1}: (6, {})} | custom-call | tf_op jit(solution)/shard_map/pallas_call | solution.py:487
  20.5 0.5 %collective-permute-done.3.near_state = f32[512,128]{1,0:T(8,128)S(1)} collective-permute-done((f32[512,128]{1,0:T(8,128)S(1)}, f32[512,128]{1,0:T(8,128)S(1)}, u32[]{:S(2)}, u32[]{:S(2)}) %collective-permute-start.3) | collective-permute-done | bytes 262176 | tf_op jit(solution)/shard_map/ppermute | solution.py:486
  21.0 2.7 %shard_map.82 = (bf16[3,2,6,128,384]{4,3,2,1,0:T(8,128)(2,1)S(1)}, f32[6,2,128,128]{3,2,1,0:T(8,128)S(1)}, f32[7,128,128]{2,1,0:T(8,128)S(1)}, f32[2,3,128,128]{3,2,1,0:T(8,128)}, f32[2,3,128,128]{3,2,1,0:T(8,128)}) custom-call(f32[512,128]{1,0:T(8,128)S(1)} %collective-permute-done.3.near_state, ...), custom_call_target="tpu_custom_call", output_to_operand_aliasing={{0}: (5, {}), {1}: (6, {}), {2}: (7, {})} | custom-call | tf_op jit(solution)/shard_map/pallas_call | solution.py:493
  23.7 1.7 %collective-permute-done.2.far_state = f32[520,128]{1,0:T(8,128)S(1)} collective-permute-done((f32[520,128]{1,0:T(8,128)S(1)}, f32[520,128]{1,0:T(8,128)S(1)}, u32[]{:S(2)}, u32[]{:S(2)}) %collective-permute-start.2) | collective-permute-done | bytes 266272 | tf_op jit(solution)/shard_map/ppermute | solution.py:485
  25.4 2.3 %shard_map.83 = (bf16[3,2,6,128,384]{4,3,2,1,0:T(8,128)(2,1)S(1)}, f32[2,3,128,128]{3,2,1,0:T(8,128)}, f32[2,3,128,128]{3,2,1,0:T(8,128)}) custom-call(f32[520,128]{1,0:T(8,128)S(1)} %collective-permute-done.2.far_state, f32[784,128]{1,0:T(8,128)S(1)} %collective-permute-done.far, ...), custom_call_target="tpu_custom_call", output_to_operand_aliasing={{0}: (6, {}), {1}: (7, {}), {2}: (8, {})} | custom-call | tf_op jit(solution)/shard_map/pallas_call | solution.py:500
Async XLA Ops:
  2.6 12.5 %collective-permute-start = (f32[784,128]{1,0:T(8,128)S(1)}, f32[784,128]{1,0:T(8,128)S(1)}, u32[]{:S(2)}, u32[]{:S(2)}) collective-permute-start(f32[784,128]{1,0:T(8,128)S(1)} %get-tuple-element.31), channel_id=1, source_target_pairs={{0,15},{1,2},{2,1},{3,4},{4,3},{5,6},{6,5},{7,8},{8,7},{9,10},{10,... | collective-permute-start | bytes 1204232 | tf_op jit(solution)/shard_map/ppermute | solution.py:459
  5.3 5.0 %collective-permute-start.1 = (f32[776,128]{1,0:T(8,128)S(1)}, f32[776,128]{1,0:T(8,128)S(1)}, u32[]{:S(2)}, u32[]{:S(2)}) collective-permute-start(f32[776,128]{1,0:T(8,128)S(1)} %get-tuple-element.33), channel_id=1, source_target_pairs={{0,1},{1,0},{2,3},{3,2},{4,5},{5,4},{6,7},{7,6},{8,9},{9,8},{10,11... | collective-permute-start | bytes 1191944 | tf_op jit(solution)/shard_map/ppermute | solution.py:460
  16.6 8.8 %collective-permute-start.2 = (f32[520,128]{1,0:T(8,128)S(1)}, f32[520,128]{1,0:T(8,128)S(1)}, u32[]{:S(2)}, u32[]{:S(2)}) collective-permute-start(f32[520,128]{1,0:T(8,128)S(1)} %get-tuple-element.43.state), channel_id=1, source_target_pairs={{0,15},{1,2},{2,1},{3,4},{4,3},{5,6},{6,5},{7,8},{8,7},{9,10},{10,... | collective-permute-start | bytes 798728 | tf_op jit(solution)/shard_map/ppermute | solution.py:485
  18.4 2.5 %collective-permute-start.3 = (f32[512,128]{1,0:T(8,128)S(1)}, f32[512,128]{1,0:T(8,128)S(1)}, u32[]{:S(2)}, u32[]{:S(2)}) collective-permute-start(f32[512,128]{1,0:T(8,128)S(1)} %get-tuple-element.44), channel_id=1, source_target_pairs={{0,1},{1,0},{2,3},{3,2},{4,5},{5,4},{6,7},{7,6},{8,9},{9,8},{10,11... | collective-permute-start | bytes 786440 | tf_op jit(solution)/shard_map/ppermute | solution.py:486

commit v4 on v3

v4 whole, which is shorter than its diff:
```python
import functools

import jax
import jax.numpy as jnp
from jax import lax
from jax.experimental import pallas as pl
from jax.experimental.pallas import tpu as pltpu
from jax.sharding import PartitionSpec as P

TERMS = 6
BS = 128
time_step = 0.5
RING = ("row", "col")
f32, bf16 = jnp.float32, jnp.bfloat16

ROWS = 6
SIGN_RE = (1.0, -1.0, -1.0, 1.0, 1.0, -1.0)
SIGN_IM = (-1.0, -1.0, 1.0, 1.0, -1.0, -1.0)
FIRST_ROWS = 4 * BS
SECOND_ROWS = 3 * BS
MORE = 8
TABLE_ROWS = 24


def own_index(row, offset):
    core = lax.axis_index("col")
    return jnp.where(core == 0, row, 1 - row), jnp.where(core == 0, 1 + offset, 1 - offset)


def own(ref, row, offset):
    r, e = own_index(row, offset)
    return ref[r, e]


def slot(ref, index):
    return ref[index * BS : (index + 1) * BS, :]


def line(ref, index):
    return ref[index : index + 1, :]


class Band:
    def __init__(self, ref, negated=False):
        self.high, self.low = ref.at[0], ref.at[1]
        self.minus = Band(ref.at[pl.ds(2, 2)]) if negated else None

    def put(self, i, j, value):
        part = slice((j - i + 1) * BS, (j - i + 2) * BS)
        high = value.astype(bf16)
        low = (value - high.astype(f32)).astype(bf16)
        self.high[i, :, part] = high
        self.low[i, :, part] = low
        if self.minus is not None:
            self.minus.high[i, :, part] = -high
            self.minus.low[i, :, part] = -low

    def left(self, i, first, last):
        part = slice((first - i + 1) * BS, (last - i + 2) * BS)
        high, low = self.high[i, :, part], self.low[i, :, part]
        return [high, high, low]

    def right(self, first, last, j, j_last):
        highs, lows = [], []
        for k in range(first, last + 1):
            part = slice((j - k + 1) * BS, (j_last - k + 2) * BS)
            highs.append(self.high[k, :, part])
            lows.append(self.low[k, :, part])
        return highs + lows + highs


def piece(h, x, rows, mids, cols):
    right = jnp.concatenate(x.right(*mids, *cols) + h.minus.right(*mids, *cols), axis=0)
    return [
        jnp.dot(
            jnp.concatenate(h.left(i, *mids) + x.left(i, *mids), axis=1), right, preferred_element_type=f32
        )
        for i in rows
    ]


def one_side(a, b, row, mids, col):
    left = jnp.concatenate(a.left(row, *mids), axis=1)
    right = jnp.concatenate(b.right(*mids, col, col), axis=0)
    return jnp.dot(left, right, preferred_element_type=f32)


def tile(h, x, i):
    upper, lower = piece(h, x, (i, i + 1), (i, i + 1), (i, i + 1))
    return upper[:, :BS], upper[:, BS:], lower[:, :BS], lower[:, BS:]


def part(h, x, i, k, j):
    return piece(h, x, (i,), (k, k), (j, j))[0]


def coefficient(term):
    return time_step / (term + 1)


SUMS = ((1, 2, 1), (1, 1, 2), (1, 3, 4), (1, 4, 3), (2, 2, 2), (2, 3, 3), (3, 2, 2), (3, 3, 3), (3, 2, 3), (3, 3, 2))
OWN = (((0, -1), (2, 1)), ((0, 0), (2, 2)), ((0, 1), (2, 3)), ((1, -1), (3, 2)), ((1, 0), (3, 3)), ((1, 1), (3, 4)))
EARLY = ((1, 2, 2), (1, 3, 3), (1, 2, 3), (1, 3, 2))
LATE = ((1, 2, 1), (1, 1, 2), (2, 2, 1), (2, 1, 2), (3, 2, 1), (3, 1, 2), (2, 2, 2), (3, 2, 2), (3, 2, 3), (3, 3, 2))
DONE_EARLY = {(2, 2): (1,), (2, 3): (1, 2), (3, 2): (1, 2), (3, 3): (1,)}
DONE_NEAR = {(3, 3): (2, 3), (3, 4): (1, 2, 3)}
DONE_FAR = {(2, 1): (1, 2, 3), (2, 2): (2, 3), (2, 3): (3,), (3, 2): (3,)}


def weighted(terms_of, signs):
    total = None
    for sign, value in zip(signs, terms_of):
        total = (value if sign > 0 else -value) if total is None else (total + value if sign > 0 else total - value)
    return total


def parts_of(values, i, j, terms):
    re_signs, im_signs = [SIGN_RE[term] for term in terms], [SIGN_IM[term] for term in terms]
    here = [values[(term, i, j)] for term in terms]
    there = here if i == j else [values[(term, j, i)] for term in terms]
    real = 0.5 * (weighted(here, re_signs) + weighted(there, re_signs).T)
    imag = 0.5 * (weighted(here, im_signs) - weighted(there, im_signs).T)
    return real, imag


def add_terms(base, values, done, phase):
    for index, (_, (i, j)) in enumerate(OWN):
        terms = [level - 1 + 3 * phase for level in done.get((i, j), ())]
        if terms:
            real, imag = parts_of(values, i, j, terms)
            base[index, 0] = base[index, 0] + real
            base[index, 1] = base[index, 1] + imag


def views(h_ref, x_ref):
    return Band(h_ref, True), [Band(x_ref.at[level]) for level in range(3)]


def before_send(h, xs, phase, table, sums, early, far, near):
    x0, x1, _ = xs
    term = 3 * phase
    t = tile(h, x0, 2)
    scale = line(table, 6 + term)
    inner = {
        (2, 2): (t[0] + part(h, x0, 2, 1, 2)) * coefficient(term),
        (3, 3): (t[3] + part(h, x0, 3, 4, 3)) * coefficient(term),
        (2, 3): t[1] * scale,
        (3, 2): t[2] * scale,
    }
    for (i, j), value in inner.items():
        x1.put(i, j, value)
    far[BS : 2 * BS, :] = inner[(2, 2)]
    near[BS : 2 * BS, :] = inner[(3, 3)]
    for index, (_, i, j) in enumerate(EARLY):
        early[index] = inner[(i, j)]
    for out, i, k in ((far, 2, 3), (near, 3, 2)):
        value = part(h, x1, i, k, i)
        out[2 * BS : 3 * BS, :] = value
        sums[SUMS.index((2, i, i))] = value


def own_first(
    re, im, ham, dip, pattern_in, field,
    far, near, table, h_ref, x_ref, sums, early, re_in, im_in,
    ham_in, dip_in, pattern, sems,
):
    copies = [
        pltpu.make_async_copy(source, target, sems.at[n])
        for n, (source, target) in enumerate(
            ((pattern_in, pattern), (ham, ham_in), (dip, dip_in), (re, re_in), (im, im_in))
        )
    ]
    for copy in copies:
        copy.start()
    copies[0].wait()
    for n, (row, offset) in enumerate(((0, -1), (0, 1), (1, 1))):
        r, e = own_index(row, offset)
        for term in range(TERMS):
            table[6 * n + term : 6 * n + term + 1, :] = jnp.full(
                (1, BS), pattern[e, r, term].astype(f32) * coefficient(term), f32
            )
    h, xs = views(h_ref, x_ref)
    for copy in copies[1:3]:
        copy.wait()
    for (row, offset), (i, j) in OWN:
        value = own(ham_in, row, offset) + field[0] * own(dip_in, row, offset)
        h.put(i, j, value)
        if j in (1, 4):
            h.put(j, i, value.T)
        if i == j:
            (far if i == 2 else near)[3 * BS : 4 * BS, :] = value
    for copy in copies[3:]:
        copy.wait()
    for (row, offset), (i, j) in OWN:
        real, imag = own(re_in, row, offset), own(im_in, row, offset)
        xs[0].put(i, j, real + imag)
        if j in (1, 4):
            xs[0].put(j, i, (real - imag).T)
        if i == j:
            (far if i == 2 else near)[0:BS, :] = real + imag
    before_send(h, xs, 0, table, sums, early, far, near)


def own_rest(h, xs, phase, table, early, base, sums):
    x0, x1, x2 = xs
    term = 3 * phase
    values = {(term, i, j): early[index] for index, (_, i, j) in enumerate(EARLY)}
    t = tile(h, x1, 2)
    scale = line(table, 6 + term + 1)
    for (i, j), value in (((2, 3), t[1] * scale), ((3, 2), t[2] * scale)):
        x2.put(i, j, value)
        values[(term + 1, i, j)] = value
    for a, b in ((3, 4), (2, 1)):
        sums[SUMS.index((1, a, b))] = part(h, x0, a, a, b)
        sums[SUMS.index((1, b, a))] = part(h, x0, b, a, a)
    sums[SUMS.index((3, 2, 2))] = part(h, x2, 2, 3, 2)
    sums[SUMS.index((3, 3, 3))] = part(h, x2, 3, 2, 3)
    add_terms(base, values, DONE_EARLY, phase)


def side(h, xs, a, b, payload, phase, scales, sums, record):
    x0, x1, x2 = xs
    c = [coefficient(3 * phase + n) for n in range(3)]
    low = min(a, b)
    at_a, at_b = (0, 3) if a == low else (3, 0)
    up, down = (low, low + 1), (low + 1, low)

    def known(level, i, j):
        return sums[SUMS.index((level, i, j))]

    def put(level, i, j, value):
        record(level, i, j, value)
        if level < 3:
            xs[level].put(i, j, value)

    x0.put(b, b, slot(payload, 0))
    x1.put(b, b, slot(payload, 1))
    put(1, a, b, (part(h, x0, a, b, b) + known(1, a, b)) * scales[0])
    put(1, b, a, (part(h, x0, b, b, a) + known(1, b, a)) * scales[0])
    t = tile(h, x1, low)
    put(2, a, a, (t[at_a] + known(2, a, a)) * c[1])
    put(2, b, b, (t[at_b] + slot(payload, 2)) * c[1])
    put(2, *up, t[1] * scales[1])
    put(2, *down, t[2] * scales[1])
    t = tile(h, x2, low)
    put(3, *up, t[1] * scales[2])
    put(3, *down, t[2] * scales[2])
    put(3, a, a, (t[at_a] + known(3, a, a)) * c[2])


def near_side(h, xs, near, phase, table, base, sums):
    term = 3 * phase
    values = {}

    def record(level, i, j, value):
        values[(term + level - 1, i, j)] = value

    scales = [line(table, 12 + term + n) for n in range(3)]
    side(h, xs, 3, 4, near, phase, scales, sums, record)
    x2 = xs[2]
    sums[SUMS.index((3, 2, 3))] = one_side(h, x2, 2, (2, 3), 3) + one_side(x2, h.minus, 2, (3, 3), 3)
    sums[SUMS.index((3, 3, 2))] = one_side(h, x2, 3, (3, 3), 2) + one_side(x2, h.minus, 3, (2, 3), 2)
    add_terms(base, values, DONE_NEAR, phase)
    return values


def far_side(h, xs, far, phase, table, sums, record):
    term = 3 * phase
    scales = [line(table, term + n) for n in range(3)]
    side(h, xs, 2, 1, far, phase, scales, sums, record)
    x2 = xs[2]
    scale = line(table, 6 + term + 2)
    record(3, 2, 3, (one_side(x2, h.minus, 2, (2, 2), 3) + sums[SUMS.index((3, 2, 3))]) * scale)
    record(3, 3, 2, (one_side(h, x2, 3, (2, 2), 2) + sums[SUMS.index((3, 3, 2))]) * scale)


def rest_first(re_in, im_in, table, early, h_ref, x_in, sums_in, x_ref, sums, base):
    h, xs = views(h_ref, x_ref)
    for index, ((row, offset), _) in enumerate(OWN):
        base[index, 0], base[index, 1] = own(re_in, row, offset), own(im_in, row, offset)
    own_rest(h, xs, 0, table, early, base, sums)


def near_first(near, table, h_in, x_in, sums_in, base_in, h_ref, x_ref, sums, base, inner_state):
    h, xs = views(h_ref, x_ref)
    h.put(4, 4, slot(near, 3))
    values = near_side(h, xs, near, 0, table, base, sums)
    for i, j in ((3, 3), (3, 4), (4, 3)):
        xs[0].put(i, j, values[(2, i, j)])
    inner_state[...] = values[(2, 3, 3)]


def far_first(far, table, inner_state, h_in, x_in, sums_in, h_ref, x_ref, sums, late, early, far_next, near_next):
    h, xs = views(h_ref, x_ref)
    h.put(1, 1, slot(far, 3))
    state = {}

    def record(level, i, j, value):
        if (level, i, j) in LATE:
            late[LATE.index((level, i, j))] = value
        if level == 3:
            state[(i, j)] = value

    far_side(h, xs, far, 0, table, sums, record)
    for (i, j), value in state.items():
        xs[0].put(i, j, value)
    far_next[0:BS, :] = state[(2, 2)]
    near_next[0:BS, :] = inner_state[...]
    before_send(h, xs, 1, table, sums, early, far_next, near_next)


def rest_second(late, early, table, h_ref, x_in, sums_in, base_in, x_ref, sums, base):
    h, xs = views(h_ref, x_ref)
    values = {(level - 1, i, j): late[index] for index, (level, i, j) in enumerate(LATE)}
    add_terms(base, values, DONE_FAR, 0)
    own_rest(h, xs, 1, table, early, base, sums)


def near_second(near, table, h_ref, x_in, sums_in, base_in, x_ref, sums, base, out_re, out_im, sems):
    h, xs = views(h_ref, x_ref)
    near_side(h, xs, near, 1, table, base, sums)
    copies = []
    for index, ((row, offset), _) in tuple(enumerate(OWN))[4:]:
        r, e = own_index(row, offset)
        for a, out in enumerate((out_re, out_im)):
            copies.append(pltpu.make_async_copy(base.at[index, a], out.at[r, e], sems.at[len(copies)]))
    for copy in copies:
        copy.start()
    for copy in copies:
        copy.wait()


def far_second(far, table, sums, base, h_ref, x_in, in_re, in_im, x_ref, out_re, out_im, stage, sems):
    h, xs = views(h_ref, x_ref)
    values = {}

    def record(level, i, j, value):
        values[(level + 2, i, j)] = value

    far_side(h, xs, far, 1, table, sums, record)
    copies = []
    for index in (2, 3, 0, 1):
        (row, offset), (i, j) = OWN[index]
        real, imag = parts_of(values, i, j, [level + 2 for level in DONE_FAR[(i, j)]])
        stage[index, 0], stage[index, 1] = base[index, 0] + real, base[index, 1] + imag
        r, e = own_index(row, offset)
        for a, out in enumerate((out_re, out_im)):
            copies.append(pltpu.make_async_copy(stage.at[index, a], out.at[r, e], sems.at[len(copies)]))
            copies[-1].start()
    for copy in copies:
        copy.wait()


VECTOR = pl.BlockSpec(memory_space=pltpu.VMEM)
SCALAR = pl.BlockSpec(memory_space=pltpu.SMEM)
BIG = pl.BlockSpec(memory_space=pltpu.HBM)


def call(kernel, ins, outs, scratch=(), aliases=None):
    return pl.pallas_call(
        kernel,
        out_shape=[shape for shape, _ in outs],
        in_specs=ins,
        out_specs=[spec for _, spec in outs],
        scratch_shapes=list(scratch),
        input_output_aliases=aliases or {},
        compiler_params=pltpu.CompilerParams(vmem_limit_bytes=24 * 2**20),
        cost_estimate=pl.CostEstimate(flops=0, bytes_accessed=0, transcendentals=0),
    )


def vector(*shape, dtype=f32):
    return jax.ShapeDtypeStruct(shape, dtype), VECTOR


def body(density_real, density_imag, hamiltonian, dipole, field, pattern):
    count = lax.axis_size(RING)
    pair = [(i, i ^ 1) for i in range(count)]
    cross = [(i, (i + 1) % count if i % 2 else (i - 1) % count) for i in range(count)]
    pattern = jnp.transpose(pattern, (2, 1, 0))
    whole = density_real.shape
    inputs = [
        pltpu.with_memory_space_constraint(x, pltpu.HBM)
        for x in (density_real, density_imag, hamiltonian, dipole, pattern)
    ]
    dma = pltpu.SemaphoreType.DMA
    h_out, x_out = vector(4, ROWS, BS, 3 * BS, dtype=bf16), vector(3, 2, ROWS, BS, 3 * BS, dtype=bf16)
    base_out, sums_out = vector(len(OWN), 2, BS, BS), vector(len(SUMS), BS, BS)
    early_out, late_out = vector(len(EARLY), BS, BS), vector(len(LATE), BS, BS)
    out = (jax.ShapeDtypeStruct(whole, f32), BIG)

    far, near, table, h, x, sums, early, re_in, im_in = call(
        own_first,
        [BIG] * 5 + [SCALAR],
        [
            vector(FIRST_ROWS + MORE, BS),
            vector(FIRST_ROWS, BS),
            vector(TABLE_ROWS, BS),
            h_out,
            x_out,
            sums_out,
            early_out,
            vector(*whole),
            vector(*whole),
        ],
        [pltpu.VMEM(whole, f32)] * 2 + [pltpu.SMEM(pattern.shape, jnp.int32), dma((5,))],
    )(*inputs, field)
    far = lax.ppermute(far, RING, cross)
    near = lax.ppermute(near, RING, pair)
    x, sums, base = call(
        rest_first,
        [VECTOR] * 7,
        [x_out, sums_out, base_out],
        aliases={5: 0, 6: 1},
    )(re_in, im_in, table, early, h, x, sums)
    h, x, sums, base, inner_state = call(
        near_first,
        [VECTOR] * 6,
        [h_out, x_out, sums_out, base_out, vector(BS, BS)],
        aliases={2: 0, 3: 1, 4: 2, 5: 3},
    )(near, table, h, x, sums, base)
    h, x, sums, late, early, far, near = call(
        far_first,
        [VECTOR] * 6,
        [
            h_out,
            x_out,
            sums_out,
            late_out,
            early_out,
            vector(SECOND_ROWS + MORE, BS),
            vector(SECOND_ROWS, BS),
        ],
        aliases={3: 0, 4: 1, 5: 2},
    )(far, table, inner_state, h, x, sums)
    far = lax.ppermute(far, RING, cross)
    near = lax.ppermute(near, RING, pair)
    x, sums, base = call(
        rest_second,
        [VECTOR] * 7,
        [x_out, sums_out, base_out],
        aliases={4: 0, 5: 1, 6: 2},
    )(late, early, table, h, x, sums, base)
    x, sums, base, out_re, out_im = call(
        near_second,
        [VECTOR] * 6,
        [x_out, sums_out, base_out, out, out],
        [dma((4,))],
        aliases={3: 0, 4: 1, 5: 2},
    )(near, table, h, x, sums, base)
    _, out_re, out_im = call(
        far_second,
        [VECTOR] * 6 + [BIG] * 2,
        [x_out, out, out],
        [pltpu.VMEM((4, 2, BS, BS), f32), dma((8,))],
        aliases={5: 0, 6: 1, 7: 2},
    )(far, table, sums, base, h, x, out_re, out_im)
    return out_re, out_im


def solution(mesh):
    in_specs = (
        P(("row", "col"), None, None, None),
        P(("row", "col"), None, None, None),
        P(("row", "col"), None, None, None),
        P(("parts", "row", "col"), None, None, None),
        P("parts"),
        P(None, ("row", "col"), None),
    )
    out_specs = (
        P(("parts", "row", "col"), None, None, None),
        P(("parts", "row", "col"), None, None, None),
    )
    return jax.shard_map(body, mesh=mesh, in_specs=in_specs, out_specs=out_specs, check_vma=False)
```

time: 27.9 us -> 25 us (0.90)
  the two profiles are of different devices: /device:TPU:1 before, /device:TPU:0 now
where the time goes in v4:
time: 25 us; the launch traced here: 24.8 us
  Pallas kernels  10.5 us (42%)
  starting transfers between devices  10 us (40%)
  waiting for transfers between devices  3.02 us (12%)
  between operations  1.32 us (5%)
    ppermute x2, starting transfers between devices, body(): far = lax.ppermute(far, RING, cross)  10 us
    pallas_call x1, Pallas kernels, body(): call(own_first, [BIG] * 5 + [SCALAR], [vector(FIRST_ROWS + MORE, BS), vec...  2.1 us
    pallas_call x1, Pallas kernels, body(): call(far_second, [VECTOR] * 6 + [BIG] * 2, [x_out, out, out], [pltpu.VMEM...  2.05 us
    pallas_call x1, Pallas kernels, body(): call(near_second, [VECTOR] * 6, [x_out, sums_out, base_out, out, out], [d...  1.89 us
    pallas_call x1, Pallas kernels, body(): call(far_first, [VECTOR] * 6, [h_out, x_out, sums_out, late_out, early_ou...  1.75 us
    ppermute x2, waiting for transfers between devices, body(): far = lax.ppermute(far, RING, cross)  1.52 us
    ppermute x2, waiting for transfers between devices, body(): near = lax.ppermute(near, RING, pair)  1.49 us
    pallas_call x1, Pallas kernels, body(): call(near_first, [VECTOR] * 6, [h_out, x_out, sums_out, base_out, vector(...  1.22 us
  transfers between devices with their start and end apart: 4, of which 4 were waited for; matrix products, arithmetic and copies ran while one was open for 0% of the time, Pallas kernels for 18%

profile of v4, /device:TPU:0, one launch (start us, length us, event | category | flops | bytes accessed | tf_op | source)
XLA Modules:
  0.0 24.8 jit_solution(3759706737616106843)
XLA Ops:
  1.3 2.1 %shard_map.77 = (f32[520,128]{1,0:T(8,128)S(1)}, f32[512,128]{1,0:T(8,128)S(1)}, f32[24,128]{1,0:T(8,128)S(1)}, bf16[4,6,128,384]{3,2,1,0:T(8,128)(2,1)S(1)}, bf...) custom-call(f32[2,3,128,128]{3,2,1,0:T(8,128)} %re.1, ...), custom_call_target="tpu_custom_call" | custom-call | tf_op jit(solution)/shard_map/pallas_call | solution.py:392
  3.4 5.5 %collective-permute-start = (f32[520,128]{1,0:T(8,128)S(1)}, f32[520,128]{1,0:T(8,128)S(1)}, u32[]{:S(2)}, u32[]{:S(2)}) collective-permute-start(f32[520,128]{1,0:T(8,128)S(1)} %get-tuple-element.36), channel_id=1, source_target_pairs={{0,15},{1,2},{2,1},{3,4},{4,3},{5,6},{6,5},{7,8},{8,7},{9,10},{10,... | collective-permute-start | bytes 798728 | tf_op jit(solution)/shard_map/ppermute | solution.py:408
  8.9 0.0 collective-permute-start.1
  8.9 0.7 %shard_map.78 = (bf16[3,2,6,128,384]{4,3,2,1,0:T(8,128)(2,1)S(1)}, f32[10,128,128]{2,1,0:T(8,128)S(1)}, f32[6,2,128,128]{3,2,1,0:T(8,128)S(1)}) custom-call(f32[2,3,128,128]{3,2,1,0:T(8,128)S(1)} %get-tuple-element.40.re_in, f32[2,3,128,128]{3,2,1,0:T(8,128)S(1)} %get-tuple-element.41.im_in, ...), custom_call_target="tpu_custom_call", output_to_operand_aliasing={{0}: (5, {}), {1}: (6, {})} | custom-call | tf_op jit(solution)/shard_map/pallas_call | solution.py:410
  9.6 0.8 %collective-permute-done.1.near = f32[512,128]{1,0:T(8,128)S(1)} collective-permute-done((f32[512,128]{1,0:T(8,128)S(1)}, f32[512,128]{1,0:T(8,128)S(1)}, u32[]{:S(2)}, u32[]{:S(2)}) %collective-permute-start.1) | collective-permute-done | bytes 262176 | tf_op jit(solution)/shard_map/ppermute | solution.py:409
  10.4 1.2 %shard_map.79 = (bf16[4,6,128,384]{3,2,1,0:T(8,128)(2,1)S(1)}, bf16[3,2,6,128,384]{4,3,2,1,0:T(8,128)(2,1)S(1)}, f32[10,128,128]{2,1,0:T(8,128)S(1)}, f32[6,2,128,128]{3,2,1,0:T(8,128)S(1)}, f32[128,128]{1,0:T(8,128)S(1)}) custom-call(f32[512,128]{1,0:T(8,128)S(1)} %collective-permute-done.1., ...), custom_call_target="tpu_custom_call", output_to_operand_aliasing={{0}: (2, {}), {1}: (3, {}), {2}: (4, {}), {3}: (5, {})} | custom-call | tf_op jit(solution)/shard_map/pallas_call | solution.py:416
  11.7 1.4 %collective-permute-done.far = f32[520,128]{1,0:T(8,128)S(1)} collective-permute-done((f32[520,128]{1,0:T(8,128)S(1)}, f32[520,128]{1,0:T(8,128)S(1)}, u32[]{:S(2)}, u32[]{:S(2)}) %collective-permute-start) | collective-permute-done | bytes 266272 | tf_op jit(solution)/shard_map/ppermute | solution.py:408
  13.1 1.7 %shard_map.80 = (bf16[4,6,128,384]{3,2,1,0:T(8,128)(2,1)S(1)}, bf16[3,2,6,128,384]{4,3,2,1,0:T(8,128)(2,1)S(1)}, f32[10,128,128]{2,1,0:T(8,128)S(1)}, f32[10,128...) custom-call(f32[520,128]{1,0:T(8,128)S(1)} %collective-permute-done., ...), custom_call_target="tpu_custom_call", output_to_operand_aliasing={{0}: (3, {}), {1}: (4, {}), {2}: (5, {})} | custom-call | tf_op jit(solution)/shard_map/pallas_call | solution.py:422
  14.8 4.5 %collective-permute-start.2 = (f32[392,128]{1,0:T(8,128)S(1)}, f32[392,128]{1,0:T(8,128)S(1)}, u32[]{:S(2)}, u32[]{:S(2)}) collective-permute-start(f32[392,128]{1,0:T(8,128)S(1)} %get-tuple-element.52), channel_id=1, source_target_pairs={{0,15},{1,2},{2,1},{3,4},{4,3},{5,6},{6,5},{7,8},{8,7},{9,10},{10,... | collective-permute-start | bytes 602120 | tf_op jit(solution)/shard_map/ppermute | solution.py:436
  19.4 0.0 collective-permute-start.3
  19.4 0.8 %shard_map.81 = (bf16[3,2,6,128,384]{4,3,2,1,0:T(8,128)(2,1)S(1)}, f32[10,128,128]{2,1,0:T(8,128)S(1)}, f32[6,2,128,128]{3,2,1,0:T(8,128)S(1)}) custom-call(f32[10,128,128]{2,1,0:T(8,128)S(1)} %get-tuple-element.55.late, f32[4,128,128]{2,1,0:T(8,128)S(1)} %get-tuple-element.56.early, ...), custom_call_target="tpu_custom_call", output_to_operand_aliasing={{0}: (4, {}), {1}: (5, {}), {2}: (6, {})} | custom-call | tf_op jit(solution)/shard_map/pallas_call | solution.py:438
  20.1 0.7 %collective-permute-done.3.near = f32[384,128]{1,0:T(8,128)S(1)} collective-permute-done((f32[384,128]{1,0:T(8,128)S(1)}, f32[384,128]{1,0:T(8,128)S(1)}, u32[]{:S(2)}, u32[]{:S(2)}) %collective-permute-start.3) | collective-permute-done | bytes 196640 | tf_op jit(solution)/shard_map/ppermute | solution.py:437
  20.8 1.9 %shard_map.82 = (bf16[3,2,6,128,384]{4,3,2,1,0:T(8,128)(2,1)S(1)}, f32[10,128,128]{2,1,0:T(8,128)S(1)}, f32[6,2,128,128]{3,2,1,0:T(8,128)S(1)}, f32[2,3,128,128]{3,2,1,0:T(8,128)}, f32[2,3,128,128]{3,2,1,0:T(8,128)}) custom-call(f32[384,128]{1,0:T(8,128)S(1)} %collective-permute-done.3.near, ...), custom_call_target="tpu_custom_call", output_to_operand_aliasing={{0}: (3, {}), {1}: (4, {}), {2}: (5, {})} | custom-call | tf_op jit(solution)/shard_map/pallas_call | solution.py:444
  22.7 0.1 collective-permute-done.2.far
  22.8 2.0 %shard_map.83 = (bf16[3,2,6,128,384]{4,3,2,1,0:T(8,128)(2,1)S(1)}, f32[2,3,128,128]{3,2,1,0:T(8,128)}, f32[2,3,128,128]{3,2,1,0:T(8,128)}) custom-call(f32[392,128]{1,0:T(8,128)S(1)} %collective-permute-done.2.far, f32[24,128]{1,0:T(8,128)S(1)} %get-tuple-element.37.table, ...), custom_call_target="tpu_custom_call", output_to_operand_aliasing={{0}: (5, {}), {1}: (6, {}), {2}: (7, {})} | custom-call | tf_op jit(solution)/shard_map/pallas_call | solution.py:451
Async XLA Ops:
  3.4 9.7 %collective-permute-start = (f32[520,128]{1,0:T(8,128)S(1)}, f32[520,128]{1,0:T(8,128)S(1)}, u32[]{:S(2)}, u32[]{:S(2)}) collective-permute-start(f32[520,128]{1,0:T(8,128)S(1)} %get-tuple-element.36), channel_id=1, source_target_pairs={{0,15},{1,2},{2,1},{3,4},{4,3},{5,6},{6,5},{7,8},{8,7},{9,10},{10,... | collective-permute-start | bytes 798728 | tf_op jit(solution)/shard_map/ppermute | solution.py:408
  8.9 1.5 %collective-permute-start.1 = (f32[512,128]{1,0:T(8,128)S(1)}, f32[512,128]{1,0:T(8,128)S(1)}, u32[]{:S(2)}, u32[]{:S(2)}) collective-permute-start(f32[512,128]{1,0:T(8,128)S(1)} %get-tuple-element.38), channel_id=1, source_target_pairs={{0,1},{1,0},{2,3},{3,2},{4,5},{5,4},{6,7},{7,6},{8,9},{9,8},{10,11... | collective-permute-start | bytes 786440 | tf_op jit(solution)/shard_map/ppermute | solution.py:409
  14.8 7.9 %collective-permute-start.2 = (f32[392,128]{1,0:T(8,128)S(1)}, f32[392,128]{1,0:T(8,128)S(1)}, u32[]{:S(2)}, u32[]{:S(2)}) collective-permute-start(f32[392,128]{1,0:T(8,128)S(1)} %get-tuple-element.52), channel_id=1, source_target_pairs={{0,15},{1,2},{2,1},{3,4},{4,3},{5,6},{6,5},{7,8},{8,7},{9,10},{10,... | collective-permute-start | bytes 602120 | tf_op jit(solution)/shard_map/ppermute | solution.py:436
  19.4 1.4 %collective-permute-start.3 = (f32[384,128]{1,0:T(8,128)S(1)}, f32[384,128]{1,0:T(8,128)S(1)}, u32[]{:S(2)}, u32[]{:S(2)}) collective-permute-start(f32[384,128]{1,0:T(8,128)S(1)} %get-tuple-element.53), channel_id=1, source_target_pairs={{0,1},{1,0},{2,3},{3,2},{4,5},{5,4},{6,7},{7,6},{8,9},{9,8},{10,11... | collective-permute-start | bytes 589832 | tf_op jit(solution)/shard_map/ppermute | solution.py:437

commit v5 on v4

--- a/solution.py
+++ b/solution.py
@@ -70,13 +70,13 @@
 
 
 def piece(h, x, rows, mids, cols):
-    right = jnp.concatenate(x.right(*mids, *cols) + h.minus.right(*mids, *cols), axis=0)
-    return [
-        jnp.dot(
-            jnp.concatenate(h.left(i, *mids) + x.left(i, *mids), axis=1), right, preferred_element_type=f32
-        )
-        for i in rows
-    ]
+    after_h = jnp.concatenate(x.right(*mids, *cols), axis=0)
+    after_x = jnp.concatenate(h.minus.right(*mids, *cols), axis=0)
+
+    def product(left, right):
+        return jnp.dot(jnp.concatenate(left, axis=1), right, preferred_element_type=f32)
+
+    return [product(h.left(i, *mids), after_h) + product(x.left(i, *mids), after_x) for i in rows]
 
 
 def one_side(a, b, row, mids, col):
@@ -316,37 +316,36 @@
     own_rest(h, xs, 1, table, early, base, sums)
 
 
-def near_second(near, table, h_ref, x_in, sums_in, base_in, x_ref, sums, base, out_re, out_im, sems):
+def near_second(near, table, h_ref, x_in, sums_in, base_in, x_ref, sums, base):
     h, xs = views(h_ref, x_ref)
     near_side(h, xs, near, 1, table, base, sums)
+
+
+def far_second(far, table, sums, base, h_ref, x_in, x_ref, out_re, out_im, stage, sems):
+    h, xs = views(h_ref, x_ref)
+    outs = (out_re, out_im)
+
+    def start(index, source):
+        row, offset = OWN[index][0]
+        r, e = own_index(row, offset)
+        for a, out in enumerate(outs):
+            copies.append(pltpu.make_async_copy(source.at[index, a], out.at[r, e], sems.at[len(copies)]))
+            copies[-1].start()
+
     copies = []
-    for index, ((row, offset), _) in tuple(enumerate(OWN))[4:]:
-        r, e = own_index(row, offset)
-        for a, out in enumerate((out_re, out_im)):
-            copies.append(pltpu.make_async_copy(base.at[index, a], out.at[r, e], sems.at[len(copies)]))
-    for copy in copies:
-        copy.start()
-    for copy in copies:
-        copy.wait()
-
-
-def far_second(far, table, sums, base, h_ref, x_in, in_re, in_im, x_ref, out_re, out_im, stage, sems):
-    h, xs = views(h_ref, x_ref)
+    for index in (4, 5):
+        start(index, base)
     values = {}
 
     def record(level, i, j, value):
         values[(level + 2, i, j)] = value
 
     far_side(h, xs, far, 1, table, sums, record)
-    copies = []
     for index in (2, 3, 0, 1):
-        (row, offset), (i, j) = OWN[index]
+        i, j = OWN[index][1]
         real, imag = parts_of(values, i, j, [level + 2 for level in DONE_FAR[(i, j)]])
         stage[index, 0], stage[index, 1] = base[index, 0] + real, base[index, 1] + imag
-        r, e = own_index(row, offset)
-        for a, out in enumerate((out_re, out_im)):
-            copies.append(pltpu.make_async_copy(stage.at[index, a], out.at[r, e], sems.at[len(copies)]))
-            copies[-1].start()
+        start(index, stage)
     for copy in copies:
         copy.wait()
 
@@ -441,20 +440,19 @@
         [x_out, sums_out, base_out],
         aliases={4: 0, 5: 1, 6: 2},
     )(late, early, table, h, x, sums, base)
-    x, sums, base, out_re, out_im = call(
+    x, sums, base = call(
         near_second,
         [VECTOR] * 6,
-        [x_out, sums_out, base_out, out, out],
-        [dma((4,))],
+        [x_out, sums_out, base_out],
         aliases={3: 0, 4: 1, 5: 2},
     )(near, table, h, x, sums, base)
     _, out_re, out_im = call(
         far_second,
-        [VECTOR] * 6 + [BIG] * 2,
+        [VECTOR] * 6,
         [x_out, out, out],
-        [pltpu.VMEM((4, 2, BS, BS), f32), dma((8,))],
-        aliases={5: 0, 6: 1, 7: 2},
-    )(far, table, sums, base, h, x, out_re, out_im)
+        [pltpu.VMEM((4, 2, BS, BS), f32), dma((12,))],
+        aliases={5: 0},
+    )(far, table, sums, base, h, x)
     return out_re, out_im
 
 

time: 25 us -> 24.6 us (0.984)
  Pallas kernels: 10.5 us -> 9.07 us
  waiting for transfers between devices: 3.02 us -> 4 us
    ppermute x2, waiting for transfers between devices: 1.52 us -> 2.48 us  [body(): far = lax.ppermute(far, RING, cross)]
    pallas_call x2, Pallas kernels: 3.94 us -> 3.01 us  [the longest x1 1.95 us: body(): call(far_second, [VECTOR] * 6, [x_out, out, out], [pltpu.VMEM((4, 2, BS,...]
  transfers between devices with their start and end apart: 4 -> 4, of which waited for: 4 -> 4; matrix products, arithmetic and copies ran while one was open for 0% -> 0% of each run, Pallas kernels for 18% -> 15%
where the time goes in v5:
time: 24.6 us; the launch traced here: 24.4 us
  starting transfers between devices  10 us (41%)
  Pallas kernels  9.07 us (37%)
  waiting for transfers between devices  4 us (16%)
  between operations  1.31 us (5%)
    ppermute x2, starting transfers between devices, body(): far = lax.ppermute(far, RING, cross)  10 us
    ppermute x2, waiting for transfers between devices, body(): far = lax.ppermute(far, RING, cross)  2.48 us
    pallas_call x1, Pallas kernels, body(): call(own_first, [BIG] * 5 + [SCALAR], [vector(FIRST_ROWS + MORE, BS), vec...  2.02 us
    pallas_call x1, Pallas kernels, body(): call(far_second, [VECTOR] * 6, [x_out, out, out], [pltpu.VMEM((4, 2, BS,...  1.95 us
    ppermute x2, waiting for transfers between devices, body(): near = lax.ppermute(near, RING, pair)  1.51 us
    pallas_call x1, Pallas kernels, body(): call(far_first, [VECTOR] * 6, [h_out, x_out, sums_out, late_out, early_ou...  1.5 us
    pallas_call x1, Pallas kernels, body(): call(near_first, [VECTOR] * 6, [h_out, x_out, sums_out, base_out, vector(...  1.09 us
    pallas_call x1, Pallas kernels, body(): call(near_second, [VECTOR] * 6, [x_out, sums_out, base_out], aliases={3:...  1.07 us
  transfers between devices with their start and end apart: 4, of which 4 were waited for; matrix products, arithmetic and copies ran while one was open for 0% of the time, Pallas kernels for 15%

profile of v5, /device:TPU:0, one launch (start us, length us, event | category | flops | bytes accessed | tf_op | source)
XLA Modules:
  0.0 24.4 jit_solution(12644481310189862091)
XLA Ops:
  1.3 2.0 %shard_map.77 = (f32[520,128]{1,0:T(8,128)S(1)}, f32[512,128]{1,0:T(8,128)S(1)}, f32[24,128]{1,0:T(8,128)S(1)}, bf16[4,6,128,384]{3,2,1,0:T(8,128)(2,1)S(1)}, bf...) custom-call(f32[2,3,128,128]{3,2,1,0:T(8,128)} %re.1, ...), custom_call_target="tpu_custom_call" | custom-call | tf_op jit(solution)/shard_map/pallas_call | solution.py:391
  3.3 5.5 %collective-permute-start = (f32[520,128]{1,0:T(8,128)S(1)}, f32[520,128]{1,0:T(8,128)S(1)}, u32[]{:S(2)}, u32[]{:S(2)}) collective-permute-start(f32[520,128]{1,0:T(8,128)S(1)} %get-tuple-element.34), channel_id=1, source_target_pairs={{0,15},{1,2},{2,1},{3,4},{4,3},{5,6},{6,5},{7,8},{8,7},{9,10},{10,... | collective-permute-start | bytes 798728 | tf_op jit(solution)/shard_map/ppermute | solution.py:407
  8.8 0.0 collective-permute-start.1
  8.8 0.7 %shard_map.78 = (bf16[3,2,6,128,384]{4,3,2,1,0:T(8,128)(2,1)S(1)}, f32[10,128,128]{2,1,0:T(8,128)S(1)}, f32[6,2,128,128]{3,2,1,0:T(8,128)S(1)}) custom-call(f32[2,3,128,128]{3,2,1,0:T(8,128)S(1)} %get-tuple-element.38.re_in, f32[2,3,128,128]{3,2,1,0:T(8,128)S(1)} %get-tuple-element.39.im_in, ...), custom_call_target="tpu_custom_call", output_to_operand_aliasing={{0}: (5, {}), {1}: (6, {})} | custom-call | tf_op jit(solution)/shard_map/pallas_call | solution.py:409
  9.5 0.8 %collective-permute-done.1.near = f32[512,128]{1,0:T(8,128)S(1)} collective-permute-done((f32[512,128]{1,0:T(8,128)S(1)}, f32[512,128]{1,0:T(8,128)S(1)}, u32[]{:S(2)}, u32[]{:S(2)}) %collective-permute-start.1) | collective-permute-done | bytes 262176 | tf_op jit(solution)/shard_map/ppermute | solution.py:408
  10.4 1.1 %shard_map.79 = (bf16[4,6,128,384]{3,2,1,0:T(8,128)(2,1)S(1)}, bf16[3,2,6,128,384]{4,3,2,1,0:T(8,128)(2,1)S(1)}, f32[10,128,128]{2,1,0:T(8,128)S(1)}, f32[6,2,128,128]{3,2,1,0:T(8,128)S(1)}, f32[128,128]{1,0:T(8,128)S(1)}) custom-call(f32[512,128]{1,0:T(8,128)S(1)} %collective-permute-done.1., ...), custom_call_target="tpu_custom_call", output_to_operand_aliasing={{0}: (2, {}), {1}: (3, {}), {2}: (4, {}), {3}: (5, {})} | custom-call | tf_op jit(solution)/shard_map/pallas_call | solution.py:415
  11.4 1.6 %collective-permute-done.far = f32[520,128]{1,0:T(8,128)S(1)} collective-permute-done((f32[520,128]{1,0:T(8,128)S(1)}, f32[520,128]{1,0:T(8,128)S(1)}, u32[]{:S(2)}, u32[]{:S(2)}) %collective-permute-start) | collective-permute-done | bytes 266272 | tf_op jit(solution)/shard_map/ppermute | solution.py:407
  13.0 1.5 %shard_map.80 = (bf16[4,6,128,384]{3,2,1,0:T(8,128)(2,1)S(1)}, bf16[3,2,6,128,384]{4,3,2,1,0:T(8,128)(2,1)S(1)}, f32[10,128,128]{2,1,0:T(8,128)S(1)}, f32[10,128...) custom-call(f32[520,128]{1,0:T(8,128)S(1)} %collective-permute-done., ...), custom_call_target="tpu_custom_call", output_to_operand_aliasing={{0}: (3, {}), {1}: (4, {}), {2}: (5, {})} | custom-call | tf_op jit(solution)/shard_map/pallas_call | solution.py:421
  14.5 4.5 %collective-permute-start.2 = (f32[392,128]{1,0:T(8,128)S(1)}, f32[392,128]{1,0:T(8,128)S(1)}, u32[]{:S(2)}, u32[]{:S(2)}) collective-permute-start(f32[392,128]{1,0:T(8,128)S(1)} %get-tuple-element.50), channel_id=1, source_target_pairs={{0,15},{1,2},{2,1},{3,4},{4,3},{5,6},{6,5},{7,8},{8,7},{9,10},{10,... | collective-permute-start | bytes 602120 | tf_op jit(solution)/shard_map/ppermute | solution.py:435
  19.0 0.0 collective-permute-start.3
  19.0 0.7 %shard_map.81 = (bf16[3,2,6,128,384]{4,3,2,1,0:T(8,128)(2,1)S(1)}, f32[10,128,128]{2,1,0:T(8,128)S(1)}, f32[6,2,128,128]{3,2,1,0:T(8,128)S(1)}) custom-call(f32[10,128,128]{2,1,0:T(8,128)S(1)} %get-tuple-element.53.late, f32[4,128,128]{2,1,0:T(8,128)S(1)} %get-tuple-element.54.early, ...), custom_call_target="tpu_custom_call", output_to_operand_aliasing={{0}: (4, {}), {1}: (5, {}), {2}: (6, {})} | custom-call | tf_op jit(solution)/shard_map/pallas_call | solution.py:437
  19.8 0.7 %collective-permute-done.3.near = f32[384,128]{1,0:T(8,128)S(1)} collective-permute-done((f32[384,128]{1,0:T(8,128)S(1)}, f32[384,128]{1,0:T(8,128)S(1)}, u32[]{:S(2)}, u32[]{:S(2)}) %collective-permute-start.3) | collective-permute-done | bytes 196640 | tf_op jit(solution)/shard_map/ppermute | solution.py:436
  20.5 1.1 %shard_map.82 = (bf16[3,2,6,128,384]{4,3,2,1,0:T(8,128)(2,1)S(1)}, f32[10,128,128]{2,1,0:T(8,128)S(1)}, f32[6,2,128,128]{3,2,1,0:T(8,128)S(1)}) custom-call(f32[384,128]{1,0:T(8,128)S(1)} %collective-permute-done.3.near, f32[24,128]{1,0:T(8,128)S(1)} %get-tuple-element.35.table, ...), custom_call_target="tpu_custom_call", output_to_operand_aliasing={{0}: (3, {}), {1}: (4, {}), {2}: (5, {})} | custom-call | tf_op jit(solution)/shard_map/pallas_call | solution.py:443
  21.6 0.9 %collective-permute-done.2.far = f32[392,128]{1,0:T(8,128)S(1)} collective-permute-done((f32[392,128]{1,0:T(8,128)S(1)}, f32[392,128]{1,0:T(8,128)S(1)}, u32[]{:S(2)}, u32[]{:S(2)}) %collective-permute-start.2) | collective-permute-done | bytes 200736 | tf_op jit(solution)/shard_map/ppermute | solution.py:435
  22.5 1.9 %shard_map.83 = (bf16[3,2,6,128,384]{4,3,2,1,0:T(8,128)(2,1)S(1)}, f32[2,3,128,128]{3,2,1,0:T(8,128)}, f32[2,3,128,128]{3,2,1,0:T(8,128)}) custom-call(f32[392,128]{1,0:T(8,128)S(1)} %collective-permute-done.2.far, f32[24,128]{1,0:T(8,128)S(1)} %get-tuple-element.35.table, ...), custom_call_target="tpu_custom_call", output_to_operand_aliasing={{0}: (5, {})} | custom-call | tf_op jit(solution)/shard_map/pallas_call | solution.py:449
Async XLA Ops:
  3.3 9.7 %collective-permute-start = (f32[520,128]{1,0:T(8,128)S(1)}, f32[520,128]{1,0:T(8,128)S(1)}, u32[]{:S(2)}, u32[]{:S(2)}) collective-permute-start(f32[520,128]{1,0:T(8,128)S(1)} %get-tuple-element.34), channel_id=1, source_target_pairs={{0,15},{1,2},{2,1},{3,4},{4,3},{5,6},{6,5},{7,8},{8,7},{9,10},{10,... | collective-permute-start | bytes 798728 | tf_op jit(solution)/shard_map/ppermute | solution.py:407
  8.8 1.5 %collective-permute-start.1 = (f32[512,128]{1,0:T(8,128)S(1)}, f32[512,128]{1,0:T(8,128)S(1)}, u32[]{:S(2)}, u32[]{:S(2)}) collective-permute-start(f32[512,128]{1,0:T(8,128)S(1)} %get-tuple-element.36), channel_id=1, source_target_pairs={{0,1},{1,0},{2,3},{3,2},{4,5},{5,4},{6,7},{7,6},{8,9},{9,8},{10,11... | collective-permute-start | bytes 786440 | tf_op jit(solution)/shard_map/ppermute | solution.py:408
  14.5 7.9 %collective-permute-start.2 = (f32[392,128]{1,0:T(8,128)S(1)}, f32[392,128]{1,0:T(8,128)S(1)}, u32[]{:S(2)}, u32[]{:S(2)}) collective-permute-start(f32[392,128]{1,0:T(8,128)S(1)} %get-tuple-element.50), channel_id=1, source_target_pairs={{0,15},{1,2},{2,1},{3,4},{4,3},{5,6},{6,5},{7,8},{8,7},{9,10},{10,... | collective-permute-start | bytes 602120 | tf_op jit(solution)/shard_map/ppermute | solution.py:435
  19.0 1.4 %collective-permute-start.3 = (f32[384,128]{1,0:T(8,128)S(1)}, f32[384,128]{1,0:T(8,128)S(1)}, u32[]{:S(2)}, u32[]{:S(2)}) collective-permute-start(f32[384,128]{1,0:T(8,128)S(1)} %get-tuple-element.51), channel_id=1, source_target_pairs={{0,1},{1,0},{2,3},{3,2},{4,5},{5,4},{6,7},{7,6},{8,9},{9,8},{10,11... | collective-permute-start | bytes 589832 | tf_op jit(solution)/shard_map/ppermute | solution.py:436

commit v6 on v5

--- a/solution.py
+++ b/solution.py
@@ -136,32 +136,40 @@
     return Band(h_ref, True), [Band(x_ref.at[level]) for level in range(3)]
 
 
-def before_send(h, xs, phase, table, sums, early, far, near):
+def before_far(h, xs, phase, table, sums, early, far, carry):
     x0, x1, _ = xs
     term = 3 * phase
     t = tile(h, x0, 2)
     scale = line(table, 6 + term)
     inner = {
         (2, 2): (t[0] + part(h, x0, 2, 1, 2)) * coefficient(term),
-        (3, 3): (t[3] + part(h, x0, 3, 4, 3)) * coefficient(term),
         (2, 3): t[1] * scale,
         (3, 2): t[2] * scale,
     }
     for (i, j), value in inner.items():
         x1.put(i, j, value)
+        early[EARLY.index((1, i, j))] = value
+    carry[...] = t[3]
     far[BS : 2 * BS, :] = inner[(2, 2)]
-    near[BS : 2 * BS, :] = inner[(3, 3)]
-    for index, (_, i, j) in enumerate(EARLY):
-        early[index] = inner[(i, j)]
-    for out, i, k in ((far, 2, 3), (near, 3, 2)):
-        value = part(h, x1, i, k, i)
-        out[2 * BS : 3 * BS, :] = value
-        sums[SUMS.index((2, i, i))] = value
+    value = part(h, x1, 2, 3, 2)
+    far[2 * BS : 3 * BS, :] = value
+    sums[SUMS.index((2, 2, 2))] = value
+
+
+def before_near(carry, h_ref, near_in, x_in, sums_in, early_in, near, x_ref, sums, early, *, phase):
+    h, (x0, x1, _) = views(h_ref, x_ref)
+    value = (carry[...] + part(h, x0, 3, 4, 3)) * coefficient(3 * phase)
+    x1.put(3, 3, value)
+    early[EARLY.index((1, 3, 3))] = value
+    near[BS : 2 * BS, :] = value
+    value = part(h, x1, 3, 2, 3)
+    near[2 * BS : 3 * BS, :] = value
+    sums[SUMS.index((2, 3, 3))] = value
 
 
 def own_first(
     re, im, ham, dip, pattern_in, field,
-    far, near, table, h_ref, x_ref, sums, early, re_in, im_in,
+    far, near, table, h_ref, x_ref, sums, early, carry, re_in, im_in,
     ham_in, dip_in, pattern, sems,
 ):
     copies = [
@@ -198,7 +206,7 @@
             xs[0].put(j, i, (real - imag).T)
         if i == j:
             (far if i == 2 else near)[0:BS, :] = real + imag
-    before_send(h, xs, 0, table, sums, early, far, near)
+    before_far(h, xs, 0, table, sums, early, far, carry)
 
 
 def own_rest(h, xs, phase, table, early, base, sums):
@@ -242,10 +250,14 @@
     put(2, b, b, (t[at_b] + slot(payload, 2)) * c[1])
     put(2, *up, t[1] * scales[1])
     put(2, *down, t[2] * scales[1])
-    t = tile(h, x2, low)
-    put(3, *up, t[1] * scales[2])
-    put(3, *down, t[2] * scales[2])
-    put(3, a, a, (t[at_a] + known(3, a, a)) * c[2])
+
+    def last():
+        t = tile(h, x2, low)
+        put(3, *up, t[1] * scales[2])
+        put(3, *down, t[2] * scales[2])
+        put(3, a, a, (t[at_a] + known(3, a, a)) * c[2])
+
+    return last
 
 
 def near_side(h, xs, near, phase, table, base, sums):
@@ -256,7 +268,7 @@
         values[(term + level - 1, i, j)] = value
 
     scales = [line(table, 12 + term + n) for n in range(3)]
-    side(h, xs, 3, 4, near, phase, scales, sums, record)
+    side(h, xs, 3, 4, near, phase, scales, sums, record)()
     x2 = xs[2]
     sums[SUMS.index((3, 2, 3))] = one_side(h, x2, 2, (2, 3), 3) + one_side(x2, h.minus, 2, (3, 3), 3)
     sums[SUMS.index((3, 3, 2))] = one_side(h, x2, 3, (3, 3), 2) + one_side(x2, h.minus, 3, (2, 3), 2)
@@ -264,14 +276,16 @@
     return values
 
 
-def far_side(h, xs, far, phase, table, sums, record):
+def far_side(h, xs, far, phase, table, sums, record, between=lambda: None):
     term = 3 * phase
     scales = [line(table, term + n) for n in range(3)]
-    side(h, xs, 2, 1, far, phase, scales, sums, record)
+    last = side(h, xs, 2, 1, far, phase, scales, sums, record)
     x2 = xs[2]
     scale = line(table, 6 + term + 2)
     record(3, 2, 3, (one_side(x2, h.minus, 2, (2, 2), 3) + sums[SUMS.index((3, 2, 3))]) * scale)
     record(3, 3, 2, (one_side(h, x2, 3, (2, 2), 2) + sums[SUMS.index((3, 3, 2))]) * scale)
+    between()
+    last()
 
 
 def rest_first(re_in, im_in, table, early, h_ref, x_in, sums_in, x_ref, sums, base):
@@ -290,7 +304,9 @@
     inner_state[...] = values[(2, 3, 3)]
 
 
-def far_first(far, table, inner_state, h_in, x_in, sums_in, h_ref, x_ref, sums, late, early, far_next, near_next):
+def far_first(
+    far, table, inner_state, h_in, x_in, sums_in, h_ref, x_ref, sums, late, early, far_next, near_next, carry
+):
     h, xs = views(h_ref, x_ref)
     h.put(1, 1, slot(far, 3))
     state = {}
@@ -306,7 +322,7 @@
         xs[0].put(i, j, value)
     far_next[0:BS, :] = state[(2, 2)]
     near_next[0:BS, :] = inner_state[...]
-    before_send(h, xs, 1, table, sums, early, far_next, near_next)
+    before_far(h, xs, 1, table, sums, early, far_next, carry)
 
 
 def rest_second(late, early, table, h_ref, x_in, sums_in, base_in, x_ref, sums, base):
@@ -323,29 +339,40 @@
 
 def far_second(far, table, sums, base, h_ref, x_in, x_ref, out_re, out_im, stage, sems):
     h, xs = views(h_ref, x_ref)
-    outs = (out_re, out_im)
-
-    def start(index, source):
-        row, offset = OWN[index][0]
+    copies = []
+    for index, ((row, offset), _) in enumerate(OWN):
         r, e = own_index(row, offset)
-        for a, out in enumerate(outs):
+        source = stage if index < 4 else base
+        for a, out in enumerate((out_re, out_im)):
             copies.append(pltpu.make_async_copy(source.at[index, a], out.at[r, e], sems.at[len(copies)]))
-            copies[-1].start()
-
-    copies = []
-    for index in (4, 5):
-        start(index, base)
+
+    def send(first):
+        for copy in copies[2 * first : 2 * first + 4]:
+            copy.start()
+
+    def apart(first):
+        pl.when(lax.axis_index("col") >= 0)(lambda: send(first))
+
+    apart(4)
     values = {}
 
     def record(level, i, j, value):
         values[(level + 2, i, j)] = value
 
-    far_side(h, xs, far, 1, table, sums, record)
-    for index in (2, 3, 0, 1):
+    def finish(index):
         i, j = OWN[index][1]
         real, imag = parts_of(values, i, j, [level + 2 for level in DONE_FAR[(i, j)]])
         stage[index, 0], stage[index, 1] = base[index, 0] + real, base[index, 1] + imag
-        start(index, stage)
+
+    def between():
+        finish(2)
+        finish(3)
+        apart(2)
+
+    far_side(h, xs, far, 1, table, sums, record, between)
+    finish(0)
+    finish(1)
+    send(0)
     for copy in copies:
         copy.wait()
 
@@ -385,10 +412,10 @@
     dma = pltpu.SemaphoreType.DMA
     h_out, x_out = vector(4, ROWS, BS, 3 * BS, dtype=bf16), vector(3, 2, ROWS, BS, 3 * BS, dtype=bf16)
     base_out, sums_out = vector(len(OWN), 2, BS, BS), vector(len(SUMS), BS, BS)
-    early_out, late_out = vector(len(EARLY), BS, BS), vector(len(LATE), BS, BS)
+    carry_out, early_out, late_out = vector(BS, BS), vector(len(EARLY), BS, BS), vector(len(LATE), BS, BS)
     out = (jax.ShapeDtypeStruct(whole, f32), BIG)
 
-    far, near, table, h, x, sums, early, re_in, im_in = call(
+    far, near, table, h, x, sums, early, carry, re_in, im_in = call(
         own_first,
         [BIG] * 5 + [SCALAR],
         [
@@ -399,12 +426,19 @@
             x_out,
             sums_out,
             early_out,
+            carry_out,
             vector(*whole),
             vector(*whole),
         ],
         [pltpu.VMEM(whole, f32)] * 2 + [pltpu.SMEM(pattern.shape, jnp.int32), dma((5,))],
     )(*inputs, field)
     far = lax.ppermute(far, RING, cross)
+    near, x, sums, early = call(
+        functools.partial(before_near, phase=0),
+        [VECTOR] * 6,
+        [vector(FIRST_ROWS, BS), x_out, sums_out, early_out],
+        aliases={2: 0, 3: 1, 4: 2, 5: 3},
+    )(carry, h, near, x, sums, early)
     near = lax.ppermute(near, RING, pair)
     x, sums, base = call(
         rest_first,
@@ -418,7 +452,7 @@
         [h_out, x_out, sums_out, base_out, vector(BS, BS)],
         aliases={2: 0, 3: 1, 4: 2, 5: 3},
     )(near, table, h, x, sums, base)
-    h, x, sums, late, early, far, near = call(
+    h, x, sums, late, early, far, near, carry = call(
         far_first,
         [VECTOR] * 6,
         [
@@ -429,10 +463,17 @@
             early_out,
             vector(SECOND_ROWS + MORE, BS),
             vector(SECOND_ROWS, BS),
+            carry_out,
         ],
         aliases={3: 0, 4: 1, 5: 2},
     )(far, table, inner_state, h, x, sums)
     far = lax.ppermute(far, RING, cross)
+    near, x, sums, early = call(
+        functools.partial(before_near, phase=1),
+        [VECTOR] * 6,
+        [vector(SECOND_ROWS, BS), x_out, sums_out, early_out],
+        aliases={2: 0, 3: 1, 4: 2, 5: 3},
+    )(carry, h, near, x, sums, early)
     near = lax.ppermute(near, RING, pair)
     x, sums, base = call(
         rest_second,

time: 24.6 us -> 24.4 us (level)
  waiting for transfers between devices: 4 us -> 3.32 us
  Pallas kernels: 9.07 us -> 9.38 us
    ppermute x2, waiting for transfers between devices: 2.48 us -> 1.83 us  [body(): far = lax.ppermute(far, RING, cross)]
    pallas_call x0 -> x2, Pallas kernels: none -> 0.51 us  [the longest x1 0.26 us: body(): call(functools.partial(before_near, phase=1), [VECTOR] * 6, [vector(SECON...]
  transfers between devices with their start and end apart: 4 -> 4, of which waited for: 4 -> 4; matrix products, arithmetic and copies ran while one was open for 0% -> 0% of each run, Pallas kernels for 15% -> 17%
where the time goes in v6:
time: 24.4 us; the launch traced here: 24.2 us
  starting transfers between devices  10.2 us (42%)
  Pallas kernels  9.38 us (38%)
  waiting for transfers between devices  3.32 us (14%)
  between operations  1.35 us (6%)
    ppermute x2, starting transfers between devices, body(): far = lax.ppermute(far, RING, cross)  10 us
    pallas_call x1, Pallas kernels, body(): call(own_first, [BIG] * 5 + [SCALAR], [vector(FIRST_ROWS + MORE, BS), vec...  1.98 us
    pallas_call x1, Pallas kernels, body(): call(far_second, [VECTOR] * 6, [x_out, out, out], [pltpu.VMEM((4, 2, BS,...  1.86 us
    ppermute x2, waiting for transfers between devices, body(): far = lax.ppermute(far, RING, cross)  1.83 us
    ppermute x2, waiting for transfers between devices, body(): near = lax.ppermute(near, RING, pair)  1.5 us
    pallas_call x1, Pallas kernels, body(): call(far_first, [VECTOR] * 6, [h_out, x_out, sums_out, late_out, early_ou...  1.44 us
    pallas_call x1, Pallas kernels, body(): call(near_first, [VECTOR] * 6, [h_out, x_out, sums_out, base_out, vector(...  1.08 us
    pallas_call x1, Pallas kernels, body(): call(near_second, [VECTOR] * 6, [x_out, sums_out, base_out], aliases={3:...  1.07 us
  transfers between devices with their start and end apart: 4, of which 4 were waited for; matrix products, arithmetic and copies ran while one was open for 0% of the time, Pallas kernels for 17%

profile of v6, /device:TPU:0, one launch (start us, length us, event | category | flops | bytes accessed | tf_op | source)
XLA Modules:
  0.0 24.2 jit_solution(10244338981862583553)
XLA Ops:
  1.3 2.0 %shard_map.77 = (f32[520,128]{1,0:T(8,128)S(1)}, f32[512,128]{1,0:T(8,128)S(1)}, f32[24,128]{1,0:T(8,128)S(1)}, bf16[4,6,128,384]{3,2,1,0:T(8,128)(2,1)S(1)}, bf...) custom-call(f32[2,3,128,128]{3,2,1,0:T(8,128)} %re.1, ...), custom_call_target="tpu_custom_call" | custom-call | tf_op jit(solution)/shard_map/pallas_call | solution.py:418
  3.3 5.5 %collective-permute-start = (f32[520,128]{1,0:T(8,128)S(1)}, f32[520,128]{1,0:T(8,128)S(1)}, u32[]{:S(2)}, u32[]{:S(2)}) collective-permute-start(f32[520,128]{1,0:T(8,128)S(1)} %get-tuple-element.44), channel_id=1, source_target_pairs={{0,15},{1,2},{2,1},{3,4},{4,3},{5,6},{6,5},{7,8},{8,7},{9,10},{10,... | collective-permute-start | bytes 798728 | tf_op jit(solution)/shard_map/ppermute | solution.py:435
  8.8 0.3 %shard_map.78 = (f32[512,128]{1,0:T(8,128)S(1)}, bf16[3,2,6,128,384]{4,3,2,1,0:T(8,128)(2,1)S(1)}, f32[10,128,128]{2,1,0:T(8,128)S(1)}, f32[4,128,128]{2,1,0:T(8,128)S(1)}) custom-call(f32[128,128]{1,0:T(8,128)S(1)} %get-tuple-element.46.carry, ...), custom_call_target="tpu_custom_call", output_to_operand_aliasing={{0}: (2, {}), {1}: (3, {}), {2}: (4, {}), {3}: (5, {})} | custom-call | tf_op jit(solution)/shard_map/pallas_call | solution.py:436
  9.0 0.1 collective-permute-start.1
  9.1 0.7 %shard_map.79 = (bf16[3,2,6,128,384]{4,3,2,1,0:T(8,128)(2,1)S(1)}, f32[10,128,128]{2,1,0:T(8,128)S(1)}, f32[6,2,128,128]{3,2,1,0:T(8,128)S(1)}) custom-call(f32[2,3,128,128]{3,2,1,0:T(8,128)S(1)} %get-tuple-element.53.re_in, f32[2,3,128,128]{3,2,1,0:T(8,128)S(1)} %get-tuple-element.54.im_in, ...), custom_call_target="tpu_custom_call", output_to_operand_aliasing={{0}: (5, {}), {1}: (6, {})} | custom-call | tf_op jit(solution)/shard_map/pallas_call | solution.py:443
  9.8 0.8 %collective-permute-done.1.near = f32[512,128]{1,0:T(8,128)S(1)} collective-permute-done((f32[512,128]{1,0:T(8,128)S(1)}, f32[512,128]{1,0:T(8,128)S(1)}, u32[]{:S(2)}, u32[]{:S(2)}) %collective-permute-start.1) | collective-permute-done | bytes 262176 | tf_op jit(solution)/shard_map/ppermute | solution.py:442
  10.6 1.1 %shard_map.80 = (bf16[4,6,128,384]{3,2,1,0:T(8,128)(2,1)S(1)}, bf16[3,2,6,128,384]{4,3,2,1,0:T(8,128)(2,1)S(1)}, f32[10,128,128]{2,1,0:T(8,128)S(1)}, f32[6,2,128,128]{3,2,1,0:T(8,128)S(1)}, f32[128,128]{1,0:T(8,128)S(1)}) custom-call(f32[512,128]{1,0:T(8,128)S(1)} %collective-permute-done.1., ...), custom_call_target="tpu_custom_call", output_to_operand_aliasing={{0}: (2, {}), {1}: (3, {}), {2}: (4, {}), {3}: (5, {})} | custom-call | tf_op jit(solution)/shard_map/pallas_call | solution.py:449
  11.7 1.3 %collective-permute-done.far = f32[520,128]{1,0:T(8,128)S(1)} collective-permute-done((f32[520,128]{1,0:T(8,128)S(1)}, f32[520,128]{1,0:T(8,128)S(1)}, u32[]{:S(2)}, u32[]{:S(2)}) %collective-permute-start) | collective-permute-done | bytes 266272 | tf_op jit(solution)/shard_map/ppermute | solution.py:435
  13.0 1.4 %shard_map.81 = (bf16[4,6,128,384]{3,2,1,0:T(8,128)(2,1)S(1)}, bf16[3,2,6,128,384]{4,3,2,1,0:T(8,128)(2,1)S(1)}, f32[10,128,128]{2,1,0:T(8,128)S(1)}, f32[10,128...) custom-call(f32[520,128]{1,0:T(8,128)S(1)} %collective-permute-done., ...), custom_call_target="tpu_custom_call", output_to_operand_aliasing={{0}: (3, {}), {1}: (4, {}), {2}: (5, {})} | custom-call | tf_op jit(solution)/shard_map/pallas_call | solution.py:455
  14.4 4.5 %collective-permute-start.2 = (f32[392,128]{1,0:T(8,128)S(1)}, f32[392,128]{1,0:T(8,128)S(1)}, u32[]{:S(2)}, u32[]{:S(2)}) collective-permute-start(f32[392,128]{1,0:T(8,128)S(1)} %get-tuple-element.65), channel_id=1, source_target_pairs={{0,15},{1,2},{2,1},{3,4},{4,3},{5,6},{6,5},{7,8},{8,7},{9,10},{10,... | collective-permute-start | bytes 602120 | tf_op jit(solution)/shard_map/ppermute | solution.py:470
  18.9 0.3 %shard_map.82 = (f32[384,128]{1,0:T(8,128)S(1)}, bf16[3,2,6,128,384]{4,3,2,1,0:T(8,128)(2,1)S(1)}, f32[10,128,128]{2,1,0:T(8,128)S(1)}, f32[4,128,128]{2,1,0:T(8,128)S(1)}) custom-call(f32[128,128]{1,0:T(8,128)S(1)} %get-tuple-element.66.carry, ...), custom_call_target="tpu_custom_call", output_to_operand_aliasing={{0}: (2, {}), {1}: (3, {}), {2}: (4, {}), {3}: (5, {})} | custom-call | tf_op jit(solution)/shard_map/pallas_call | solution.py:471
  19.2 0.1 collective-permute-start.3
  19.3 0.7 %shard_map.83 = (bf16[3,2,6,128,384]{4,3,2,1,0:T(8,128)(2,1)S(1)}, f32[10,128,128]{2,1,0:T(8,128)S(1)}, f32[6,2,128,128]{3,2,1,0:T(8,128)S(1)}) custom-call(f32[10,128,128]{2,1,0:T(8,128)S(1)} %get-tuple-element.73.late, f32[4,128,128]{2,1,0:T(8,128)S(1)} %get-tuple-element.74.early, ...), custom_call_target="tpu_custom_call", output_to_operand_aliasing={{0}: (4, {}), {1}: (5, {}), {2}: (6, {})} | custom-call | tf_op jit(solution)/shard_map/pallas_call | solution.py:478
  20.0 0.7 %collective-permute-done.3.near = f32[384,128]{1,0:T(8,128)S(1)} collective-permute-done((f32[384,128]{1,0:T(8,128)S(1)}, f32[384,128]{1,0:T(8,128)S(1)}, u32[]{:S(2)}, u32[]{:S(2)}) %collective-permute-start.3) | collective-permute-done | bytes 196640 | tf_op jit(solution)/shard_map/ppermute | solution.py:477
  20.7 1.1 %shard_map.84 = (bf16[3,2,6,128,384]{4,3,2,1,0:T(8,128)(2,1)S(1)}, f32[10,128,128]{2,1,0:T(8,128)S(1)}, f32[6,2,128,128]{3,2,1,0:T(8,128)S(1)}) custom-call(f32[384,128]{1,0:T(8,128)S(1)} %collective-permute-done.3.near, f32[24,128]{1,0:T(8,128)S(1)} %get-tuple-element.45.table, ...), custom_call_target="tpu_custom_call", output_to_operand_aliasing={{0}: (3, {}), {1}: (4, {}), {2}: (5, {})} | custom-call | tf_op jit(solution)/shard_map/pallas_call | solution.py:484
  21.8 0.6 %collective-permute-done.2.far = f32[392,128]{1,0:T(8,128)S(1)} collective-permute-done((f32[392,128]{1,0:T(8,128)S(1)}, f32[392,128]{1,0:T(8,128)S(1)}, u32[]{:S(2)}, u32[]{:S(2)}) %collective-permute-start.2) | collective-permute-done | bytes 200736 | tf_op jit(solution)/shard_map/ppermute | solution.py:470
  22.3 1.9 %shard_map.85 = (bf16[3,2,6,128,384]{4,3,2,1,0:T(8,128)(2,1)S(1)}, f32[2,3,128,128]{3,2,1,0:T(8,128)}, f32[2,3,128,128]{3,2,1,0:T(8,128)}) custom-call(f32[392,128]{1,0:T(8,128)S(1)} %collective-permute-done.2.far, f32[24,128]{1,0:T(8,128)S(1)} %get-tuple-element.45.table, ...), custom_call_target="tpu_custom_call", output_to_operand_aliasing={{0}: (5, {})} | custom-call | tf_op jit(solution)/shard_map/pallas_call | solution.py:490
Async XLA Ops:
  3.3 9.7 %collective-permute-start = (f32[520,128]{1,0:T(8,128)S(1)}, f32[520,128]{1,0:T(8,128)S(1)}, u32[]{:S(2)}, u32[]{:S(2)}) collective-permute-start(f32[520,128]{1,0:T(8,128)S(1)} %get-tuple-element.44), channel_id=1, source_target_pairs={{0,15},{1,2},{2,1},{3,4},{4,3},{5,6},{6,5},{7,8},{8,7},{9,10},{10,... | collective-permute-start | bytes 798728 | tf_op jit(solution)/shard_map/ppermute | solution.py:435
  9.0 1.6 %collective-permute-start.1 = (f32[512,128]{1,0:T(8,128)S(1)}, f32[512,128]{1,0:T(8,128)S(1)}, u32[]{:S(2)}, u32[]{:S(2)}) collective-permute-start(f32[512,128]{1,0:T(8,128)S(1)} %get-tuple-element.52), channel_id=1, source_target_pairs={{0,1},{1,0},{2,3},{3,2},{4,5},{5,4},{6,7},{7,6},{8,9},{9,8},{10,11... | collective-permute-start | bytes 786440 | tf_op jit(solution)/shard_map/ppermute | solution.py:442
  14.4 7.9 %collective-permute-start.2 = (f32[392,128]{1,0:T(8,128)S(1)}, f32[392,128]{1,0:T(8,128)S(1)}, u32[]{:S(2)}, u32[]{:S(2)}) collective-permute-start(f32[392,128]{1,0:T(8,128)S(1)} %get-tuple-element.65), channel_id=1, source_target_pairs={{0,15},{1,2},{2,1},{3,4},{4,3},{5,6},{6,5},{7,8},{8,7},{9,10},{10,... | collective-permute-start | bytes 602120 | tf_op jit(solution)/shard_map/ppermute | solution.py:470
  19.2 1.5 %collective-permute-start.3 = (f32[384,128]{1,0:T(8,128)S(1)}, f32[384,128]{1,0:T(8,128)S(1)}, u32[]{:S(2)}, u32[]{:S(2)}) collective-permute-start(f32[384,128]{1,0:T(8,128)S(1)} %get-tuple-element.72), channel_id=1, source_target_pairs={{0,1},{1,0},{2,3},{3,2},{4,5},{5,4},{6,7},{7,6},{8,9},{9,8},{10,11... | collective-permute-start | bytes 589832 | tf_op jit(solution)/shard_map/ppermute | solution.py:477

commit v7 on v6

--- a/solution.py
+++ b/solution.py
@@ -16,7 +16,7 @@
 ROWS = 6
 SIGN_RE = (1.0, -1.0, -1.0, 1.0, 1.0, -1.0)
 SIGN_IM = (-1.0, -1.0, 1.0, 1.0, -1.0, -1.0)
-FIRST_ROWS = 4 * BS
+FIRST_ROWS = 3 * BS + BS // 2 + 8
 SECOND_ROWS = 3 * BS
 MORE = 8
 TABLE_ROWS = 24
@@ -92,6 +92,35 @@
 
 def part(h, x, i, k, j):
     return piece(h, x, (i,), (k, k), (j, j))[0]
+
+
+def half_places():
+    shape = (BS // 2, BS)
+    return lax.broadcasted_iota(jnp.int32, shape, 0), lax.broadcasted_iota(jnp.int32, shape, 1)
+
+
+def swap_halves(rows):
+    return jnp.concatenate([rows[:, BS // 2 :], rows[:, : BS // 2]], axis=1)
+
+
+def put_symmetric(payload, block):
+    r, c = half_places()
+    turned = swap_halves(block[BS // 2 :])
+    first = 3 * BS
+    payload[first : first + BS // 2, :] = jnp.where(c < r, turned, block[: BS // 2])
+    payload[first + BS // 2 : first + BS // 2 + 1, :] = jnp.sum(jnp.where(c == r, turned, 0.0), axis=0, keepdims=True)
+
+
+def get_symmetric(payload):
+    r, c = half_places()
+    first = 3 * BS
+    rows = payload[first : first + BS // 2, :]
+    turned = jnp.concatenate([rows, rows], axis=0).T
+    upper = jnp.where(c < r, turned[: BS // 2], rows)
+    quarter = jnp.where(c < r, rows, turned[: BS // 2])
+    quarter = jnp.where(c == r, line(payload, first + BS // 2), quarter)
+    lower = jnp.where(c < BS // 2, turned[BS // 2 :], swap_halves(quarter))
+    return jnp.concatenate([upper, lower], axis=0)
 
 
 def coefficient(term):
@@ -196,7 +225,7 @@
         if j in (1, 4):
             h.put(j, i, value.T)
         if i == j:
-            (far if i == 2 else near)[3 * BS : 4 * BS, :] = value
+            put_symmetric(far if i == 2 else near, value)
     for copy in copies[3:]:
         copy.wait()
     for (row, offset), (i, j) in OWN:
@@ -252,10 +281,11 @@
     put(2, *down, t[2] * scales[1])
 
     def last():
-        t = tile(h, x2, low)
-        put(3, *up, t[1] * scales[2])
-        put(3, *down, t[2] * scales[2])
-        put(3, a, a, (t[at_a] + known(3, a, a)) * c[2])
+        row = piece(h, x2, (a,), (low, low + 1), (low, low + 1))[0]
+        here, there = (row[:, :BS], row[:, BS:]) if a == low else (row[:, BS:], row[:, :BS])
+        put(3, a, b, there * scales[2])
+        put(3, a, a, (here + known(3, a, a)) * c[2])
+        put(3, b, a, piece(h, x2, (b,), (low, low + 1), (a, a))[0] * scales[2])
 
     return last
 
@@ -297,7 +327,7 @@
 
 def near_first(near, table, h_in, x_in, sums_in, base_in, h_ref, x_ref, sums, base, inner_state):
     h, xs = views(h_ref, x_ref)
-    h.put(4, 4, slot(near, 3))
+    h.put(4, 4, get_symmetric(near))
     values = near_side(h, xs, near, 0, table, base, sums)
     for i, j in ((3, 3), (3, 4), (4, 3)):
         xs[0].put(i, j, values[(2, i, j)])
@@ -308,7 +338,7 @@
     far, table, inner_state, h_in, x_in, sums_in, h_ref, x_ref, sums, late, early, far_next, near_next, carry
 ):
     h, xs = views(h_ref, x_ref)
-    h.put(1, 1, slot(far, 3))
+    h.put(1, 1, get_symmetric(far))
     state = {}
 
     def record(level, i, j, value):

time: 24.4 us -> 24.2 us (level)
  waiting for transfers between devices: 3.32 us -> 2.94 us
  Pallas kernels: 9.38 us -> 9.7 us
    ppermute x2, waiting for transfers between devices: 1.83 us -> 1.49 us  [body(): far = lax.ppermute(far, RING, cross)]
  transfers between devices with their start and end apart: 4 -> 4, of which waited for: 4 -> 4; matrix products, arithmetic and copies ran while one was open for 0% -> 0% of each run, Pallas kernels for 17% -> 18%
where the time goes in v7:
time: 24.2 us; the launch traced here: 24 us
  starting transfers between devices  10 us (41%)
  Pallas kernels  9.7 us (40%)
  waiting for transfers between devices  2.94 us (12%)
  between operations  1.35 us (6%)
    ppermute x2, starting transfers between devices, body(): far = lax.ppermute(far, RING, cross)  9.9 us
    pallas_call x1, Pallas kernels, body(): call(own_first, [BIG] * 5 + [SCALAR], [vector(FIRST_ROWS + MORE, BS), vec...  1.98 us
    pallas_call x1, Pallas kernels, body(): call(far_second, [VECTOR] * 6, [x_out, out, out], [pltpu.VMEM((4, 2, BS,...  1.87 us
    pallas_call x1, Pallas kernels, body(): call(far_first, [VECTOR] * 6, [h_out, x_out, sums_out, late_out, early_ou...  1.57 us
    ppermute x2, waiting for transfers between devices, body(): far = lax.ppermute(far, RING, cross)  1.49 us
    ppermute x2, waiting for transfers between devices, body(): near = lax.ppermute(near, RING, pair)  1.45 us
    pallas_call x1, Pallas kernels, body(): call(near_first, [VECTOR] * 6, [h_out, x_out, sums_out, base_out, vector(...  1.23 us
    pallas_call x1, Pallas kernels, body(): call(near_second, [VECTOR] * 6, [x_out, sums_out, base_out], aliases={3:...  1.08 us
  transfers between devices with their start and end apart: 4, of which 4 were waited for; matrix products, arithmetic and copies ran while one was open for 0% of the time, Pallas kernels for 18%

profile of v7, /device:TPU:0, one launch (start us, length us, event | category | flops | bytes accessed | tf_op | source)
XLA Modules:
  0.0 24.0 jit_solution(13703262578255391575)
XLA Ops:
  1.3 2.0 %shard_map.77 = (f32[464,128]{1,0:T(8,128)S(1)}, f32[456,128]{1,0:T(8,128)S(1)}, f32[24,128]{1,0:T(8,128)S(1)}, bf16[4,6,128,384]{3,2,1,0:T(8,128)(2,1)S(1)}, bf...) custom-call(f32[2,3,128,128]{3,2,1,0:T(8,128)} %re.1, ...), custom_call_target="tpu_custom_call" | custom-call | tf_op jit(solution)/shard_map/pallas_call | solution.py:448
  3.3 5.5 %collective-permute-start = (f32[464,128]{1,0:T(8,128)S(1)}, f32[464,128]{1,0:T(8,128)S(1)}, u32[]{:S(2)}, u32[]{:S(2)}) collective-permute-start(f32[464,128]{1,0:T(8,128)S(1)} %get-tuple-element.44), channel_id=1, source_target_pairs={{0,15},{1,2},{2,1},{3,4},{4,3},{5,6},{6,5},{7,8},{8,7},{9,10},{10,... | collective-permute-start | bytes 712712 | tf_op jit(solution)/shard_map/ppermute | solution.py:465
  8.8 0.3 %shard_map.78 = (f32[456,128]{1,0:T(8,128)S(1)}, bf16[3,2,6,128,384]{4,3,2,1,0:T(8,128)(2,1)S(1)}, f32[10,128,128]{2,1,0:T(8,128)S(1)}, f32[4,128,128]{2,1,0:T(8,128)S(1)}) custom-call(f32[128,128]{1,0:T(8,128)S(1)} %get-tuple-element.46.carry, ...), custom_call_target="tpu_custom_call", output_to_operand_aliasing={{0}: (2, {}), {1}: (3, {}), {2}: (4, {}), {3}: (5, {})} | custom-call | tf_op jit(solution)/shard_map/pallas_call | solution.py:466
  9.0 0.1 collective-permute-start.1
  9.1 0.7 %shard_map.79 = (bf16[3,2,6,128,384]{4,3,2,1,0:T(8,128)(2,1)S(1)}, f32[10,128,128]{2,1,0:T(8,128)S(1)}, f32[6,2,128,128]{3,2,1,0:T(8,128)S(1)}) custom-call(f32[2,3,128,128]{3,2,1,0:T(8,128)S(1)} %get-tuple-element.53.re_in, f32[2,3,128,128]{3,2,1,0:T(8,128)S(1)} %get-tuple-element.54.im_in, ...), custom_call_target="tpu_custom_call", output_to_operand_aliasing={{0}: (5, {}), {1}: (6, {})} | custom-call | tf_op jit(solution)/shard_map/pallas_call | solution.py:473
  9.8 0.8 %collective-permute-done.1.near = f32[456,128]{1,0:T(8,128)S(1)} collective-permute-done((f32[456,128]{1,0:T(8,128)S(1)}, f32[456,128]{1,0:T(8,128)S(1)}, u32[]{:S(2)}, u32[]{:S(2)}) %collective-permute-start.1) | collective-permute-done | bytes 233504 | tf_op jit(solution)/shard_map/ppermute | solution.py:472
  10.6 1.2 %shard_map.80 = (bf16[4,6,128,384]{3,2,1,0:T(8,128)(2,1)S(1)}, bf16[3,2,6,128,384]{4,3,2,1,0:T(8,128)(2,1)S(1)}, f32[10,128,128]{2,1,0:T(8,128)S(1)}, f32[6,2,128,128]{3,2,1,0:T(8,128)S(1)}, f32[128,128]{1,0:T(8,128)S(1)}) custom-call(f32[456,128]{1,0:T(8,128)S(1)} %collective-permute-done.1., ...), custom_call_target="tpu_custom_call", output_to_operand_aliasing={{0}: (2, {}), {1}: (3, {}), {2}: (4, {}), {3}: (5, {})} | custom-call | tf_op jit(solution)/shard_map/pallas_call | solution.py:479
  11.8 0.8 %collective-permute-done.far = f32[464,128]{1,0:T(8,128)S(1)} collective-permute-done((f32[464,128]{1,0:T(8,128)S(1)}, f32[464,128]{1,0:T(8,128)S(1)}, u32[]{:S(2)}, u32[]{:S(2)}) %collective-permute-start) | collective-permute-done | bytes 237600 | tf_op jit(solution)/shard_map/ppermute | solution.py:465
  12.7 1.6 %shard_map.81 = (bf16[4,6,128,384]{3,2,1,0:T(8,128)(2,1)S(1)}, bf16[3,2,6,128,384]{4,3,2,1,0:T(8,128)(2,1)S(1)}, f32[10,128,128]{2,1,0:T(8,128)S(1)}, f32[10,128...) custom-call(f32[464,128]{1,0:T(8,128)S(1)} %collective-permute-done., ...), custom_call_target="tpu_custom_call", output_to_operand_aliasing={{0}: (3, {}), {1}: (4, {}), {2}: (5, {})} | custom-call | tf_op jit(solution)/shard_map/pallas_call | solution.py:485
  14.2 4.4 %collective-permute-start.2 = (f32[392,128]{1,0:T(8,128)S(1)}, f32[392,128]{1,0:T(8,128)S(1)}, u32[]{:S(2)}, u32[]{:S(2)}) collective-permute-start(f32[392,128]{1,0:T(8,128)S(1)} %get-tuple-element.65), channel_id=1, source_target_pairs={{0,15},{1,2},{2,1},{3,4},{4,3},{5,6},{6,5},{7,8},{8,7},{9,10},{10,... | collective-permute-start | bytes 602120 | tf_op jit(solution)/shard_map/ppermute | solution.py:500
  18.6 0.3 %shard_map.82 = (f32[384,128]{1,0:T(8,128)S(1)}, bf16[3,2,6,128,384]{4,3,2,1,0:T(8,128)(2,1)S(1)}, f32[10,128,128]{2,1,0:T(8,128)S(1)}, f32[4,128,128]{2,1,0:T(8,128)S(1)}) custom-call(f32[128,128]{1,0:T(8,128)S(1)} %get-tuple-element.66.carry, ...), custom_call_target="tpu_custom_call", output_to_operand_aliasing={{0}: (2, {}), {1}: (3, {}), {2}: (4, {}), {3}: (5, {})} | custom-call | tf_op jit(solution)/shard_map/pallas_call | solution.py:501
  18.9 0.1 collective-permute-start.3
  19.0 0.7 %shard_map.83 = (bf16[3,2,6,128,384]{4,3,2,1,0:T(8,128)(2,1)S(1)}, f32[10,128,128]{2,1,0:T(8,128)S(1)}, f32[6,2,128,128]{3,2,1,0:T(8,128)S(1)}) custom-call(f32[10,128,128]{2,1,0:T(8,128)S(1)} %get-tuple-element.73.late, f32[4,128,128]{2,1,0:T(8,128)S(1)} %get-tuple-element.74.early, ...), custom_call_target="tpu_custom_call", output_to_operand_aliasing={{0}: (4, {}), {1}: (5, {}), {2}: (6, {})} | custom-call | tf_op jit(solution)/shard_map/pallas_call | solution.py:508
  19.7 0.7 %collective-permute-done.3.near = f32[384,128]{1,0:T(8,128)S(1)} collective-permute-done((f32[384,128]{1,0:T(8,128)S(1)}, f32[384,128]{1,0:T(8,128)S(1)}, u32[]{:S(2)}, u32[]{:S(2)}) %collective-permute-start.3) | collective-permute-done | bytes 196640 | tf_op jit(solution)/shard_map/ppermute | solution.py:507
  20.4 1.1 %shard_map.84 = (bf16[3,2,6,128,384]{4,3,2,1,0:T(8,128)(2,1)S(1)}, f32[10,128,128]{2,1,0:T(8,128)S(1)}, f32[6,2,128,128]{3,2,1,0:T(8,128)S(1)}) custom-call(f32[384,128]{1,0:T(8,128)S(1)} %collective-permute-done.3.near, f32[24,128]{1,0:T(8,128)S(1)} %get-tuple-element.45.table, ...), custom_call_target="tpu_custom_call", output_to_operand_aliasing={{0}: (3, {}), {1}: (4, {}), {2}: (5, {})} | custom-call | tf_op jit(solution)/shard_map/pallas_call | solution.py:514
  21.5 0.6 %collective-permute-done.2.far = f32[392,128]{1,0:T(8,128)S(1)} collective-permute-done((f32[392,128]{1,0:T(8,128)S(1)}, f32[392,128]{1,0:T(8,128)S(1)}, u32[]{:S(2)}, u32[]{:S(2)}) %collective-permute-start.2) | collective-permute-done | bytes 200736 | tf_op jit(solution)/shard_map/ppermute | solution.py:500
  22.1 1.9 %shard_map.85 = (bf16[3,2,6,128,384]{4,3,2,1,0:T(8,128)(2,1)S(1)}, f32[2,3,128,128]{3,2,1,0:T(8,128)}, f32[2,3,128,128]{3,2,1,0:T(8,128)}) custom-call(f32[392,128]{1,0:T(8,128)S(1)} %collective-permute-done.2.far, f32[24,128]{1,0:T(8,128)S(1)} %get-tuple-element.45.table, ...), custom_call_target="tpu_custom_call", output_to_operand_aliasing={{0}: (5, {})} | custom-call | tf_op jit(solution)/shard_map/pallas_call | solution.py:520
Async XLA Ops:
  3.3 9.4 %collective-permute-start = (f32[464,128]{1,0:T(8,128)S(1)}, f32[464,128]{1,0:T(8,128)S(1)}, u32[]{:S(2)}, u32[]{:S(2)}) collective-permute-start(f32[464,128]{1,0:T(8,128)S(1)} %get-tuple-element.44), channel_id=1, source_target_pairs={{0,15},{1,2},{2,1},{3,4},{4,3},{5,6},{6,5},{7,8},{8,7},{9,10},{10,... | collective-permute-start | bytes 712712 | tf_op jit(solution)/shard_map/ppermute | solution.py:465
  9.0 1.6 %collective-permute-start.1 = (f32[456,128]{1,0:T(8,128)S(1)}, f32[456,128]{1,0:T(8,128)S(1)}, u32[]{:S(2)}, u32[]{:S(2)}) collective-permute-start(f32[456,128]{1,0:T(8,128)S(1)} %get-tuple-element.52), channel_id=1, source_target_pairs={{0,1},{1,0},{2,3},{3,2},{4,5},{5,4},{6,7},{7,6},{8,9},{9,8},{10,11... | collective-permute-start | bytes 700424 | tf_op jit(solution)/shard_map/ppermute | solution.py:472
  14.2 7.9 %collective-permute-start.2 = (f32[392,128]{1,0:T(8,128)S(1)}, f32[392,128]{1,0:T(8,128)S(1)}, u32[]{:S(2)}, u32[]{:S(2)}) collective-permute-start(f32[392,128]{1,0:T(8,128)S(1)} %get-tuple-element.65), channel_id=1, source_target_pairs={{0,15},{1,2},{2,1},{3,4},{4,3},{5,6},{6,5},{7,8},{8,7},{9,10},{10,... | collective-permute-start | bytes 602120 | tf_op jit(solution)/shard_map/ppermute | solution.py:500
  18.9 1.5 %collective-permute-start.3 = (f32[384,128]{1,0:T(8,128)S(1)}, f32[384,128]{1,0:T(8,128)S(1)}, u32[]{:S(2)}, u32[]{:S(2)}) collective-permute-start(f32[384,128]{1,0:T(8,128)S(1)} %get-tuple-element.72), channel_id=1, source_target_pairs={{0,1},{1,0},{2,3},{3,2},{4,5},{5,4},{6,7},{7,6},{8,9},{9,8},{10,11... | collective-permute-start | bytes 589832 | tf_op jit(solution)/shard_map/ppermute | solution.py:507

commit v8 on v7

--- a/solution.py
+++ b/solution.py
@@ -17,8 +17,10 @@
 SIGN_RE = (1.0, -1.0, -1.0, 1.0, 1.0, -1.0)
 SIGN_IM = (-1.0, -1.0, 1.0, 1.0, -1.0, -1.0)
 FIRST_ROWS = 3 * BS + BS // 2 + 8
-SECOND_ROWS = 3 * BS
+SECOND_ROWS = 2 * BS
 MORE = 8
+PART_ROWS = SECOND_ROWS + 2 * MORE
+FAR_PART_ROWS = SECOND_ROWS + 2 * MORE
 TABLE_ROWS = 24
 
 
@@ -179,20 +181,30 @@
         x1.put(i, j, value)
         early[EARLY.index((1, i, j))] = value
     carry[...] = t[3]
-    far[BS : 2 * BS, :] = inner[(2, 2)]
+    first = 1 - phase
+    far[first * BS : (first + 1) * BS, :] = inner[(2, 2)]
     value = part(h, x1, 2, 3, 2)
-    far[2 * BS : 3 * BS, :] = value
+    far[(first + 1) * BS : (first + 2) * BS, :] = value
     sums[SUMS.index((2, 2, 2))] = value
 
 
-def before_near(carry, h_ref, near_in, x_in, sums_in, early_in, near, x_ref, sums, early, *, phase):
+def before_near_first(carry, h_ref, near_in, x_in, sums_in, early_in, near, x_ref, sums, early):
+    before_near(carry, h_ref, x_ref, sums, early, near, 0)
+
+
+def before_near_second(carry, h_ref, x_in, sums_in, early_in, near, x_ref, sums, early):
+    before_near(carry, h_ref, x_ref, sums, early, near, 1)
+
+
+def before_near(carry, h_ref, x_ref, sums, early, near, phase):
     h, (x0, x1, _) = views(h_ref, x_ref)
+    first = 1 - phase
     value = (carry[...] + part(h, x0, 3, 4, 3)) * coefficient(3 * phase)
     x1.put(3, 3, value)
     early[EARLY.index((1, 3, 3))] = value
-    near[BS : 2 * BS, :] = value
+    near[first * BS : (first + 1) * BS, :] = value
     value = part(h, x1, 3, 2, 3)
-    near[2 * BS : 3 * BS, :] = value
+    near[(first + 1) * BS : (first + 2) * BS, :] = value
     sums[SUMS.index((2, 3, 3))] = value
 
 
@@ -255,7 +267,7 @@
     add_terms(base, values, DONE_EARLY, phase)
 
 
-def side(h, xs, a, b, payload, phase, scales, sums, record):
+def side(h, xs, a, b, start, payload, phase, scales, sums, record):
     x0, x1, x2 = xs
     c = [coefficient(3 * phase + n) for n in range(3)]
     low = min(a, b)
@@ -270,13 +282,14 @@
         if level < 3:
             xs[level].put(i, j, value)
 
-    x0.put(b, b, slot(payload, 0))
-    x1.put(b, b, slot(payload, 1))
+    first = 1 - phase
+    x0.put(b, b, start)
+    x1.put(b, b, slot(payload, first))
     put(1, a, b, (part(h, x0, a, b, b) + known(1, a, b)) * scales[0])
     put(1, b, a, (part(h, x0, b, b, a) + known(1, b, a)) * scales[0])
     t = tile(h, x1, low)
     put(2, a, a, (t[at_a] + known(2, a, a)) * c[1])
-    put(2, b, b, (t[at_b] + slot(payload, 2)) * c[1])
+    put(2, b, b, (t[at_b] + slot(payload, first + 1)) * c[1])
     put(2, *up, t[1] * scales[1])
     put(2, *down, t[2] * scales[1])
 
@@ -285,12 +298,18 @@
         here, there = (row[:, :BS], row[:, BS:]) if a == low else (row[:, BS:], row[:, :BS])
         put(3, a, b, there * scales[2])
         put(3, a, a, (here + known(3, a, a)) * c[2])
-        put(3, b, a, piece(h, x2, (b,), (low, low + 1), (a, a))[0] * scales[2])
+        if phase:
+            put(3, b, a, piece(h, x2, (b,), (low, low + 1), (a, a))[0] * scales[2])
+            return None
+        row = piece(h, x2, (b,), (low, low + 1), (low, low + 1))[0]
+        here, there = (row[:, :BS], row[:, BS:]) if b == low else (row[:, BS:], row[:, :BS])
+        put(3, b, a, there * scales[2])
+        return here
 
     return last
 
 
-def near_side(h, xs, near, phase, table, base, sums):
+def near_side(h, xs, start, near, phase, table, base, sums):
     term = 3 * phase
     values = {}
 
@@ -298,24 +317,24 @@
         values[(term + level - 1, i, j)] = value
 
     scales = [line(table, 12 + term + n) for n in range(3)]
-    side(h, xs, 3, 4, near, phase, scales, sums, record)()
+    own_part = side(h, xs, 3, 4, start, near, phase, scales, sums, record)()
     x2 = xs[2]
     sums[SUMS.index((3, 2, 3))] = one_side(h, x2, 2, (2, 3), 3) + one_side(x2, h.minus, 2, (3, 3), 3)
     sums[SUMS.index((3, 3, 2))] = one_side(h, x2, 3, (3, 3), 2) + one_side(x2, h.minus, 3, (2, 3), 2)
     add_terms(base, values, DONE_NEAR, phase)
-    return values
-
-
-def far_side(h, xs, far, phase, table, sums, record, between=lambda: None):
+    return values, own_part
+
+
+def far_side(h, xs, start, far, phase, table, sums, record, between=lambda: None):
     term = 3 * phase
     scales = [line(table, term + n) for n in range(3)]
-    last = side(h, xs, 2, 1, far, phase, scales, sums, record)
+    last = side(h, xs, 2, 1, start, far, phase, scales, sums, record)
     x2 = xs[2]
     scale = line(table, 6 + term + 2)
     record(3, 2, 3, (one_side(x2, h.minus, 2, (2, 2), 3) + sums[SUMS.index((3, 2, 3))]) * scale)
     record(3, 3, 2, (one_side(h, x2, 3, (2, 2), 2) + sums[SUMS.index((3, 3, 2))]) * scale)
     between()
-    last()
+    return last()
 
 
 def rest_first(re_in, im_in, table, early, h_ref, x_in, sums_in, x_ref, sums, base):
@@ -325,18 +344,21 @@
     own_rest(h, xs, 0, table, early, base, sums)
 
 
-def near_first(near, table, h_in, x_in, sums_in, base_in, h_ref, x_ref, sums, base, inner_state):
+def near_first(
+    near, table, h_in, x_in, sums_in, base_in, h_ref, x_ref, sums, base, own_part, part_far, part_near
+):
     h, xs = views(h_ref, x_ref)
     h.put(4, 4, get_symmetric(near))
-    values = near_side(h, xs, near, 0, table, base, sums)
+    values, own_part[...] = near_side(h, xs, slot(near, 0), near, 0, table, base, sums)
     for i, j in ((3, 3), (3, 4), (4, 3)):
         xs[0].put(i, j, values[(2, i, j)])
-    inner_state[...] = values[(2, 3, 3)]
-
-
-def far_first(
-    far, table, inner_state, h_in, x_in, sums_in, h_ref, x_ref, sums, late, early, far_next, near_next, carry
-):
+    part_far[0:BS, :] = sums[SUMS.index((3, 2, 2))]
+    part_far[BS:, :] = jnp.zeros((FAR_PART_ROWS - BS, BS), f32)
+    part_near[0:BS, :] = sums[SUMS.index((3, 3, 3))]
+    part_near[BS:, :] = jnp.zeros((PART_ROWS - BS, BS), f32)
+
+
+def far_first(far, table, h_in, x_in, sums_in, h_ref, x_ref, sums, late, early, far_next, own_part, carry):
     h, xs = views(h_ref, x_ref)
     h.put(1, 1, get_symmetric(far))
     state = {}
@@ -347,11 +369,9 @@
         if level == 3:
             state[(i, j)] = value
 
-    far_side(h, xs, far, 0, table, sums, record)
+    own_part[...] = far_side(h, xs, slot(far, 0), far, 0, table, sums, record)
     for (i, j), value in state.items():
         xs[0].put(i, j, value)
-    far_next[0:BS, :] = state[(2, 2)]
-    near_next[0:BS, :] = inner_state[...]
     before_far(h, xs, 1, table, sums, early, far_next, carry)
 
 
@@ -362,12 +382,13 @@
     own_rest(h, xs, 1, table, early, base, sums)
 
 
-def near_second(near, table, h_ref, x_in, sums_in, base_in, x_ref, sums, base):
-    h, xs = views(h_ref, x_ref)
-    near_side(h, xs, near, 1, table, base, sums)
-
-
-def far_second(far, table, sums, base, h_ref, x_in, x_ref, out_re, out_im, stage, sems):
+def near_second(near, own_part, part_near, table, h_ref, x_in, sums_in, base_in, x_ref, sums, base):
+    h, xs = views(h_ref, x_ref)
+    start = (own_part[...] + part_near[0:BS, :]) * coefficient(2)
+    near_side(h, xs, start, near, 1, table, base, sums)
+
+
+def far_second(far, own_part, part_far, table, sums, base, h_ref, x_in, x_ref, out_re, out_im, stage, sems):
     h, xs = views(h_ref, x_ref)
     copies = []
     for index, ((row, offset), _) in enumerate(OWN):
@@ -399,7 +420,8 @@
         finish(3)
         apart(2)
 
-    far_side(h, xs, far, 1, table, sums, record, between)
+    start = (own_part[...] + part_far[0:BS, :]) * coefficient(2)
+    far_side(h, xs, start, far, 1, table, sums, record, between)
     finish(0)
     finish(1)
     send(0)
@@ -449,7 +471,7 @@
         own_first,
         [BIG] * 5 + [SCALAR],
         [
-            vector(FIRST_ROWS + MORE, BS),
+            vector(FIRST_ROWS + 2 * MORE, BS),
             vector(FIRST_ROWS, BS),
             vector(TABLE_ROWS, BS),
             h_out,
@@ -464,7 +486,7 @@
     )(*inputs, field)
     far = lax.ppermute(far, RING, cross)
     near, x, sums, early = call(
-        functools.partial(before_near, phase=0),
+        before_near_first,
         [VECTOR] * 6,
         [vector(FIRST_ROWS, BS), x_out, sums_out, early_out],
         aliases={2: 0, 3: 1, 4: 2, 5: 3},
@@ -476,15 +498,17 @@
         [x_out, sums_out, base_out],
         aliases={5: 0, 6: 1},
     )(re_in, im_in, table, early, h, x, sums)
-    h, x, sums, base, inner_state = call(
+    h, x, sums, base, own_near, part_far, part_near = call(
         near_first,
         [VECTOR] * 6,
-        [h_out, x_out, sums_out, base_out, vector(BS, BS)],
+        [h_out, x_out, sums_out, base_out, carry_out, vector(FAR_PART_ROWS, BS), vector(PART_ROWS, BS)],
         aliases={2: 0, 3: 1, 4: 2, 5: 3},
     )(near, table, h, x, sums, base)
-    h, x, sums, late, early, far, near, carry = call(
+    part_far = lax.ppermute(part_far, RING, cross)
+    part_near = lax.ppermute(part_near, RING, pair)
+    h, x, sums, late, early, far, own_far, carry = call(
         far_first,
-        [VECTOR] * 6,
+        [VECTOR] * 5,
         [
             h_out,
             x_out,
@@ -492,18 +516,18 @@
             late_out,
             early_out,
             vector(SECOND_ROWS + MORE, BS),
-            vector(SECOND_ROWS, BS),
+            carry_out,
             carry_out,
         ],
-        aliases={3: 0, 4: 1, 5: 2},
-    )(far, table, inner_state, h, x, sums)
+        aliases={2: 0, 3: 1, 4: 2},
+    )(far, table, h, x, sums)
     far = lax.ppermute(far, RING, cross)
     near, x, sums, early = call(
-        functools.partial(before_near, phase=1),
-        [VECTOR] * 6,
+        before_near_second,
+        [VECTOR] * 5,
         [vector(SECOND_ROWS, BS), x_out, sums_out, early_out],
-        aliases={2: 0, 3: 1, 4: 2, 5: 3},
-    )(carry, h, near, x, sums, early)
+        aliases={2: 1, 3: 2, 4: 3},
+    )(carry, h, x, sums, early)
     near = lax.ppermute(near, RING, pair)
     x, sums, base = call(
         rest_second,
@@ -513,17 +537,17 @@
     )(late, early, table, h, x, sums, base)
     x, sums, base = call(
         near_second,
-        [VECTOR] * 6,
+        [VECTOR] * 8,
         [x_out, sums_out, base_out],
-        aliases={3: 0, 4: 1, 5: 2},
-    )(near, table, h, x, sums, base)
+        aliases={5: 0, 6: 1, 7: 2},
+    )(near, own_near, part_near, table, h, x, sums, base)
     _, out_re, out_im = call(
         far_second,
-        [VECTOR] * 6,
+        [VECTOR] * 8,
         [x_out, out, out],
         [pltpu.VMEM((4, 2, BS, BS), f32), dma((12,))],
-        aliases={5: 0},
-    )(far, table, sums, base, h, x)
+        aliases={7: 0},
+    )(far, own_far, part_far, table, sums, base, h, x)
     return out_re, out_im
 
 

time: 24.2 us -> 23.7 us (0.979)
  waiting for transfers between devices: 2.94 us -> 1.53 us
  starting transfers between devices: 10 us -> 10.9 us
    ppermute x2, waiting for transfers between devices: 1.49 us -> 0.17 us  [body(): far = lax.ppermute(far, RING, cross)]
    ppermute x0 -> x2, starting transfers between devices: none -> 0.76 us  [the longest x1 0.55 us: body(): part_far = lax.ppermute(part_far, RING, cross)]
  transfers between devices with their start and end apart: 4 -> 6, of which waited for: 4 -> 3; matrix products, arithmetic and copies ran while one was open for 0% -> 0% of each run, Pallas kernels for 18% -> 25%
where the time goes in v8:
time: 23.7 us; the launch traced here: 23.5 us
  starting transfers between devices  10.9 us (46%)
  Pallas kernels  9.67 us (41%)
  waiting for transfers between devices  1.53 us (6%)
  between operations  1.36 us (6%)
    ppermute x2, starting transfers between devices, body(): far = lax.ppermute(far, RING, cross)  10 us
    pallas_call x1, Pallas kernels, body(): call(own_first, [BIG] * 5 + [SCALAR], [vector(FIRST_ROWS + 2 * MORE, BS),...  1.98 us
    pallas_call x1, Pallas kernels, body(): call(far_second, [VECTOR] * 8, [x_out, out, out], [pltpu.VMEM((4, 2, BS,...  1.85 us
    pallas_call x1, Pallas kernels, body(): call(far_first, [VECTOR] * 5, [h_out, x_out, sums_out, late_out, early_ou...  1.58 us
    ppermute x2, waiting for transfers between devices, body(): near = lax.ppermute(near, RING, pair)  1.35 us
    pallas_call x1, Pallas kernels, body(): call(near_first, [VECTOR] * 6, [h_out, x_out, sums_out, base_out, carry_o...  1.22 us
    pallas_call x1, Pallas kernels, body(): call(near_second, [VECTOR] * 8, [x_out, sums_out, base_out], aliases={5:...  1.09 us
    pallas_call x1, Pallas kernels, body(): call(rest_second, [VECTOR] * 7, [x_out, sums_out, base_out], aliases={4:...  0.74 us
  transfers between devices with their start and end apart: 6, of which 3 were waited for; matrix products, arithmetic and copies ran while one was open for 0% of the time, Pallas kernels for 25%

profile of v8, /device:TPU:0, one launch (start us, length us, event | category | flops | bytes accessed | tf_op | source)
XLA Modules:
  0.0 23.5 jit_solution(12869802070539881034)
XLA Ops:
  1.3 2.0 %shard_map.77 = (f32[472,128]{1,0:T(8,128)S(1)}, f32[456,128]{1,0:T(8,128)S(1)}, f32[24,128]{1,0:T(8,128)S(1)}, bf16[4,6,128,384]{3,2,1,0:T(8,128)(2,1)S(1)}, bf...) custom-call(f32[2,3,128,128]{3,2,1,0:T(8,128)} %re.1, ...), custom_call_target="tpu_custom_call" | custom-call | tf_op jit(solution)/shard_map/pallas_call | solution.py:470
  3.3 5.5 %collective-permute-start = (f32[472,128]{1,0:T(8,128)S(1)}, f32[472,128]{1,0:T(8,128)S(1)}, u32[]{:S(2)}, u32[]{:S(2)}) collective-permute-start(f32[472,128]{1,0:T(8,128)S(1)} %get-tuple-element.46), channel_id=1, source_target_pairs={{0,15},{1,2},{2,1},{3,4},{4,3},{5,6},{6,5},{7,8},{8,7},{9,10},{10,... | collective-permute-start | bytes 725000 | tf_op jit(solution)/shard_map/ppermute | solution.py:487
  8.8 0.3 %shard_map.78 = (f32[456,128]{1,0:T(8,128)S(1)}, bf16[3,2,6,128,384]{4,3,2,1,0:T(8,128)(2,1)S(1)}, f32[10,128,128]{2,1,0:T(8,128)S(1)}, f32[4,128,128]{2,1,0:T(8,128)S(1)}) custom-call(f32[128,128]{1,0:T(8,128)S(1)} %get-tuple-element.48.carry, ...), custom_call_target="tpu_custom_call", output_to_operand_aliasing={{0}: (2, {}), {1}: (3, {}), {2}: (4, {}), {3}: (5, {})} | custom-call | tf_op jit(solution)/shard_map/pallas_call | solution.py:488
  9.0 0.1 collective-permute-start.1
  9.1 0.7 %shard_map.79 = (bf16[3,2,6,128,384]{4,3,2,1,0:T(8,128)(2,1)S(1)}, f32[10,128,128]{2,1,0:T(8,128)S(1)}, f32[6,2,128,128]{3,2,1,0:T(8,128)S(1)}) custom-call(f32[2,3,128,128]{3,2,1,0:T(8,128)S(1)} %get-tuple-element.55.re_in, f32[2,3,128,128]{3,2,1,0:T(8,128)S(1)} %get-tuple-element.56.im_in, ...), custom_call_target="tpu_custom_call", output_to_operand_aliasing={{0}: (5, {}), {1}: (6, {})} | custom-call | tf_op jit(solution)/shard_map/pallas_call | solution.py:495
  9.8 0.8 %collective-permute-done.1.near = f32[456,128]{1,0:T(8,128)S(1)} collective-permute-done((f32[456,128]{1,0:T(8,128)S(1)}, f32[456,128]{1,0:T(8,128)S(1)}, u32[]{:S(2)}, u32[]{:S(2)}) %collective-permute-start.1) | collective-permute-done | bytes 233504 | tf_op jit(solution)/shard_map/ppermute | solution.py:494
  10.6 1.2 %shard_map.80 = (bf16[4,6,128,384]{3,2,1,0:T(8,128)(2,1)S(1)}, bf16[3,2,6,128,384]{4,3,2,1,0:T(8,128)(2,1)S(1)}, f32[10,128,128]{2,1,0:T(8,128)S(1)}, f32[6,2,12...) custom-call(f32[456,128]{1,0:T(8,128)S(1)} %collective-permute-done., ...), custom_call_target="tpu_custom_call", output_to_operand_aliasing={{0}: (2, {}), {1}: (3, {}), {2}: (4, {}), {3}: (5, {})} | custom-call | tf_op jit(solution)/shard_map/pallas_call | solution.py:501
  11.8 0.2 collective-permute-start.5
  12.0 0.6 %collective-permute-start.3 = (f32[272,128]{1,0:T(8,128)S(1)}, f32[272,128]{1,0:T(8,128)S(1)}, u32[]{:S(2)}, u32[]{:S(2)}) collective-permute-start(f32[272,128]{1,0:T(8,128)S(1)} %get-tuple-element.68), channel_id=1, source_target_pairs={{0,15},{1,2},{2,1},{3,4},{4,3},{5,6},{6,5},{7,8},{8,7},{9,10},{10,... | collective-permute-start | bytes 417800 | tf_op jit(solution)/shard_map/ppermute | solution.py:507
  12.6 0.1 collective-permute-done.far
  12.7 1.6 %shard_map.81 = (bf16[4,6,128,384]{3,2,1,0:T(8,128)(2,1)S(1)}, bf16[3,2,6,128,384]{4,3,2,1,0:T(8,128)(2,1)S(1)}, f32[10,128,128]{2,1,0:T(8,128)S(1)}, f32[10,128...) custom-call(f32[472,128]{1,0:T(8,128)S(1)} %collective-permute-done., ...), custom_call_target="tpu_custom_call", output_to_operand_aliasing={{0}: (2, {}), {1}: (3, {}), {2}: (4, {})} | custom-call | tf_op jit(solution)/shard_map/pallas_call | solution.py:509
  14.3 4.5 %collective-permute-start.2 = (f32[264,128]{1,0:T(8,128)S(1)}, f32[264,128]{1,0:T(8,128)S(1)}, u32[]{:S(2)}, u32[]{:S(2)}) collective-permute-start(f32[264,128]{1,0:T(8,128)S(1)} %get-tuple-element.66), channel_id=1, source_target_pairs={{0,15},{1,2},{2,1},{3,4},{4,3},{5,6},{6,5},{7,8},{8,7},{9,10},{10,... | collective-permute-start | bytes 405512 | tf_op jit(solution)/shard_map/ppermute | solution.py:524
  18.8 0.3 %shard_map.82 = (f32[256,128]{1,0:T(8,128)S(1)}, bf16[3,2,6,128,384]{4,3,2,1,0:T(8,128)(2,1)S(1)}, f32[10,128,128]{2,1,0:T(8,128)S(1)}, f32[4,128,128]{2,1,0:T(8,128)S(1)}) custom-call(f32[128,128]{1,0:T(8,128)S(1)} %get-tuple-element.69.carry, ...), custom_call_target="tpu_custom_call", output_to_operand_aliasing={{1}: (2, {}), {2}: (3, {}), {3}: (4, {})} | custom-call | tf_op jit(solution)/shard_map/pallas_call | solution.py:525
  19.1 0.1 collective-permute-start.4
  19.1 0.7 %shard_map.83 = (bf16[3,2,6,128,384]{4,3,2,1,0:T(8,128)(2,1)S(1)}, f32[10,128,128]{2,1,0:T(8,128)S(1)}, f32[6,2,128,128]{3,2,1,0:T(8,128)S(1)}) custom-call(f32[10,128,128]{2,1,0:T(8,128)S(1)} %get-tuple-element.77.late, f32[4,128,128]{2,1,0:T(8,128)S(1)} %get-tuple-element.78.early, ...), custom_call_target="tpu_custom_call", output_to_operand_aliasing={{0}: (4, {}), {1}: (5, {}), {2}: (6, {})} | custom-call | tf_op jit(solution)/shard_map/pallas_call | solution.py:532
  19.9 0.6 %collective-permute-done.4.near = f32[256,128]{1,0:T(8,128)S(1)} collective-permute-done((f32[256,128]{1,0:T(8,128)S(1)}, f32[256,128]{1,0:T(8,128)S(1)}, u32[]{:S(2)}, u32[]{:S(2)}) %collective-permute-start.4) | collective-permute-done | bytes 131104 | tf_op jit(solution)/shard_map/ppermute | solution.py:531
  20.5 0.0 collective-permute-done.5.part_near
  20.5 1.1 %shard_map.84 = (bf16[3,2,6,128,384]{4,3,2,1,0:T(8,128)(2,1)S(1)}, f32[10,128,128]{2,1,0:T(8,128)S(1)}, f32[6,2,128,128]{3,2,1,0:T(8,128)S(1)}) custom-call(f32[256,128]{1,0:T(8,128)S(1)} %collective-permute-done.4.near, f32[128,128]{1,0:T(8,128)S(1)} %get-tuple-element.75.own_part, ...), custom_call_target="tpu_custom_call", output_to_operand_aliasing={{0}: (5, {}), {1}: (6, {}), {2}: (7, {})} | custom-call | tf_op jit(solution)/shard_map/pallas_call | solution.py:538
  21.6 0.0 collective-permute-done.3.part_far
  21.6 0.0 collective-permute-done.2.far
  21.6 1.8 %shard_map.85 = (bf16[3,2,6,128,384]{4,3,2,1,0:T(8,128)(2,1)S(1)}, f32[2,3,128,128]{3,2,1,0:T(8,128)}, f32[2,3,128,128]{3,2,1,0:T(8,128)}) custom-call(f32[264,128]{1,0:T(8,128)S(1)} %collective-permute-done.2.far, f32[128,128]{1,0:T(8,128)S(1)} %get-tuple-element.67.own_part, ...), custom_call_target="tpu_custom_call", output_to_operand_aliasing={{0}: (7, {})} | custom-call | tf_op jit(solution)/shard_map/pallas_call | solution.py:544
Async XLA Ops:
  3.3 9.5 %collective-permute-start = (f32[472,128]{1,0:T(8,128)S(1)}, f32[472,128]{1,0:T(8,128)S(1)}, u32[]{:S(2)}, u32[]{:S(2)}) collective-permute-start(f32[472,128]{1,0:T(8,128)S(1)} %get-tuple-element.46), channel_id=1, source_target_pairs={{0,15},{1,2},{2,1},{3,4},{4,3},{5,6},{6,5},{7,8},{8,7},{9,10},{10,... | collective-permute-start | bytes 725000 | tf_op jit(solution)/shard_map/ppermute | solution.py:487
  9.0 1.6 %collective-permute-start.1 = (f32[456,128]{1,0:T(8,128)S(1)}, f32[456,128]{1,0:T(8,128)S(1)}, u32[]{:S(2)}, u32[]{:S(2)}) collective-permute-start(f32[456,128]{1,0:T(8,128)S(1)} %get-tuple-element.54), channel_id=1, source_target_pairs={{0,1},{1,0},{2,3},{3,2},{4,5},{5,4},{6,7},{7,6},{8,9},{9,8},{10,11... | collective-permute-start | bytes 700424 | tf_op jit(solution)/shard_map/ppermute | solution.py:494
  11.8 8.7 %collective-permute-start.5 = (f32[272,128]{1,0:T(8,128)S(1)}, f32[272,128]{1,0:T(8,128)S(1)}, u32[]{:S(2)}, u32[]{:S(2)}) collective-permute-start(f32[272,128]{1,0:T(8,128)S(1)} %get-tuple-element.76), channel_id=1, source_target_pairs={{0,1},{1,0},{2,3},{3,2},{4,5},{5,4},{6,7},{7,6},{8,9},{9,8},{10,11... | collective-permute-start | bytes 417800 | tf_op jit(solution)/shard_map/ppermute | solution.py:508
  12.0 9.6 %collective-permute-start.3 = (f32[272,128]{1,0:T(8,128)S(1)}, f32[272,128]{1,0:T(8,128)S(1)}, u32[]{:S(2)}, u32[]{:S(2)}) collective-permute-start(f32[272,128]{1,0:T(8,128)S(1)} %get-tuple-element.68), channel_id=1, source_target_pairs={{0,15},{1,2},{2,1},{3,4},{4,3},{5,6},{6,5},{7,8},{8,7},{9,10},{10,... | collective-permute-start | bytes 417800 | tf_op jit(solution)/shard_map/ppermute | solution.py:507
  14.3 7.3 %collective-permute-start.2 = (f32[264,128]{1,0:T(8,128)S(1)}, f32[264,128]{1,0:T(8,128)S(1)}, u32[]{:S(2)}, u32[]{:S(2)}) collective-permute-start(f32[264,128]{1,0:T(8,128)S(1)} %get-tuple-element.66), channel_id=1, source_target_pairs={{0,15},{1,2},{2,1},{3,4},{4,3},{5,6},{6,5},{7,8},{8,7},{9,10},{10,... | collective-permute-start | bytes 405512 | tf_op jit(solution)/shard_map/ppermute | solution.py:524
  19.1 1.4 %collective-permute-start.4 = (f32[256,128]{1,0:T(8,128)S(1)}, f32[256,128]{1,0:T(8,128)S(1)}, u32[]{:S(2)}, u32[]{:S(2)}) collective-permute-start(f32[256,128]{1,0:T(8,128)S(1)} %get-tuple-element.74), channel_id=1, source_target_pairs={{0,1},{1,0},{2,3},{3,2},{4,5},{5,4},{6,7},{7,6},{8,9},{9,8},{10,11... | collective-permute-start | bytes 393224 | tf_op jit(solution)/shard_map/ppermute | solution.py:531

commit v9 on v8

--- a/solution.py
+++ b/solution.py
@@ -21,7 +21,8 @@
 MORE = 8
 PART_ROWS = SECOND_ROWS + 2 * MORE
 FAR_PART_ROWS = SECOND_ROWS + 2 * MORE
-TABLE_ROWS = 24
+TABLE_ROWS = 32
+TABLE_FIELD = 24
 
 
 def own_index(row, offset):
@@ -188,7 +189,19 @@
     sums[SUMS.index((2, 2, 2))] = value
 
 
-def before_near_first(carry, h_ref, near_in, x_in, sums_in, early_in, near, x_ref, sums, early):
+def before_near_first(
+    carry, table, re_in, im_in, ham_in, dip_in, h_in, x_in, sums_in, early_in, h_ref, near, x_ref, sums, early
+):
+    h, xs = views(h_ref, x_ref)
+    f = line(table, TABLE_FIELD)
+    put_symmetric(near, own(ham_in, 1, 0) + f * own(dip_in, 1, 0))
+    near[0:BS, :] = own(re_in, 1, 0) + own(im_in, 1, 0)
+    value = own(ham_in, 1, 1) + f * own(dip_in, 1, 1)
+    h.put(3, 4, value)
+    h.put(4, 3, value.T)
+    real, imag = own(re_in, 1, 1), own(im_in, 1, 1)
+    xs[0].put(3, 4, real + imag)
+    xs[0].put(4, 3, (real - imag).T)
     before_near(carry, h_ref, x_ref, sums, early, near, 0)
 
 
@@ -210,8 +223,8 @@
 
 def own_first(
     re, im, ham, dip, pattern_in, field,
-    far, near, table, h_ref, x_ref, sums, early, carry, re_in, im_in,
-    ham_in, dip_in, pattern, sems,
+    far, table, h_ref, x_ref, sums, early, carry, re_in, im_in, ham_in, dip_in,
+    pattern, sems,
 ):
     copies = [
         pltpu.make_async_copy(source, target, sems.at[n])
@@ -228,25 +241,26 @@
             table[6 * n + term : 6 * n + term + 1, :] = jnp.full(
                 (1, BS), pattern[e, r, term].astype(f32) * coefficient(term), f32
             )
+    table[TABLE_FIELD : TABLE_FIELD + 1, :] = jnp.full((1, BS), field[0], f32)
     h, xs = views(h_ref, x_ref)
     for copy in copies[1:3]:
         copy.wait()
-    for (row, offset), (i, j) in OWN:
+    for (row, offset), (i, j) in OWN[:5]:
         value = own(ham_in, row, offset) + field[0] * own(dip_in, row, offset)
         h.put(i, j, value)
-        if j in (1, 4):
+        if j == 1:
             h.put(j, i, value.T)
-        if i == j:
-            put_symmetric(far if i == 2 else near, value)
+        if (i, j) == (2, 2):
+            put_symmetric(far, value)
     for copy in copies[3:]:
         copy.wait()
-    for (row, offset), (i, j) in OWN:
+    for (row, offset), (i, j) in OWN[:5]:
         real, imag = own(re_in, row, offset), own(im_in, row, offset)
         xs[0].put(i, j, real + imag)
-        if j in (1, 4):
+        if j == 1:
             xs[0].put(j, i, (real - imag).T)
-        if i == j:
-            (far if i == 2 else near)[0:BS, :] = real + imag
+        if (i, j) == (2, 2):
+            far[0:BS, :] = real + imag
     before_far(h, xs, 0, table, sums, early, far, carry)
 
 
@@ -467,30 +481,28 @@
     carry_out, early_out, late_out = vector(BS, BS), vector(len(EARLY), BS, BS), vector(len(LATE), BS, BS)
     out = (jax.ShapeDtypeStruct(whole, f32), BIG)
 
-    far, near, table, h, x, sums, early, carry, re_in, im_in = call(
+    far, table, h, x, sums, early, carry, re_in, im_in, ham_in, dip_in = call(
         own_first,
         [BIG] * 5 + [SCALAR],
         [
             vector(FIRST_ROWS + 2 * MORE, BS),
-            vector(FIRST_ROWS, BS),
             vector(TABLE_ROWS, BS),
             h_out,
             x_out,
             sums_out,
             early_out,
             carry_out,
-            vector(*whole),
-            vector(*whole),
-        ],
-        [pltpu.VMEM(whole, f32)] * 2 + [pltpu.SMEM(pattern.shape, jnp.int32), dma((5,))],
+        ]
+        + [vector(*whole)] * 4,
+        [pltpu.SMEM(pattern.shape, jnp.int32), dma((5,))],
     )(*inputs, field)
     far = lax.ppermute(far, RING, cross)
-    near, x, sums, early = call(
+    h, near, x, sums, early = call(
         before_near_first,
-        [VECTOR] * 6,
-        [vector(FIRST_ROWS, BS), x_out, sums_out, early_out],
-        aliases={2: 0, 3: 1, 4: 2, 5: 3},
-    )(carry, h, near, x, sums, early)
+        [VECTOR] * 10,
+        [h_out, vector(FIRST_ROWS, BS), x_out, sums_out, early_out],
+        aliases={6: 0, 7: 2, 8: 3, 9: 4},
+    )(carry, table, re_in, im_in, ham_in, dip_in, h, x, sums, early)
     near = lax.ppermute(near, RING, pair)
     x, sums, base = call(
         rest_first,

time: 23.7 us -> 23.7 us (level)
  transfers between devices with their start and end apart: 6 -> 6, of which waited for: 3 -> 2; matrix products, arithmetic and copies ran while one was open for 0% -> 0% of each run, Pallas kernels for 25% -> 26%
where the time goes in v9:
time: 23.7 us; the launch traced here: 23.5 us
  starting transfers between devices  10.9 us (46%)
  Pallas kernels  9.86 us (42%)
  waiting for transfers between devices  1.38 us (6%)
  between operations  1.36 us (6%)
    ppermute x2, starting transfers between devices, body(): far = lax.ppermute(far, RING, cross)  10 us
    pallas_call x1, Pallas kernels, body(): call(own_first, [BIG] * 5 + [SCALAR], [vector(FIRST_ROWS + 2 * MORE, BS),...  1.97 us
    pallas_call x1, Pallas kernels, body(): call(far_second, [VECTOR] * 8, [x_out, out, out], [pltpu.VMEM((4, 2, BS,...  1.87 us
    pallas_call x1, Pallas kernels, body(): call(far_first, [VECTOR] * 5, [h_out, x_out, sums_out, late_out, early_ou...  1.61 us
    ppermute x2, waiting for transfers between devices, body(): near = lax.ppermute(near, RING, pair)  1.33 us
    pallas_call x1, Pallas kernels, body(): call(near_first, [VECTOR] * 6, [h_out, x_out, sums_out, base_out, carry_o...  1.22 us
    pallas_call x1, Pallas kernels, body(): call(near_second, [VECTOR] * 8, [x_out, sums_out, base_out], aliases={5:...  1.08 us
    pallas_call x1, Pallas kernels, body(): call(rest_second, [VECTOR] * 7, [x_out, sums_out, base_out], aliases={4:...  0.75 us
  transfers between devices with their start and end apart: 6, of which 2 were waited for; matrix products, arithmetic and copies ran while one was open for 0% of the time, Pallas kernels for 26%

profile of v9, /device:TPU:0, one launch (start us, length us, event | category | flops | bytes accessed | tf_op | source)
XLA Modules:
  0.0 23.5 jit_solution(8016438974899575893)
XLA Ops:
  1.3 2.0 %shard_map.77 = (f32[472,128]{1,0:T(8,128)S(1)}, f32[32,128]{1,0:T(8,128)S(1)}, bf16[4,6,128,384]{3,2,1,0:T(8,128)(2,1)S(1)}, bf16[3,2,6,128,384]{4,3,2,1,0:T(8,...) custom-call(f32[2,3,128,128]{3,2,1,0:T(8,128)} %re.1, ...), custom_call_target="tpu_custom_call" | custom-call | tf_op jit(solution)/shard_map/pallas_call | solution.py:484
  3.3 5.5 %collective-permute-start = (f32[472,128]{1,0:T(8,128)S(1)}, f32[472,128]{1,0:T(8,128)S(1)}, u32[]{:S(2)}, u32[]{:S(2)}) collective-permute-start(f32[472,128]{1,0:T(8,128)S(1)} %get-tuple-element.48), channel_id=1, source_target_pairs={{0,15},{1,2},{2,1},{3,4},{4,3},{5,6},{6,5},{7,8},{8,7},{9,10},{10,... | collective-permute-start | bytes 725000 | tf_op jit(solution)/shard_map/ppermute | solution.py:499
  8.8 0.4 %shard_map.78 = (bf16[4,6,128,384]{3,2,1,0:T(8,128)(2,1)S(1)}, f32[456,128]{1,0:T(8,128)S(1)}, bf16[3,2,6,128,384]{4,3,2,1,0:T(8,128)(2,1)S(1)}, f32[10,128,128]{2,1,0:T(8,128)S(1)}, f32[4,128,128]{2,1,0:T(8,128)S(1)}) custom-call(f32[128,128]{1,0:T(8,128)S(1)} %get-tuple-element.50.carry, ...), custom_call_target="tpu_custom_call", output_to_operand_aliasing={{0}: (6, {}), {2}: (7, {}), {3}: (8, {}), {4}: (9, {})} | custom-call | tf_op jit(solution)/shard_map/pallas_call | solution.py:500
  9.1 0.1 collective-permute-start.1
  9.2 0.7 %shard_map.79 = (bf16[3,2,6,128,384]{4,3,2,1,0:T(8,128)(2,1)S(1)}, f32[10,128,128]{2,1,0:T(8,128)S(1)}, f32[6,2,128,128]{3,2,1,0:T(8,128)S(1)}) custom-call(f32[2,3,128,128]{3,2,1,0:T(8,128)S(1)} %get-tuple-element.51.re_in, f32[2,3,128,128]{3,2,1,0:T(8,128)S(1)} %get-tuple-element.52.im_in, ...), custom_call_target="tpu_custom_call", output_to_operand_aliasing={{0}: (5, {}), {1}: (6, {})} | custom-call | tf_op jit(solution)/shard_map/pallas_call | solution.py:507
  10.0 0.8 %collective-permute-done.1.near = f32[456,128]{1,0:T(8,128)S(1)} collective-permute-done((f32[456,128]{1,0:T(8,128)S(1)}, f32[456,128]{1,0:T(8,128)S(1)}, u32[]{:S(2)}, u32[]{:S(2)}) %collective-permute-start.1) | collective-permute-done | bytes 233504 | tf_op jit(solution)/shard_map/ppermute | solution.py:506
  10.7 1.2 %shard_map.80 = (bf16[4,6,128,384]{3,2,1,0:T(8,128)(2,1)S(1)}, bf16[3,2,6,128,384]{4,3,2,1,0:T(8,128)(2,1)S(1)}, f32[10,128,128]{2,1,0:T(8,128)S(1)}, f32[6,2,12...) custom-call(f32[456,128]{1,0:T(8,128)S(1)} %collective-permute-done., ...), custom_call_target="tpu_custom_call", output_to_operand_aliasing={{0}: (2, {}), {1}: (3, {}), {2}: (4, {}), {3}: (5, {})} | custom-call | tf_op jit(solution)/shard_map/pallas_call | solution.py:513
  11.9 0.2 collective-permute-start.5
  12.1 0.6 %collective-permute-start.3 = (f32[272,128]{1,0:T(8,128)S(1)}, f32[272,128]{1,0:T(8,128)S(1)}, u32[]{:S(2)}, u32[]{:S(2)}) collective-permute-start(f32[272,128]{1,0:T(8,128)S(1)} %get-tuple-element.72), channel_id=1, source_target_pairs={{0,15},{1,2},{2,1},{3,4},{4,3},{5,6},{6,5},{7,8},{8,7},{9,10},{10,... | collective-permute-start | bytes 417800 | tf_op jit(solution)/shard_map/ppermute | solution.py:519
  12.7 0.0 collective-permute-done.far
  12.7 1.6 %shard_map.81 = (bf16[4,6,128,384]{3,2,1,0:T(8,128)(2,1)S(1)}, bf16[3,2,6,128,384]{4,3,2,1,0:T(8,128)(2,1)S(1)}, f32[10,128,128]{2,1,0:T(8,128)S(1)}, f32[10,128...) custom-call(f32[472,128]{1,0:T(8,128)S(1)} %collective-permute-done., ...), custom_call_target="tpu_custom_call", output_to_operand_aliasing={{0}: (2, {}), {1}: (3, {}), {2}: (4, {})} | custom-call | tf_op jit(solution)/shard_map/pallas_call | solution.py:521
  14.3 4.5 %collective-permute-start.2 = (f32[264,128]{1,0:T(8,128)S(1)}, f32[264,128]{1,0:T(8,128)S(1)}, u32[]{:S(2)}, u32[]{:S(2)}) collective-permute-start(f32[264,128]{1,0:T(8,128)S(1)} %get-tuple-element.70), channel_id=1, source_target_pairs={{0,15},{1,2},{2,1},{3,4},{4,3},{5,6},{6,5},{7,8},{8,7},{9,10},{10,... | collective-permute-start | bytes 405512 | tf_op jit(solution)/shard_map/ppermute | solution.py:536
  18.8 0.3 %shard_map.82 = (f32[256,128]{1,0:T(8,128)S(1)}, bf16[3,2,6,128,384]{4,3,2,1,0:T(8,128)(2,1)S(1)}, f32[10,128,128]{2,1,0:T(8,128)S(1)}, f32[4,128,128]{2,1,0:T(8,128)S(1)}) custom-call(f32[128,128]{1,0:T(8,128)S(1)} %get-tuple-element.73.carry, ...), custom_call_target="tpu_custom_call", output_to_operand_aliasing={{1}: (2, {}), {2}: (3, {}), {3}: (4, {})} | custom-call | tf_op jit(solution)/shard_map/pallas_call | solution.py:537
  19.1 0.1 collective-permute-start.4
  19.2 0.8 %shard_map.83 = (bf16[3,2,6,128,384]{4,3,2,1,0:T(8,128)(2,1)S(1)}, f32[10,128,128]{2,1,0:T(8,128)S(1)}, f32[6,2,128,128]{3,2,1,0:T(8,128)S(1)}) custom-call(f32[10,128,128]{2,1,0:T(8,128)S(1)} %get-tuple-element.81.late, f32[4,128,128]{2,1,0:T(8,128)S(1)} %get-tuple-element.82.early, ...), custom_call_target="tpu_custom_call", output_to_operand_aliasing={{0}: (4, {}), {1}: (5, {}), {2}: (6, {})} | custom-call | tf_op jit(solution)/shard_map/pallas_call | solution.py:544
  19.9 0.6 %collective-permute-done.4.near = f32[256,128]{1,0:T(8,128)S(1)} collective-permute-done((f32[256,128]{1,0:T(8,128)S(1)}, f32[256,128]{1,0:T(8,128)S(1)}, u32[]{:S(2)}, u32[]{:S(2)}) %collective-permute-start.4) | collective-permute-done | bytes 131104 | tf_op jit(solution)/shard_map/ppermute | solution.py:543
  20.5 0.0 collective-permute-done.5.part_near
  20.5 1.1 %shard_map.84 = (bf16[3,2,6,128,384]{4,3,2,1,0:T(8,128)(2,1)S(1)}, f32[10,128,128]{2,1,0:T(8,128)S(1)}, f32[6,2,128,128]{3,2,1,0:T(8,128)S(1)}) custom-call(f32[256,128]{1,0:T(8,128)S(1)} %collective-permute-done.4.near, f32[128,128]{1,0:T(8,128)S(1)} %get-tuple-element.79.own_part, ...), custom_call_target="tpu_custom_call", output_to_operand_aliasing={{0}: (5, {}), {1}: (6, {}), {2}: (7, {})} | custom-call | tf_op jit(solution)/shard_map/pallas_call | solution.py:550
  21.6 0.0 collective-permute-done.3.part_far
  21.6 0.0 collective-permute-done.2.far
  21.6 1.9 %shard_map.85 = (bf16[3,2,6,128,384]{4,3,2,1,0:T(8,128)(2,1)S(1)}, f32[2,3,128,128]{3,2,1,0:T(8,128)}, f32[2,3,128,128]{3,2,1,0:T(8,128)}) custom-call(f32[264,128]{1,0:T(8,128)S(1)} %collective-permute-done.2.far, f32[128,128]{1,0:T(8,128)S(1)} %get-tuple-element.71.own_part, ...), custom_call_target="tpu_custom_call", output_to_operand_aliasing={{0}: (7, {})} | custom-call | tf_op jit(solution)/shard_map/pallas_call | solution.py:556
Async XLA Ops:
  3.3 9.5 %collective-permute-start = (f32[472,128]{1,0:T(8,128)S(1)}, f32[472,128]{1,0:T(8,128)S(1)}, u32[]{:S(2)}, u32[]{:S(2)}) collective-permute-start(f32[472,128]{1,0:T(8,128)S(1)} %get-tuple-element.48), channel_id=1, source_target_pairs={{0,15},{1,2},{2,1},{3,4},{4,3},{5,6},{6,5},{7,8},{8,7},{9,10},{10,... | collective-permute-start | bytes 725000 | tf_op jit(solution)/shard_map/ppermute | solution.py:499
  9.1 1.6 %collective-permute-start.1 = (f32[456,128]{1,0:T(8,128)S(1)}, f32[456,128]{1,0:T(8,128)S(1)}, u32[]{:S(2)}, u32[]{:S(2)}) collective-permute-start(f32[456,128]{1,0:T(8,128)S(1)} %get-tuple-element.59), channel_id=1, source_target_pairs={{0,1},{1,0},{2,3},{3,2},{4,5},{5,4},{6,7},{7,6},{8,9},{9,8},{10,11... | collective-permute-start | bytes 700424 | tf_op jit(solution)/shard_map/ppermute | solution.py:506
  11.9 8.6 %collective-permute-start.5 = (f32[272,128]{1,0:T(8,128)S(1)}, f32[272,128]{1,0:T(8,128)S(1)}, u32[]{:S(2)}, u32[]{:S(2)}) collective-permute-start(f32[272,128]{1,0:T(8,128)S(1)} %get-tuple-element.80), channel_id=1, source_target_pairs={{0,1},{1,0},{2,3},{3,2},{4,5},{5,4},{6,7},{7,6},{8,9},{9,8},{10,11... | collective-permute-start | bytes 417800 | tf_op jit(solution)/shard_map/ppermute | solution.py:520
  12.1 9.5 %collective-permute-start.3 = (f32[272,128]{1,0:T(8,128)S(1)}, f32[272,128]{1,0:T(8,128)S(1)}, u32[]{:S(2)}, u32[]{:S(2)}) collective-permute-start(f32[272,128]{1,0:T(8,128)S(1)} %get-tuple-element.72), channel_id=1, source_target_pairs={{0,15},{1,2},{2,1},{3,4},{4,3},{5,6},{6,5},{7,8},{8,7},{9,10},{10,... | collective-permute-start | bytes 417800 | tf_op jit(solution)/shard_map/ppermute | solution.py:519
  14.3 7.3 %collective-permute-start.2 = (f32[264,128]{1,0:T(8,128)S(1)}, f32[264,128]{1,0:T(8,128)S(1)}, u32[]{:S(2)}, u32[]{:S(2)}) collective-permute-start(f32[264,128]{1,0:T(8,128)S(1)} %get-tuple-element.70), channel_id=1, source_target_pairs={{0,15},{1,2},{2,1},{3,4},{4,3},{5,6},{6,5},{7,8},{8,7},{9,10},{10,... | collective-permute-start | bytes 405512 | tf_op jit(solution)/shard_map/ppermute | solution.py:536
  19.1 1.4 %collective-permute-start.4 = (f32[256,128]{1,0:T(8,128)S(1)}, f32[256,128]{1,0:T(8,128)S(1)}, u32[]{:S(2)}, u32[]{:S(2)}) collective-permute-start(f32[256,128]{1,0:T(8,128)S(1)} %get-tuple-element.78), channel_id=1, source_target_pairs={{0,1},{1,0},{2,3},{3,2},{4,5},{5,4},{6,7},{7,6},{8,9},{9,8},{10,11... | collective-permute-start | bytes 393224 | tf_op jit(solution)/shard_map/ppermute | solution.py:543

commit v10 on v8

--- a/solution.py
+++ b/solution.py
@@ -267,7 +267,7 @@
     add_terms(base, values, DONE_EARLY, phase)
 
 
-def side(h, xs, a, b, start, payload, phase, scales, sums, record):
+def side(h, xs, a, b, start, payload, phase, scales, sums, record, place=lambda: None):
     x0, x1, x2 = xs
     c = [coefficient(3 * phase + n) for n in range(3)]
     low = min(a, b)
@@ -285,8 +285,10 @@
     first = 1 - phase
     x0.put(b, b, start)
     x1.put(b, b, slot(payload, first))
-    put(1, a, b, (part(h, x0, a, b, b) + known(1, a, b)) * scales[0])
-    put(1, b, a, (part(h, x0, b, b, a) + known(1, b, a)) * scales[0])
+    row, col = one_side(h, x0, a, (b, b), b), one_side(x0, h.minus, b, (b, b), a)
+    place()
+    put(1, a, b, (row + one_side(x0, h.minus, a, (b, b), b) + known(1, a, b)) * scales[0])
+    put(1, b, a, (col + one_side(h, x0, b, (b, b), a) + known(1, b, a)) * scales[0])
     t = tile(h, x1, low)
     put(2, a, a, (t[at_a] + known(2, a, a)) * c[1])
     put(2, b, b, (t[at_b] + slot(payload, first + 1)) * c[1])
@@ -325,10 +327,10 @@
     return values, own_part
 
 
-def far_side(h, xs, start, far, phase, table, sums, record, between=lambda: None):
+def far_side(h, xs, start, far, phase, table, sums, record, between=lambda: None, place=lambda: None):
     term = 3 * phase
     scales = [line(table, term + n) for n in range(3)]
-    last = side(h, xs, 2, 1, start, far, phase, scales, sums, record)
+    last = side(h, xs, 2, 1, start, far, phase, scales, sums, record, place)
     x2 = xs[2]
     scale = line(table, 6 + term + 2)
     record(3, 2, 3, (one_side(x2, h.minus, 2, (2, 2), 3) + sums[SUMS.index((3, 2, 3))]) * scale)
@@ -360,7 +362,6 @@
 
 def far_first(far, table, h_in, x_in, sums_in, h_ref, x_ref, sums, late, early, far_next, own_part, carry):
     h, xs = views(h_ref, x_ref)
-    h.put(1, 1, get_symmetric(far))
     state = {}
 
     def record(level, i, j, value):
@@ -369,7 +370,9 @@
         if level == 3:
             state[(i, j)] = value
 
-    own_part[...] = far_side(h, xs, slot(far, 0), far, 0, table, sums, record)
+    own_part[...] = far_side(
+        h, xs, slot(far, 0), far, 0, table, sums, record, place=lambda: h.put(1, 1, get_symmetric(far))
+    )
     for (i, j), value in state.items():
         xs[0].put(i, j, value)
     before_far(h, xs, 1, table, sums, early, far_next, carry)

time: 23.7 us -> 23.7 us (level)
  no operation moved by 1% of the time
where the time goes in v10:
time: 23.7 us; the launch traced here: 23.5 us
  starting transfers between devices  10.9 us (46%)
  Pallas kernels  9.67 us (41%)
  waiting for transfers between devices  1.53 us (6%)
  between operations  1.36 us (6%)
    ppermute x2, starting transfers between devices, body(): far = lax.ppermute(far, RING, cross)  10 us
    pallas_call x1, Pallas kernels, body(): call(own_first, [BIG] * 5 + [SCALAR], [vector(FIRST_ROWS + 2 * MORE, BS),...  1.98 us
    pallas_call x1, Pallas kernels, body(): call(far_second, [VECTOR] * 8, [x_out, out, out], [pltpu.VMEM((4, 2, BS,...  1.85 us
    pallas_call x1, Pallas kernels, body(): call(far_first, [VECTOR] * 5, [h_out, x_out, sums_out, late_out, early_ou...  1.58 us
    ppermute x2, waiting for transfers between devices, body(): near = lax.ppermute(near, RING, pair)  1.36 us
    pallas_call x1, Pallas kernels, body(): call(near_first, [VECTOR] * 6, [h_out, x_out, sums_out, base_out, carry_o...  1.21 us
    pallas_call x1, Pallas kernels, body(): call(near_second, [VECTOR] * 8, [x_out, sums_out, base_out], aliases={5:...  1.09 us
    pallas_call x1, Pallas kernels, body(): call(rest_second, [VECTOR] * 7, [x_out, sums_out, base_out], aliases={4:...  0.73 us
  transfers between devices with their start and end apart: 6, of which 3 were waited for; matrix products, arithmetic and copies ran while one was open for 0% of the time, Pallas kernels for 25%

profile of v10, /device:TPU:0, one launch (start us, length us, event | category | flops | bytes accessed | tf_op | source)
XLA Modules:
  0.0 23.5 jit_solution(16001425411626912886)
XLA Ops:
  1.3 2.0 %shard_map.77 = (f32[472,128]{1,0:T(8,128)S(1)}, f32[456,128]{1,0:T(8,128)S(1)}, f32[24,128]{1,0:T(8,128)S(1)}, bf16[4,6,128,384]{3,2,1,0:T(8,128)(2,1)S(1)}, bf...) custom-call(f32[2,3,128,128]{3,2,1,0:T(8,128)} %re.1, ...), custom_call_target="tpu_custom_call" | custom-call | tf_op jit(solution)/shard_map/pallas_call | solution.py:473
  3.3 5.5 %collective-permute-start = (f32[472,128]{1,0:T(8,128)S(1)}, f32[472,128]{1,0:T(8,128)S(1)}, u32[]{:S(2)}, u32[]{:S(2)}) collective-permute-start(f32[472,128]{1,0:T(8,128)S(1)} %get-tuple-element.46), channel_id=1, source_target_pairs={{0,15},{1,2},{2,1},{3,4},{4,3},{5,6},{6,5},{7,8},{8,7},{9,10},{10,... | collective-permute-start | bytes 725000 | tf_op jit(solution)/shard_map/ppermute | solution.py:490
  8.8 0.3 %shard_map.78 = (f32[456,128]{1,0:T(8,128)S(1)}, bf16[3,2,6,128,384]{4,3,2,1,0:T(8,128)(2,1)S(1)}, f32[10,128,128]{2,1,0:T(8,128)S(1)}, f32[4,128,128]{2,1,0:T(8,128)S(1)}) custom-call(f32[128,128]{1,0:T(8,128)S(1)} %get-tuple-element.48.carry, ...), custom_call_target="tpu_custom_call", output_to_operand_aliasing={{0}: (2, {}), {1}: (3, {}), {2}: (4, {}), {3}: (5, {})} | custom-call | tf_op jit(solution)/shard_map/pallas_call | solution.py:491
  9.0 0.1 collective-permute-start.1
  9.1 0.7 %shard_map.79 = (bf16[3,2,6,128,384]{4,3,2,1,0:T(8,128)(2,1)S(1)}, f32[10,128,128]{2,1,0:T(8,128)S(1)}, f32[6,2,128,128]{3,2,1,0:T(8,128)S(1)}) custom-call(f32[2,3,128,128]{3,2,1,0:T(8,128)S(1)} %get-tuple-element.55.re_in, f32[2,3,128,128]{3,2,1,0:T(8,128)S(1)} %get-tuple-element.56.im_in, ...), custom_call_target="tpu_custom_call", output_to_operand_aliasing={{0}: (5, {}), {1}: (6, {})} | custom-call | tf_op jit(solution)/shard_map/pallas_call | solution.py:498
  9.8 0.8 %collective-permute-done.1.near = f32[456,128]{1,0:T(8,128)S(1)} collective-permute-done((f32[456,128]{1,0:T(8,128)S(1)}, f32[456,128]{1,0:T(8,128)S(1)}, u32[]{:S(2)}, u32[]{:S(2)}) %collective-permute-start.1) | collective-permute-done | bytes 233504 | tf_op jit(solution)/shard_map/ppermute | solution.py:497
  10.6 1.2 %shard_map.80 = (bf16[4,6,128,384]{3,2,1,0:T(8,128)(2,1)S(1)}, bf16[3,2,6,128,384]{4,3,2,1,0:T(8,128)(2,1)S(1)}, f32[10,128,128]{2,1,0:T(8,128)S(1)}, f32[6,2,12...) custom-call(f32[456,128]{1,0:T(8,128)S(1)} %collective-permute-done., ...), custom_call_target="tpu_custom_call", output_to_operand_aliasing={{0}: (2, {}), {1}: (3, {}), {2}: (4, {}), {3}: (5, {})} | custom-call | tf_op jit(solution)/shard_map/pallas_call | solution.py:504
  11.8 0.2 collective-permute-start.5
  12.0 0.6 %collective-permute-start.3 = (f32[272,128]{1,0:T(8,128)S(1)}, f32[272,128]{1,0:T(8,128)S(1)}, u32[]{:S(2)}, u32[]{:S(2)}) collective-permute-start(f32[272,128]{1,0:T(8,128)S(1)} %get-tuple-element.68), channel_id=1, source_target_pairs={{0,15},{1,2},{2,1},{3,4},{4,3},{5,6},{6,5},{7,8},{8,7},{9,10},{10,... | collective-permute-start | bytes 417800 | tf_op jit(solution)/shard_map/ppermute | solution.py:510
  12.6 0.1 collective-permute-done.far
  12.7 1.6 %shard_map.81 = (bf16[4,6,128,384]{3,2,1,0:T(8,128)(2,1)S(1)}, bf16[3,2,6,128,384]{4,3,2,1,0:T(8,128)(2,1)S(1)}, f32[10,128,128]{2,1,0:T(8,128)S(1)}, f32[10,128...) custom-call(f32[472,128]{1,0:T(8,128)S(1)} %collective-permute-done., ...), custom_call_target="tpu_custom_call", output_to_operand_aliasing={{0}: (2, {}), {1}: (3, {}), {2}: (4, {})} | custom-call | tf_op jit(solution)/shard_map/pallas_call | solution.py:512
  14.3 4.5 %collective-permute-start.2 = (f32[264,128]{1,0:T(8,128)S(1)}, f32[264,128]{1,0:T(8,128)S(1)}, u32[]{:S(2)}, u32[]{:S(2)}) collective-permute-start(f32[264,128]{1,0:T(8,128)S(1)} %get-tuple-element.66), channel_id=1, source_target_pairs={{0,15},{1,2},{2,1},{3,4},{4,3},{5,6},{6,5},{7,8},{8,7},{9,10},{10,... | collective-permute-start | bytes 405512 | tf_op jit(solution)/shard_map/ppermute | solution.py:527
  18.8 0.3 %shard_map.82 = (f32[256,128]{1,0:T(8,128)S(1)}, bf16[3,2,6,128,384]{4,3,2,1,0:T(8,128)(2,1)S(1)}, f32[10,128,128]{2,1,0:T(8,128)S(1)}, f32[4,128,128]{2,1,0:T(8,128)S(1)}) custom-call(f32[128,128]{1,0:T(8,128)S(1)} %get-tuple-element.69.carry, ...), custom_call_target="tpu_custom_call", output_to_operand_aliasing={{1}: (2, {}), {2}: (3, {}), {3}: (4, {})} | custom-call | tf_op jit(solution)/shard_map/pallas_call | solution.py:528
  19.1 0.1 collective-permute-start.4
  19.1 0.7 %shard_map.83 = (bf16[3,2,6,128,384]{4,3,2,1,0:T(8,128)(2,1)S(1)}, f32[10,128,128]{2,1,0:T(8,128)S(1)}, f32[6,2,128,128]{3,2,1,0:T(8,128)S(1)}) custom-call(f32[10,128,128]{2,1,0:T(8,128)S(1)} %get-tuple-element.77.late, f32[4,128,128]{2,1,0:T(8,128)S(1)} %get-tuple-element.78.early, ...), custom_call_target="tpu_custom_call", output_to_operand_aliasing={{0}: (4, {}), {1}: (5, {}), {2}: (6, {})} | custom-call | tf_op jit(solution)/shard_map/pallas_call | solution.py:535
  19.9 0.6 %collective-permute-done.4.near = f32[256,128]{1,0:T(8,128)S(1)} collective-permute-done((f32[256,128]{1,0:T(8,128)S(1)}, f32[256,128]{1,0:T(8,128)S(1)}, u32[]{:S(2)}, u32[]{:S(2)}) %collective-permute-start.4) | collective-permute-done | bytes 131104 | tf_op jit(solution)/shard_map/ppermute | solution.py:534
  20.5 0.0 collective-permute-done.5.part_near
  20.5 1.1 %shard_map.84 = (bf16[3,2,6,128,384]{4,3,2,1,0:T(8,128)(2,1)S(1)}, f32[10,128,128]{2,1,0:T(8,128)S(1)}, f32[6,2,128,128]{3,2,1,0:T(8,128)S(1)}) custom-call(f32[256,128]{1,0:T(8,128)S(1)} %collective-permute-done.4.near, f32[128,128]{1,0:T(8,128)S(1)} %get-tuple-element.75.own_part, ...), custom_call_target="tpu_custom_call", output_to_operand_aliasing={{0}: (5, {}), {1}: (6, {}), {2}: (7, {})} | custom-call | tf_op jit(solution)/shard_map/pallas_call | solution.py:541
  21.6 0.0 collective-permute-done.3.part_far
  21.6 0.0 collective-permute-done.2.far
  21.6 1.8 %shard_map.85 = (bf16[3,2,6,128,384]{4,3,2,1,0:T(8,128)(2,1)S(1)}, f32[2,3,128,128]{3,2,1,0:T(8,128)}, f32[2,3,128,128]{3,2,1,0:T(8,128)}) custom-call(f32[264,128]{1,0:T(8,128)S(1)} %collective-permute-done.2.far, f32[128,128]{1,0:T(8,128)S(1)} %get-tuple-element.67.own_part, ...), custom_call_target="tpu_custom_call", output_to_operand_aliasing={{0}: (7, {})} | custom-call | tf_op jit(solution)/shard_map/pallas_call | solution.py:547
Async XLA Ops:
  3.3 9.5 %collective-permute-start = (f32[472,128]{1,0:T(8,128)S(1)}, f32[472,128]{1,0:T(8,128)S(1)}, u32[]{:S(2)}, u32[]{:S(2)}) collective-permute-start(f32[472,128]{1,0:T(8,128)S(1)} %get-tuple-element.46), channel_id=1, source_target_pairs={{0,15},{1,2},{2,1},{3,4},{4,3},{5,6},{6,5},{7,8},{8,7},{9,10},{10,... | collective-permute-start | bytes 725000 | tf_op jit(solution)/shard_map/ppermute | solution.py:490
  9.0 1.6 %collective-permute-start.1 = (f32[456,128]{1,0:T(8,128)S(1)}, f32[456,128]{1,0:T(8,128)S(1)}, u32[]{:S(2)}, u32[]{:S(2)}) collective-permute-start(f32[456,128]{1,0:T(8,128)S(1)} %get-tuple-element.54), channel_id=1, source_target_pairs={{0,1},{1,0},{2,3},{3,2},{4,5},{5,4},{6,7},{7,6},{8,9},{9,8},{10,11... | collective-permute-start | bytes 700424 | tf_op jit(solution)/shard_map/ppermute | solution.py:497
  11.8 8.7 %collective-permute-start.5 = (f32[272,128]{1,0:T(8,128)S(1)}, f32[272,128]{1,0:T(8,128)S(1)}, u32[]{:S(2)}, u32[]{:S(2)}) collective-permute-start(f32[272,128]{1,0:T(8,128)S(1)} %get-tuple-element.76), channel_id=1, source_target_pairs={{0,1},{1,0},{2,3},{3,2},{4,5},{5,4},{6,7},{7,6},{8,9},{9,8},{10,11... | collective-permute-start | bytes 417800 | tf_op jit(solution)/shard_map/ppermute | solution.py:511
  12.0 9.6 %collective-permute-start.3 = (f32[272,128]{1,0:T(8,128)S(1)}, f32[272,128]{1,0:T(8,128)S(1)}, u32[]{:S(2)}, u32[]{:S(2)}) collective-permute-start(f32[272,128]{1,0:T(8,128)S(1)} %get-tuple-element.68), channel_id=1, source_target_pairs={{0,15},{1,2},{2,1},{3,4},{4,3},{5,6},{6,5},{7,8},{8,7},{9,10},{10,... | collective-permute-start | bytes 417800 | tf_op jit(solution)/shard_map/ppermute | solution.py:510
  14.3 7.3 %collective-permute-start.2 = (f32[264,128]{1,0:T(8,128)S(1)}, f32[264,128]{1,0:T(8,128)S(1)}, u32[]{:S(2)}, u32[]{:S(2)}) collective-permute-start(f32[264,128]{1,0:T(8,128)S(1)} %get-tuple-element.66), channel_id=1, source_target_pairs={{0,15},{1,2},{2,1},{3,4},{4,3},{5,6},{6,5},{7,8},{8,7},{9,10},{10,... | collective-permute-start | bytes 405512 | tf_op jit(solution)/shard_map/ppermute | solution.py:527
  19.1 1.4 %collective-permute-start.4 = (f32[256,128]{1,0:T(8,128)S(1)}, f32[256,128]{1,0:T(8,128)S(1)}, u32[]{:S(2)}, u32[]{:S(2)}) collective-permute-start(f32[256,128]{1,0:T(8,128)S(1)} %get-tuple-element.74), channel_id=1, source_target_pairs={{0,1},{1,0},{2,3},{3,2},{4,5},{5,4},{6,7},{7,6},{8,9},{9,8},{10,11... | collective-permute-start | bytes 393224 | tf_op jit(solution)/shard_map/ppermute | solution.py:534

commit v11 on v8

--- a/solution.py
+++ b/solution.py
@@ -18,9 +18,9 @@
 SIGN_IM = (-1.0, -1.0, 1.0, 1.0, -1.0, -1.0)
 FIRST_ROWS = 3 * BS + BS // 2 + 8
 SECOND_ROWS = 2 * BS
-MORE = 8
-PART_ROWS = SECOND_ROWS + 2 * MORE
-FAR_PART_ROWS = SECOND_ROWS + 2 * MORE
+MORE = 1
+PART_ROWS = SECOND_ROWS + 2
+FAR_PART_ROWS = SECOND_ROWS + 2
 TABLE_ROWS = 24
 
 

time: 23.7 us -> 23.6 us (level)
  no operation moved by 1% of the time
where the time goes in v11:
time: 23.6 us; the launch traced here: 23.4 us
  starting transfers between devices  10.9 us (46%)
  Pallas kernels  9.66 us (41%)
  waiting for transfers between devices  1.48 us (6%)
  between operations  1.36 us (6%)
    ppermute x2, starting transfers between devices, body(): far = lax.ppermute(far, RING, cross)  10 us
    pallas_call x1, Pallas kernels, body(): call(own_first, [BIG] * 5 + [SCALAR], [vector(FIRST_ROWS + 2 * MORE, BS),...  1.98 us
    pallas_call x1, Pallas kernels, body(): call(far_second, [VECTOR] * 8, [x_out, out, out], [pltpu.VMEM((4, 2, BS,...  1.85 us
    pallas_call x1, Pallas kernels, body(): call(far_first, [VECTOR] * 5, [h_out, x_out, sums_out, late_out, early_ou...  1.58 us
    ppermute x2, waiting for transfers between devices, body(): near = lax.ppermute(near, RING, pair)  1.35 us
    pallas_call x1, Pallas kernels, body(): call(near_first, [VECTOR] * 6, [h_out, x_out, sums_out, base_out, carry_o...  1.22 us
    pallas_call x1, Pallas kernels, body(): call(near_second, [VECTOR] * 8, [x_out, sums_out, base_out], aliases={5:...  1.09 us
    pallas_call x1, Pallas kernels, body(): call(rest_second, [VECTOR] * 7, [x_out, sums_out, base_out], aliases={4:...  0.73 us
  transfers between devices with their start and end apart: 6, of which 3 were waited for; matrix products, arithmetic and copies ran while one was open for 0% of the time, Pallas kernels for 25%

profile of v11, /device:TPU:0, one launch (start us, length us, event | category | flops | bytes accessed | tf_op | source)
XLA Modules:
  0.0 23.4 jit_solution(14044086565140374204)
XLA Ops:
  1.3 2.0 %shard_map.77 = (f32[458,128]{1,0:T(8,128)S(1)}, f32[456,128]{1,0:T(8,128)S(1)}, f32[24,128]{1,0:T(8,128)S(1)}, bf16[4,6,128,384]{3,2,1,0:T(8,128)(2,1)S(1)}, bf...) custom-call(f32[2,3,128,128]{3,2,1,0:T(8,128)} %re.1, ...), custom_call_target="tpu_custom_call" | custom-call | tf_op jit(solution)/shard_map/pallas_call | solution.py:470
  3.3 5.5 %collective-permute-start = (f32[458,128]{1,0:T(8,128)S(1)}, f32[458,128]{1,0:T(8,128)S(1)}, u32[]{:S(2)}, u32[]{:S(2)}) collective-permute-start(f32[458,128]{1,0:T(8,128)S(1)} %get-tuple-element.46), channel_id=1, source_target_pairs={{0,15},{1,2},{2,1},{3,4},{4,3},{5,6},{6,5},{7,8},{8,7},{9,10},{10,... | collective-permute-start | bytes 703496 | tf_op jit(solution)/shard_map/ppermute | solution.py:487
  8.8 0.3 %shard_map.78 = (f32[456,128]{1,0:T(8,128)S(1)}, bf16[3,2,6,128,384]{4,3,2,1,0:T(8,128)(2,1)S(1)}, f32[10,128,128]{2,1,0:T(8,128)S(1)}, f32[4,128,128]{2,1,0:T(8,128)S(1)}) custom-call(f32[128,128]{1,0:T(8,128)S(1)} %get-tuple-element.48.carry, ...), custom_call_target="tpu_custom_call", output_to_operand_aliasing={{0}: (2, {}), {1}: (3, {}), {2}: (4, {}), {3}: (5, {})} | custom-call | tf_op jit(solution)/shard_map/pallas_call | solution.py:488
  9.0 0.1 collective-permute-start.1
  9.1 0.7 %shard_map.79 = (bf16[3,2,6,128,384]{4,3,2,1,0:T(8,128)(2,1)S(1)}, f32[10,128,128]{2,1,0:T(8,128)S(1)}, f32[6,2,128,128]{3,2,1,0:T(8,128)S(1)}) custom-call(f32[2,3,128,128]{3,2,1,0:T(8,128)S(1)} %get-tuple-element.55.re_in, f32[2,3,128,128]{3,2,1,0:T(8,128)S(1)} %get-tuple-element.56.im_in, ...), custom_call_target="tpu_custom_call", output_to_operand_aliasing={{0}: (5, {}), {1}: (6, {})} | custom-call | tf_op jit(solution)/shard_map/pallas_call | solution.py:495
  9.8 0.8 %collective-permute-done.1.near = f32[456,128]{1,0:T(8,128)S(1)} collective-permute-done((f32[456,128]{1,0:T(8,128)S(1)}, f32[456,128]{1,0:T(8,128)S(1)}, u32[]{:S(2)}, u32[]{:S(2)}) %collective-permute-start.1) | collective-permute-done | bytes 233504 | tf_op jit(solution)/shard_map/ppermute | solution.py:494
  10.6 1.2 %shard_map.80 = (bf16[4,6,128,384]{3,2,1,0:T(8,128)(2,1)S(1)}, bf16[3,2,6,128,384]{4,3,2,1,0:T(8,128)(2,1)S(1)}, f32[10,128,128]{2,1,0:T(8,128)S(1)}, f32[6,2,12...) custom-call(f32[456,128]{1,0:T(8,128)S(1)} %collective-permute-done., ...), custom_call_target="tpu_custom_call", output_to_operand_aliasing={{0}: (2, {}), {1}: (3, {}), {2}: (4, {}), {3}: (5, {})} | custom-call | tf_op jit(solution)/shard_map/pallas_call | solution.py:501
  11.8 0.2 collective-permute-start.5
  12.0 0.6 %collective-permute-start.3 = (f32[258,128]{1,0:T(8,128)S(1)}, f32[258,128]{1,0:T(8,128)S(1)}, u32[]{:S(2)}, u32[]{:S(2)}) collective-permute-start(f32[258,128]{1,0:T(8,128)S(1)} %get-tuple-element.68), channel_id=1, source_target_pairs={{0,15},{1,2},{2,1},{3,4},{4,3},{5,6},{6,5},{7,8},{8,7},{9,10},{10,... | collective-permute-start | bytes 396296 | tf_op jit(solution)/shard_map/ppermute | solution.py:507
  12.6 0.1 collective-permute-done.far
  12.7 1.6 %shard_map.81 = (bf16[4,6,128,384]{3,2,1,0:T(8,128)(2,1)S(1)}, bf16[3,2,6,128,384]{4,3,2,1,0:T(8,128)(2,1)S(1)}, f32[10,128,128]{2,1,0:T(8,128)S(1)}, f32[10,128...) custom-call(f32[458,128]{1,0:T(8,128)S(1)} %collective-permute-done., ...), custom_call_target="tpu_custom_call", output_to_operand_aliasing={{0}: (2, {}), {1}: (3, {}), {2}: (4, {})} | custom-call | tf_op jit(solution)/shard_map/pallas_call | solution.py:509
  14.3 4.5 %collective-permute-start.2 = (f32[257,128]{1,0:T(8,128)S(1)}, f32[257,128]{1,0:T(8,128)S(1)}, u32[]{:S(2)}, u32[]{:S(2)}) collective-permute-start(f32[257,128]{1,0:T(8,128)S(1)} %get-tuple-element.66), channel_id=1, source_target_pairs={{0,15},{1,2},{2,1},{3,4},{4,3},{5,6},{6,5},{7,8},{8,7},{9,10},{10,... | collective-permute-start | bytes 394760 | tf_op jit(solution)/shard_map/ppermute | solution.py:524
  18.8 0.3 %shard_map.82 = (f32[256,128]{1,0:T(8,128)S(1)}, bf16[3,2,6,128,384]{4,3,2,1,0:T(8,128)(2,1)S(1)}, f32[10,128,128]{2,1,0:T(8,128)S(1)}, f32[4,128,128]{2,1,0:T(8,128)S(1)}) custom-call(f32[128,128]{1,0:T(8,128)S(1)} %get-tuple-element.69.carry, ...), custom_call_target="tpu_custom_call", output_to_operand_aliasing={{1}: (2, {}), {2}: (3, {}), {3}: (4, {})} | custom-call | tf_op jit(solution)/shard_map/pallas_call | solution.py:525
  19.0 0.1 collective-permute-start.4
  19.1 0.7 %shard_map.83 = (bf16[3,2,6,128,384]{4,3,2,1,0:T(8,128)(2,1)S(1)}, f32[10,128,128]{2,1,0:T(8,128)S(1)}, f32[6,2,128,128]{3,2,1,0:T(8,128)S(1)}) custom-call(f32[10,128,128]{2,1,0:T(8,128)S(1)} %get-tuple-element.77.late, f32[4,128,128]{2,1,0:T(8,128)S(1)} %get-tuple-element.78.early, ...), custom_call_target="tpu_custom_call", output_to_operand_aliasing={{0}: (4, {}), {1}: (5, {}), {2}: (6, {})} | custom-call | tf_op jit(solution)/shard_map/pallas_call | solution.py:532
  19.8 0.0 collective-permute-done.5.part_near
  19.9 0.6 %collective-permute-done.4.near = f32[256,128]{1,0:T(8,128)S(1)} collective-permute-done((f32[256,128]{1,0:T(8,128)S(1)}, f32[256,128]{1,0:T(8,128)S(1)}, u32[]{:S(2)}, u32[]{:S(2)}) %collective-permute-start.4) | collective-permute-done | bytes 131104 | tf_op jit(solution)/shard_map/ppermute | solution.py:531
  20.4 1.1 %shard_map.84 = (bf16[3,2,6,128,384]{4,3,2,1,0:T(8,128)(2,1)S(1)}, f32[10,128,128]{2,1,0:T(8,128)S(1)}, f32[6,2,128,128]{3,2,1,0:T(8,128)S(1)}) custom-call(f32[256,128]{1,0:T(8,128)S(1)} %collective-permute-done.4.near, f32[128,128]{1,0:T(8,128)S(1)} %get-tuple-element.75.own_part, ...), custom_call_target="tpu_custom_call", output_to_operand_aliasing={{0}: (5, {}), {1}: (6, {}), {2}: (7, {})} | custom-call | tf_op jit(solution)/shard_map/pallas_call | solution.py:538
  21.5 0.0 collective-permute-done.3.part_far
  21.5 0.0 collective-permute-done.2.far
  21.6 1.8 %shard_map.85 = (bf16[3,2,6,128,384]{4,3,2,1,0:T(8,128)(2,1)S(1)}, f32[2,3,128,128]{3,2,1,0:T(8,128)}, f32[2,3,128,128]{3,2,1,0:T(8,128)}) custom-call(f32[257,128]{1,0:T(8,128)S(1)} %collective-permute-done.2.far, f32[128,128]{1,0:T(8,128)S(1)} %get-tuple-element.67.own_part, ...), custom_call_target="tpu_custom_call", output_to_operand_aliasing={{0}: (7, {})} | custom-call | tf_op jit(solution)/shard_map/pallas_call | solution.py:544
Async XLA Ops:
  3.3 9.4 %collective-permute-start = (f32[458,128]{1,0:T(8,128)S(1)}, f32[458,128]{1,0:T(8,128)S(1)}, u32[]{:S(2)}, u32[]{:S(2)}) collective-permute-start(f32[458,128]{1,0:T(8,128)S(1)} %get-tuple-element.46), channel_id=1, source_target_pairs={{0,15},{1,2},{2,1},{3,4},{4,3},{5,6},{6,5},{7,8},{8,7},{9,10},{10,... | collective-permute-start | bytes 703496 | tf_op jit(solution)/shard_map/ppermute | solution.py:487
  9.0 1.6 %collective-permute-start.1 = (f32[456,128]{1,0:T(8,128)S(1)}, f32[456,128]{1,0:T(8,128)S(1)}, u32[]{:S(2)}, u32[]{:S(2)}) collective-permute-start(f32[456,128]{1,0:T(8,128)S(1)} %get-tuple-element.54), channel_id=1, source_target_pairs={{0,1},{1,0},{2,3},{3,2},{4,5},{5,4},{6,7},{7,6},{8,9},{9,8},{10,11... | collective-permute-start | bytes 700424 | tf_op jit(solution)/shard_map/ppermute | solution.py:494
  11.8 8.0 %collective-permute-start.5 = (f32[258,128]{1,0:T(8,128)S(1)}, f32[258,128]{1,0:T(8,128)S(1)}, u32[]{:S(2)}, u32[]{:S(2)}) collective-permute-start(f32[258,128]{1,0:T(8,128)S(1)} %get-tuple-element.76), channel_id=1, source_target_pairs={{0,1},{1,0},{2,3},{3,2},{4,5},{5,4},{6,7},{7,6},{8,9},{9,8},{10,11... | collective-permute-start | bytes 396296 | tf_op jit(solution)/shard_map/ppermute | solution.py:508
  12.0 9.5 %collective-permute-start.3 = (f32[258,128]{1,0:T(8,128)S(1)}, f32[258,128]{1,0:T(8,128)S(1)}, u32[]{:S(2)}, u32[]{:S(2)}) collective-permute-start(f32[258,128]{1,0:T(8,128)S(1)} %get-tuple-element.68), channel_id=1, source_target_pairs={{0,15},{1,2},{2,1},{3,4},{4,3},{5,6},{6,5},{7,8},{8,7},{9,10},{10,... | collective-permute-start | bytes 396296 | tf_op jit(solution)/shard_map/ppermute | solution.py:507
  14.3 7.3 %collective-permute-start.2 = (f32[257,128]{1,0:T(8,128)S(1)}, f32[257,128]{1,0:T(8,128)S(1)}, u32[]{:S(2)}, u32[]{:S(2)}) collective-permute-start(f32[257,128]{1,0:T(8,128)S(1)} %get-tuple-element.66), channel_id=1, source_target_pairs={{0,15},{1,2},{2,1},{3,4},{4,3},{5,6},{6,5},{7,8},{8,7},{9,10},{10,... | collective-permute-start | bytes 394760 | tf_op jit(solution)/shard_map/ppermute | solution.py:524
  19.0 1.4 %collective-permute-start.4 = (f32[256,128]{1,0:T(8,128)S(1)}, f32[256,128]{1,0:T(8,128)S(1)}, u32[]{:S(2)}, u32[]{:S(2)}) collective-permute-start(f32[256,128]{1,0:T(8,128)S(1)} %get-tuple-element.74), channel_id=1, source_target_pairs={{0,1},{1,0},{2,3},{3,2},{4,5},{5,4},{6,7},{7,6},{8,9},{9,8},{10,11... | collective-permute-start | bytes 393224 | tf_op jit(solution)/shard_map/ppermute | solution.py:531

commit v12 on v11

--- a/solution.py
+++ b/solution.py
@@ -398,7 +398,7 @@
             copies.append(pltpu.make_async_copy(source.at[index, a], out.at[r, e], sems.at[len(copies)]))
 
     def send(first):
-        for copy in copies[2 * first : 2 * first + 4]:
+        for copy in copies[2 * first : 2 * first + (4 if first > 1 else 2)]:
             copy.start()
 
     def apart(first):
@@ -422,8 +422,9 @@
 
     start = (own_part[...] + part_far[0:BS, :]) * coefficient(2)
     far_side(h, xs, start, far, 1, table, sums, record, between)
+    finish(1)
+    send(1)
     finish(0)
-    finish(1)
     send(0)
     for copy in copies:
         copy.wait()

time: 23.6 us -> 23.6 us (level)
  no operation moved by 1% of the time
where the time goes in v12:
time: 23.6 us; the launch traced here: 23.4 us
  starting transfers between devices  10.9 us (46%)
  Pallas kernels  9.65 us (41%)
  waiting for transfers between devices  1.48 us (6%)
  between operations  1.36 us (6%)
    ppermute x2, starting transfers between devices, body(): far = lax.ppermute(far, RING, cross)  10 us
    pallas_call x1, Pallas kernels, body(): call(own_first, [BIG] * 5 + [SCALAR], [vector(FIRST_ROWS + 2 * MORE, BS),...  1.98 us
    pallas_call x1, Pallas kernels, body(): call(far_second, [VECTOR] * 8, [x_out, out, out], [pltpu.VMEM((4, 2, BS,...  1.84 us
    pallas_call x1, Pallas kernels, body(): call(far_first, [VECTOR] * 5, [h_out, x_out, sums_out, late_out, early_ou...  1.58 us
    ppermute x2, waiting for transfers between devices, body(): near = lax.ppermute(near, RING, pair)  1.35 us
    pallas_call x1, Pallas kernels, body(): call(near_first, [VECTOR] * 6, [h_out, x_out, sums_out, base_out, carry_o...  1.22 us
    pallas_call x1, Pallas kernels, body(): call(near_second, [VECTOR] * 8, [x_out, sums_out, base_out], aliases={5:...  1.09 us
    pallas_call x1, Pallas kernels, body(): call(rest_second, [VECTOR] * 7, [x_out, sums_out, base_out], aliases={4:...  0.73 us
  transfers between devices with their start and end apart: 6, of which 3 were waited for; matrix products, arithmetic and copies ran while one was open for 0% of the time, Pallas kernels for 25%

profile of v12, /device:TPU:0, one launch (start us, length us, event | category | flops | bytes accessed | tf_op | source)
XLA Modules:
  0.0 23.4 jit_solution(17487588773832862518)
XLA Ops:
  1.3 2.0 %shard_map.77 = (f32[458,128]{1,0:T(8,128)S(1)}, f32[456,128]{1,0:T(8,128)S(1)}, f32[24,128]{1,0:T(8,128)S(1)}, bf16[4,6,128,384]{3,2,1,0:T(8,128)(2,1)S(1)}, bf...) custom-call(f32[2,3,128,128]{3,2,1,0:T(8,128)} %re.1, ...), custom_call_target="tpu_custom_call" | custom-call | tf_op jit(solution)/shard_map/pallas_call | solution.py:471
  3.3 5.5 %collective-permute-start = (f32[458,128]{1,0:T(8,128)S(1)}, f32[458,128]{1,0:T(8,128)S(1)}, u32[]{:S(2)}, u32[]{:S(2)}) collective-permute-start(f32[458,128]{1,0:T(8,128)S(1)} %get-tuple-element.46), channel_id=1, source_target_pairs={{0,15},{1,2},{2,1},{3,4},{4,3},{5,6},{6,5},{7,8},{8,7},{9,10},{10,... | collective-permute-start | bytes 703496 | tf_op jit(solution)/shard_map/ppermute | solution.py:488
  8.8 0.3 %shard_map.78 = (f32[456,128]{1,0:T(8,128)S(1)}, bf16[3,2,6,128,384]{4,3,2,1,0:T(8,128)(2,1)S(1)}, f32[10,128,128]{2,1,0:T(8,128)S(1)}, f32[4,128,128]{2,1,0:T(8,128)S(1)}) custom-call(f32[128,128]{1,0:T(8,128)S(1)} %get-tuple-element.48.carry, ...), custom_call_target="tpu_custom_call", output_to_operand_aliasing={{0}: (2, {}), {1}: (3, {}), {2}: (4, {}), {3}: (5, {})} | custom-call | tf_op jit(solution)/shard_map/pallas_call | solution.py:489
  9.0 0.1 collective-permute-start.1
  9.1 0.7 %shard_map.79 = (bf16[3,2,6,128,384]{4,3,2,1,0:T(8,128)(2,1)S(1)}, f32[10,128,128]{2,1,0:T(8,128)S(1)}, f32[6,2,128,128]{3,2,1,0:T(8,128)S(1)}) custom-call(f32[2,3,128,128]{3,2,1,0:T(8,128)S(1)} %get-tuple-element.55.re_in, f32[2,3,128,128]{3,2,1,0:T(8,128)S(1)} %get-tuple-element.56.im_in, ...), custom_call_target="tpu_custom_call", output_to_operand_aliasing={{0}: (5, {}), {1}: (6, {})} | custom-call | tf_op jit(solution)/shard_map/pallas_call | solution.py:496
  9.8 0.8 %collective-permute-done.1.near = f32[456,128]{1,0:T(8,128)S(1)} collective-permute-done((f32[456,128]{1,0:T(8,128)S(1)}, f32[456,128]{1,0:T(8,128)S(1)}, u32[]{:S(2)}, u32[]{:S(2)}) %collective-permute-start.1) | collective-permute-done | bytes 233504 | tf_op jit(solution)/shard_map/ppermute | solution.py:495
  10.6 1.2 %shard_map.80 = (bf16[4,6,128,384]{3,2,1,0:T(8,128)(2,1)S(1)}, bf16[3,2,6,128,384]{4,3,2,1,0:T(8,128)(2,1)S(1)}, f32[10,128,128]{2,1,0:T(8,128)S(1)}, f32[6,2,12...) custom-call(f32[456,128]{1,0:T(8,128)S(1)} %collective-permute-done., ...), custom_call_target="tpu_custom_call", output_to_operand_aliasing={{0}: (2, {}), {1}: (3, {}), {2}: (4, {}), {3}: (5, {})} | custom-call | tf_op jit(solution)/shard_map/pallas_call | solution.py:502
  11.8 0.2 collective-permute-start.5
  12.0 0.6 %collective-permute-start.3 = (f32[258,128]{1,0:T(8,128)S(1)}, f32[258,128]{1,0:T(8,128)S(1)}, u32[]{:S(2)}, u32[]{:S(2)}) collective-permute-start(f32[258,128]{1,0:T(8,128)S(1)} %get-tuple-element.68), channel_id=1, source_target_pairs={{0,15},{1,2},{2,1},{3,4},{4,3},{5,6},{6,5},{7,8},{8,7},{9,10},{10,... | collective-permute-start | bytes 396296 | tf_op jit(solution)/shard_map/ppermute | solution.py:508
  12.6 0.1 collective-permute-done.far
  12.7 1.6 %shard_map.81 = (bf16[4,6,128,384]{3,2,1,0:T(8,128)(2,1)S(1)}, bf16[3,2,6,128,384]{4,3,2,1,0:T(8,128)(2,1)S(1)}, f32[10,128,128]{2,1,0:T(8,128)S(1)}, f32[10,128...) custom-call(f32[458,128]{1,0:T(8,128)S(1)} %collective-permute-done., ...), custom_call_target="tpu_custom_call", output_to_operand_aliasing={{0}: (2, {}), {1}: (3, {}), {2}: (4, {})} | custom-call | tf_op jit(solution)/shard_map/pallas_call | solution.py:510
  14.3 4.5 %collective-permute-start.2 = (f32[257,128]{1,0:T(8,128)S(1)}, f32[257,128]{1,0:T(8,128)S(1)}, u32[]{:S(2)}, u32[]{:S(2)}) collective-permute-start(f32[257,128]{1,0:T(8,128)S(1)} %get-tuple-element.66), channel_id=1, source_target_pairs={{0,15},{1,2},{2,1},{3,4},{4,3},{5,6},{6,5},{7,8},{8,7},{9,10},{10,... | collective-permute-start | bytes 394760 | tf_op jit(solution)/shard_map/ppermute | solution.py:525
  18.8 0.3 %shard_map.82 = (f32[256,128]{1,0:T(8,128)S(1)}, bf16[3,2,6,128,384]{4,3,2,1,0:T(8,128)(2,1)S(1)}, f32[10,128,128]{2,1,0:T(8,128)S(1)}, f32[4,128,128]{2,1,0:T(8,128)S(1)}) custom-call(f32[128,128]{1,0:T(8,128)S(1)} %get-tuple-element.69.carry, ...), custom_call_target="tpu_custom_call", output_to_operand_aliasing={{1}: (2, {}), {2}: (3, {}), {3}: (4, {})} | custom-call | tf_op jit(solution)/shard_map/pallas_call | solution.py:526
  19.0 0.1 collective-permute-start.4
  19.1 0.7 %shard_map.83 = (bf16[3,2,6,128,384]{4,3,2,1,0:T(8,128)(2,1)S(1)}, f32[10,128,128]{2,1,0:T(8,128)S(1)}, f32[6,2,128,128]{3,2,1,0:T(8,128)S(1)}) custom-call(f32[10,128,128]{2,1,0:T(8,128)S(1)} %get-tuple-element.77.late, f32[4,128,128]{2,1,0:T(8,128)S(1)} %get-tuple-element.78.early, ...), custom_call_target="tpu_custom_call", output_to_operand_aliasing={{0}: (4, {}), {1}: (5, {}), {2}: (6, {})} | custom-call | tf_op jit(solution)/shard_map/pallas_call | solution.py:533
  19.8 0.0 collective-permute-done.5.part_near
  19.9 0.6 %collective-permute-done.4.near = f32[256,128]{1,0:T(8,128)S(1)} collective-permute-done((f32[256,128]{1,0:T(8,128)S(1)}, f32[256,128]{1,0:T(8,128)S(1)}, u32[]{:S(2)}, u32[]{:S(2)}) %collective-permute-start.4) | collective-permute-done | bytes 131104 | tf_op jit(solution)/shard_map/ppermute | solution.py:532
  20.4 1.1 %shard_map.84 = (bf16[3,2,6,128,384]{4,3,2,1,0:T(8,128)(2,1)S(1)}, f32[10,128,128]{2,1,0:T(8,128)S(1)}, f32[6,2,128,128]{3,2,1,0:T(8,128)S(1)}) custom-call(f32[256,128]{1,0:T(8,128)S(1)} %collective-permute-done.4.near, f32[128,128]{1,0:T(8,128)S(1)} %get-tuple-element.75.own_part, ...), custom_call_target="tpu_custom_call", output_to_operand_aliasing={{0}: (5, {}), {1}: (6, {}), {2}: (7, {})} | custom-call | tf_op jit(solution)/shard_map/pallas_call | solution.py:539
  21.5 0.0 collective-permute-done.3.part_far
  21.5 0.0 collective-permute-done.2.far
  21.6 1.8 %shard_map.85 = (bf16[3,2,6,128,384]{4,3,2,1,0:T(8,128)(2,1)S(1)}, f32[2,3,128,128]{3,2,1,0:T(8,128)}, f32[2,3,128,128]{3,2,1,0:T(8,128)}) custom-call(f32[257,128]{1,0:T(8,128)S(1)} %collective-permute-done.2.far, f32[128,128]{1,0:T(8,128)S(1)} %get-tuple-element.67.own_part, ...), custom_call_target="tpu_custom_call", output_to_operand_aliasing={{0}: (7, {})} | custom-call | tf_op jit(solution)/shard_map/pallas_call | solution.py:545
Async XLA Ops:
  3.3 9.4 %collective-permute-start = (f32[458,128]{1,0:T(8,128)S(1)}, f32[458,128]{1,0:T(8,128)S(1)}, u32[]{:S(2)}, u32[]{:S(2)}) collective-permute-start(f32[458,128]{1,0:T(8,128)S(1)} %get-tuple-element.46), channel_id=1, source_target_pairs={{0,15},{1,2},{2,1},{3,4},{4,3},{5,6},{6,5},{7,8},{8,7},{9,10},{10,... | collective-permute-start | bytes 703496 | tf_op jit(solution)/shard_map/ppermute | solution.py:488
  9.0 1.6 %collective-permute-start.1 = (f32[456,128]{1,0:T(8,128)S(1)}, f32[456,128]{1,0:T(8,128)S(1)}, u32[]{:S(2)}, u32[]{:S(2)}) collective-permute-start(f32[456,128]{1,0:T(8,128)S(1)} %get-tuple-element.54), channel_id=1, source_target_pairs={{0,1},{1,0},{2,3},{3,2},{4,5},{5,4},{6,7},{7,6},{8,9},{9,8},{10,11... | collective-permute-start | bytes 700424 | tf_op jit(solution)/shard_map/ppermute | solution.py:495
  11.8 8.0 %collective-permute-start.5 = (f32[258,128]{1,0:T(8,128)S(1)}, f32[258,128]{1,0:T(8,128)S(1)}, u32[]{:S(2)}, u32[]{:S(2)}) collective-permute-start(f32[258,128]{1,0:T(8,128)S(1)} %get-tuple-element.76), channel_id=1, source_target_pairs={{0,1},{1,0},{2,3},{3,2},{4,5},{5,4},{6,7},{7,6},{8,9},{9,8},{10,11... | collective-permute-start | bytes 396296 | tf_op jit(solution)/shard_map/ppermute | solution.py:509
  12.0 9.5 %collective-permute-start.3 = (f32[258,128]{1,0:T(8,128)S(1)}, f32[258,128]{1,0:T(8,128)S(1)}, u32[]{:S(2)}, u32[]{:S(2)}) collective-permute-start(f32[258,128]{1,0:T(8,128)S(1)} %get-tuple-element.68), channel_id=1, source_target_pairs={{0,15},{1,2},{2,1},{3,4},{4,3},{5,6},{6,5},{7,8},{8,7},{9,10},{10,... | collective-permute-start | bytes 396296 | tf_op jit(solution)/shard_map/ppermute | solution.py:508
  14.3 7.3 %collective-permute-start.2 = (f32[257,128]{1,0:T(8,128)S(1)}, f32[257,128]{1,0:T(8,128)S(1)}, u32[]{:S(2)}, u32[]{:S(2)}) collective-permute-start(f32[257,128]{1,0:T(8,128)S(1)} %get-tuple-element.66), channel_id=1, source_target_pairs={{0,15},{1,2},{2,1},{3,4},{4,3},{5,6},{6,5},{7,8},{8,7},{9,10},{10,... | collective-permute-start | bytes 394760 | tf_op jit(solution)/shard_map/ppermute | solution.py:525
  19.0 1.4 %collective-permute-start.4 = (f32[256,128]{1,0:T(8,128)S(1)}, f32[256,128]{1,0:T(8,128)S(1)}, u32[]{:S(2)}, u32[]{:S(2)}) collective-permute-start(f32[256,128]{1,0:T(8,128)S(1)} %get-tuple-element.74), channel_id=1, source_target_pairs={{0,1},{1,0},{2,3},{3,2},{4,5},{5,4},{6,7},{7,6},{8,9},{9,8},{10,11... | collective-permute-start | bytes 393224 | tf_op jit(solution)/shard_map/ppermute | solution.py:532
